TPU v7x, 1024 devices: a whole 8x8x8 slice. The times are simulated.
1024 devices in a mesh: dp: 64 (over y, x), replica: 16 (over z, core).
Axes of the slice: x: 8, y: 8, z: 8, core: 2. Of those that a mesh axis runs over, the one named last changes fastest.
Arguments:
- user_rows: bfloat16 [16, 1024, 2048], P('replica', 'dp'), may hold values from -6 to 6
- user_row: int32 [16, 1024], P('replica', 'dp'), may hold values from 0 to 1023, as said below
- segment: int32 [16, 64, 256], P('replica', 'dp'), may hold values from 0 to 15, never falling along the last dimension, each value on 1 to 32 neighbouring positions
- cand_feat: bfloat16 [16, 16384, 2048], P('replica', 'dp'), may hold values from -16 to 16
- grad_score: float32 [16, 16384], P('replica', 'dp'), may hold values from -6 to 6
- u_weight: bfloat16 [2048, 256], replicated, may hold values from -0.125 to 0.125
- v_weight: bfloat16 [256, 2048], replicated, may hold values from -0.375 to 0.375
- bias: float32 [2048], replicated, may hold values from -3 to 3
- w_out: bfloat16 [2048], replicated, may hold values from -6 to 6
Outputs:
- user_grad: float32 [16, 1024, 2048], P('replica', 'dp')
- grad_u: float32 [2048, 256], P('dp')
- grad_vt: float32 [2048, 256], P('dp')
- grad_bias: float32 [2048], P('dp')
- grad_out: float32 [2048], P('dp')
Inputs may be any that keep to these rules, and one draw needn't show every extreme that they name: `user_row`: in each group every one of the 1024 user rows is named exactly once; row j is held by the device of dp index j // 16. The 16 requests of one device name at most 1 row of any one holder, and some device reaches 1 for some holder in every draw.
All inputs are finite; a program needn't handle non-finite values.
Results may differ from a plain program's by a relative error of at most 0.013.
Values may be sent and summed in bfloat16 or wider, within the bound.
No kernel may reach another device: no remote copies, remote signals or barrier semaphores. Data moves between devices by JAX's collectives and lax.ppermute only.
A program may use at most 64 MiB of HBM per device.

v0:
```python
import math

import jax
import jax.numpy as jnp
from jax import lax
from jax.sharding import PartitionSpec as P


def per_device(
    user_rows, user_row, segment, cand_feat, grad_score, u_weight, v_weight, bias, w_out
):
    own_rows = user_rows[0]
    wanted = user_row[0]
    seg = segment[0, 0]
    feat = cand_feat[0]
    scores = grad_score[0]
    peers = lax.axis_size("dp")
    req_dev = own_rows.shape[0]
    width = own_rows.shape[1]
    rank_size = u_weight.shape[1]
    slots = max(1, 2 * req_dev // peers)
    owners = wanted // req_dev
    owner_hits = (owners[:, None] == jnp.arange(peers, dtype=jnp.int32)[None, :]).astype(jnp.int32)
    earlier = jnp.cumsum(owner_hits, axis=0) - owner_hits
    order_in = jnp.take_along_axis(earlier, owners[:, None], axis=1)[:, 0]
    placed = owners * slots + order_in
    requests = jnp.full((peers * slots,), -1, jnp.int32).at[placed].set(wanted - owners * req_dev)
    requests = requests.reshape(peers, slots)
    asked = lax.all_to_all(requests, "dp", split_axis=0, concat_axis=0, tiled=True)
    valid = asked >= 0
    picked = jnp.take(own_rows, jnp.where(valid, asked, 0), axis=0)
    picked = jnp.where(valid[..., None], picked, jnp.zeros_like(picked))
    returned = lax.all_to_all(picked, "dp", split_axis=0, concat_axis=0, tiled=True)
    local_rows = jnp.take(returned.reshape(peers * slots, width), placed, axis=0)
    user_part = jnp.take(local_rows, seg, axis=0)
    x_zero = (feat.astype(jnp.float32) + user_part.astype(jnp.float32)).astype(jnp.bfloat16)
    low = jnp.dot(x_zero, u_weight, preferred_element_type=jnp.float32).astype(jnp.bfloat16)
    scale_vec = jnp.dot(low, v_weight, preferred_element_type=jnp.float32) + bias[None, :]
    x_wide = x_zero.astype(jnp.float32)
    crossed = x_wide * scale_vec + x_wide
    upstream = scores[:, None] * w_out.astype(jnp.float32)[None, :]
    grad_scale = upstream * x_wide
    grad_scale_b = grad_scale.astype(jnp.bfloat16)
    grad_low = jnp.dot(grad_scale_b, v_weight.T, preferred_element_type=jnp.float32).astype(
        jnp.bfloat16
    )
    grad_input = upstream * (scale_vec + 1.0) + jnp.dot(
        grad_low, u_weight.T, preferred_element_type=jnp.float32
    )
    member = (seg[None, :] == jnp.arange(req_dev, dtype=jnp.int32)[:, None]).astype(jnp.float32)
    request_grad = jnp.dot(
        member, grad_input, precision=lax.Precision.HIGHEST, preferred_element_type=jnp.float32
    )
    outgoing = jnp.zeros((peers * slots, width), jnp.float32).at[placed].set(request_grad)
    arrived = lax.all_to_all(
        outgoing.reshape(peers, slots, width), "dp", split_axis=0, concat_axis=0, tiled=True
    )
    target = jnp.where(asked >= 0, asked, req_dev).reshape(-1)
    user_grad = (
        jnp.zeros((req_dev, width), jnp.float32)
        .at[target]
        .add(arrived.reshape(-1, width), mode="drop")
    )
    part_u = jnp.dot(x_zero.T, grad_low, preferred_element_type=jnp.float32)
    part_vt = jnp.dot(grad_scale_b.T, low, preferred_element_type=jnp.float32)
    part_bias = jnp.sum(grad_scale, axis=0)
    part_out = jnp.dot(
        scores[None, :],
        crossed,
        precision=lax.Precision.HIGHEST,
        preferred_element_type=jnp.float32,
    )[0]
    factor = 1.0 / math.sqrt(feat.shape[0] * peers * lax.axis_size("replica"))
    stacked = jnp.concatenate([part_u, part_vt], axis=1)
    summed, bias_sum, out_sum = (
        lax.psum_scatter(stacked, "dp", scatter_dimension=0, tiled=True),
        lax.psum_scatter(part_bias, "dp", scatter_dimension=0, tiled=True),
        lax.psum_scatter(part_out, "dp", scatter_dimension=0, tiled=True),
    )
    summed, bias_sum, out_sum = lax.psum((summed, bias_sum, out_sum), "replica")
    grad_u = summed[:, :rank_size] * factor
    grad_vt = summed[:, rank_size:] * factor
    return (user_grad[None], grad_u, grad_vt, bias_sum * factor, out_sum * factor)


def solution(mesh):
    placed = (
        P("replica", "dp", None),
        P("replica", "dp"),
        P("replica", "dp", None),
        P("replica", "dp", None),
        P("replica", "dp"),
        P(),
        P(),
        P(),
        P(),
    )
    return jax.shard_map(
        per_device,
        mesh=mesh,
        in_specs=placed,
        out_specs=(P("replica", "dp", None), P("dp", None), P("dp", None), P("dp"), P("dp")),
        check_vma=False,
    )
```

profile of v0, /device:TPU:1, one launch (start us, length us, event | category | flops | bytes accessed | tf_op | source)
XLA Modules:
  0.0 530.4 jit_solution(8528036096478809284)
XLA Ops:
  11.5 14.0 %all-to-all-start = ((s32[64,1,1]{2,1,0:T(1,128)}), s32[64,1,1]{2,1,0:T(1,128)S(1)}, u32[]{:S(2)}, u32[]{:S(2)}) async-start(s32[64,1,1]{2,1,0:T(1,128)} %copy.22), calls=%async_computation | async-start | bytes 65536 | tf_op jit(solution)/shard_map/all_to_all | solution.py:29
  27.0 9.4 %all-to-all-done = s32[64,1,1]{2,1,0:T(1,128)S(1)} async-done(((s32[64,1,1]{2,1,0:T(1,128)}), s32[64,1,1]{2,1,0:T(1,128)S(1)}, u32[]{:S(2)}, u32[]{:S(2)}) %all-to-all-start) | async-done | bytes 288 | tf_op jit(solution)/shard_map/all_to_all | solution.py:29
  36.3 2.4 and_reduce_fusion
  38.7 1.2 reduce.3
  42.1 0.9 reshape.504
  43.0 4.6 all-to-all-start.1
  47.9 12.2 %all-to-all-done.1 = bf16[64,2,1024]{2,1,0:T(2,128)(2,1)S(1)} async-done(((bf16[64,2,1024]{2,1,0:T(2,128)(2,1)}), bf16[64,2,1024]{2,1,0:T(2,128)(2,1)S(1)}, u32[]{:S(2)}, u32[]{:S(2)}) %all-to-all-start.1) | async-done | bytes 262176 | tf_op jit(solution)/shard_map/all_to_all | solution.py:33
  61.2 1.4 gather_fusion.2
  62.6 2.0 fusion
  67.3 2.5 pad_maximum_fusion
  69.8 5.3 %copy.26 = f32[2048,512]{1,0:T(8,128)} copy(f32[2048,512]{0,1:T(8,128)} %pad_maximum_fusion) | data formatting | bytes 8388608
  76.8 0.8 copy-done.2
  78.4 0.8 scatter_custom_fusion.1
  79.2 1.2 reshape.428
  80.4 4.6 all-to-all-start.2
  85.1 1.3 dynamic-slice
  87.0 1.2 reduce
  88.2 3.0 fusion.2
  91.2 224.8 %all-reduce.2 = (f32[2048]{0:T(1024)S(1)}, f32[2048]{0:T(1024)S(1)}) all-reduce(f32[2048]{0:T(1024)S(1)} %get-tuple-element.29, f32[2048]{0:T(1024)S(1)} %bitcast.90), channel_id=3, replica_groups=mesh['dp'=64,'replica'=16] {'dp'}, use_global_device_ids=true, to_apply=%region_7.8.clone | all-reduce | flops 4096 | bytes 32768
  316.1 93.6 %all-reduce.3 = (f32[32]{0:T(128)S(1)}, f32[32]{0:T(128)S(1)}) all-reduce(f32[32]{0:T(128)S(1)} %dynamic-slice.1, f32[32]{0:T(128)S(1)} %dynamic-slice.3), channel_id=1, replica_groups=mesh['dp'=64,'replica'=16] {'replica'}, use_global_device_ids=true, to_apply=%region_8.9 | all-reduce | flops 64 | bytes 512 | tf_op jit(solution)/shard_map/psum | solution.py:80
  409.7 1.7 copy.27
  411.9 2.1 scatter_custom_fusion.2
  414.0 107.2 %all-reduce.6.cloned.1.call-done = f32[32,512]{0,1:T(8,128)} async-done(((f32[32,512]{0,1:T(8,128)}), f32[32,512]{0,1:T(8,128)}) %all-reduce.6.cloned.1.call-update) | async-done | bytes 65552 | tf_op jit(solution)/shard_map/psum | solution.py:80
  521.2 1.0 slice_multiply_fusion
  (59 shorter events, 16.4 us)
Async XLA Ops:
  7.2 57.4 %copy-start = (bf16[256,2048]{1,0:T(8,128)(2,1)S(1)}, bf16[256,2048]{1,0:T(8,128)(2,1)}, u32[]{:S(2)}) copy-start(bf16[256,2048]{1,0:T(8,128)(2,1)} %param.15) | copy-start | bytes 3145732
  7.2 32.8 %copy-start.1 = (bf16[1,16,2048]{2,1,0:T(8,128)(2,1)S(1)}, bf16[1,16,2048]{2,1,0:T(8,128)(2,1)}, u32[]{:S(2)}) copy-start(bf16[1,16,2048]{2,1,0:T(8,128)(2,1)} %param.9) | copy-start | bytes 196612
  11.5 24.8 %all-to-all-start = ((s32[64,1,1]{2,1,0:T(1,128)}), s32[64,1,1]{2,1,0:T(1,128)S(1)}, u32[]{:S(2)}, u32[]{:S(2)}) async-start(s32[64,1,1]{2,1,0:T(1,128)} %copy.22), calls=%async_computation | async-start | bytes 65536 | tf_op jit(solution)/shard_map/all_to_all | solution.py:29
  40.0 7.9 %copy-start.6 = (s32[1,1,256]{2,1,0:T(1,128)S(1)}, s32[1,1,256]{2,1,0:T(1,128)}, u32[]{:S(2)}) copy-start(s32[1,1,256]{2,1,0:T(1,128)} %param.11) | copy-start | bytes 3076
  43.0 17.1 %all-to-all-start.1 = ((bf16[64,2,1024]{2,1,0:T(2,128)(2,1)}), bf16[64,2,1024]{2,1,0:T(2,128)(2,1)S(1)}, u32[]{:S(2)}, u32[]{:S(2)}) async-start(bf16[64,2,1024]{2,1,0:T(2,128)(2,1)} %reshape.504), calls=%async_computation.1 | async-start | bytes 524288 | tf_op jit(solution)/shard_map/all_to_all | solution.py:33
  47.6 362.0 %reduce-scatter.4.cloned.1.call-start = ((), (), s32[]{:S(2)}) async-start(), calls=%async_computation.5 | async-start | bytes 4259840
  61.2 1.4 copy-start.4
  64.6 1.2 copy-start.3
  75.1 0.7 copy-start.5
  76.3 1.3 copy-start.2
  80.4 331.5 %all-to-all-start.2 = ((f32[64,1,2048]{2,1,0:T(1,128)}), f32[64,1,2048]{2,1,0:T(1,128)S(1)}, u32[]{:S(2)}, u32[]{:S(2)}) async-start(f32[64,1,2048]{2,1,0:T(1,128)} %reshape.428), calls=%async_computation.2 | async-start | bytes 1048576 | tf_op jit(solution)/shard_map/all_to_all | solution.py:55
  85.0 436.2 %all-reduce.6.cloned.1.call-start = ((), (), s32[]{:S(2)}) async-start(), calls=%async_computation.4 | async-start | bytes 524288 | tf_op jit(solution)/shard_map/psum | solution.py:80
Sparse Core Ops, SparseCore 0:
  75.3 254.3 reduce-scatter.3
  411.5 109.7 all-reduce.5
where the time goes:
time: 531 us; the launch traced here: 530 us
  blocking collectives  318 us (60%)
  waiting for transfers between devices  129 us (24%)
  starting transfers between devices  23.5 us (4%)
  local copies, waits for them, and re-layouts  20.5 us (4%)
  other arithmetic  17.6 us (3%)
  between operations  15 us (3%)
  matrix products  6.66 us (1%)
    unnamed x1, blocking collectives  225 us
    psum x1, waiting for transfers between devices, per_device(): summed, bias_sum, out_sum = lax.psum((summed, bias_sum, out_sum), 'replica')  107 us
    psum x1, blocking collectives, per_device(): summed, bias_sum, out_sum = lax.psum((summed, bias_sum, out_sum), 'replica')  93.6 us
    all_to_all x1, starting transfers between devices, per_device(): lax.all_to_all(requests, 'dp', split_axis=0, concat_axis=0, tiled=True)  14 us
    unnamed x25, local copies, waits for them, and re-layouts  13.3 us
    all_to_all x1, waiting for transfers between devices, per_device(): lax.all_to_all(picked, 'dp', split_axis=0, concat_axis=0, tiled=True)  12.2 us
  transfers between devices with their start and end apart: 5, of which 3 were waited for; matrix products, arithmetic and copies ran while one was open for 3% of the time, Pallas kernels for 0%

commit v1 on v0

v1 whole, which is shorter than its diff:
```python
import functools
import math

import jax
import jax.numpy as jnp
from jax import lax
from jax.experimental import pallas as pl
from jax.experimental.pallas import tpu as pltpu
from jax.sharding import PartitionSpec as P

F32 = jnp.float32
BF16 = jnp.bfloat16
LANES = 128
PIECES = 8
NT = (((1,), (1,)), ((), ()))
TN = (((0,), (0,)), ((), ()))
PARAMS = pltpu.CompilerParams(vmem_limit_bytes=40 << 20)


def dot(a, b, dims=(((1,), (0,)), ((), ()))):
    return lax.dot_general(a, b, dims, preferred_element_type=F32)


def iota(shape, dim):
    return lax.broadcasted_iota(jnp.int32, shape, dim)


def split_in_two(x):
    high = x.astype(BF16)
    return high, (x - high.astype(F32)).astype(BF16)


def as_columns(row):
    return jnp.transpose(jnp.broadcast_to(row, (LANES, row.shape[1])))


def request_kernel(wanted_ref, seg_ref, score_ref, feat_ref, user_ref, slots_ref, swap_ref, wide):
    peers, req = slots_ref.shape[0], wanted_ref.shape[1]
    rows, width = feat_ref.shape
    piece = width // PIECES
    wanted = wanted_ref[...]
    owner = lax.div(wanted, jnp.int32(req))
    local = wanted - owner * req
    scores = score_ref[...]
    to_owner = (iota((peers, req), 0) == owner).astype(BF16)
    place = (iota((LANES, req), 0) == local).astype(BF16)
    mine = iota((req, rows), 0) == seg_ref[...]
    total_high, total_low = split_in_two(
        jnp.sum(jnp.where(mine, scores, 0.0), axis=1, keepdims=True)
    )
    lane = iota((req, LANES), 1)
    totals = jnp.where(
        lane == req,
        total_high.astype(F32),
        jnp.where(lane == req + 1, total_low.astype(F32), 0.0),
    ).astype(BF16)
    extra = dot(to_owner, place, NT) + dot(to_owner, totals)
    weights = jnp.where(mine, scores, 0.0).astype(BF16)
    weights = dot(to_owner, weights).astype(BF16)
    wide[:, :, piece:] = jnp.zeros((peers, PIECES, LANES), F32)
    wide[:, 0, piece:] = extra
    for p in range(PIECES):
        wide[:, p, :piece] = dot(weights, feat_ref[:, p * piece : (p + 1) * piece])
    slots_ref[...] = wide[...].astype(BF16)
    score_high, score_low = split_in_two(scores)
    line = iota((16, rows), 0)
    swap_ref[:rows, :] = feat_ref[...]
    swap_ref[rows : rows + 16, :] = jnp.zeros((16, width), BF16)
    swap_ref[rows : rows + 16, :rows] = jnp.where(
        line == 0,
        score_high.astype(F32),
        jnp.where(line == 1, score_low.astype(F32), 0.0),
    ).astype(BF16)
    swap_ref[rows + 16 :, :] = user_ref[...]


def main_kernel(
    at_ref, feat_ref, score_ref, user_ref, swap_ref, u_ref, v_ref, bias_ref, w_ref,
    grad_ref, half_ref, vw_ref, user_half_ref, tail_ref, both,
):
    dp, core = at_ref[0], at_ref[1]
    rows, width = feat_ref.shape
    rank = v_ref.shape[0]
    part = tail_ref.shape[0]
    w_row = w_ref[...].astype(F32)
    vw = (v_ref[...].astype(F32) * w_row).astype(BF16)
    vw_ref[...] = vw
    half_ref[...] = u_ref[...]

    @pl.when(core == 1)
    def _():
        half_ref[...] = jnp.transpose(vw)

    both[:rows, :] = feat_ref[...]
    both[rows:, :] = swap_ref[:rows, :]
    marks = swap_ref[rows : rows + 16, :rows].astype(F32)
    scores = jnp.concatenate(
        [as_columns(score_ref[...]), as_columns(marks[0:1, :] + marks[1:2, :])], axis=0
    )
    low = dot(both[...], half_ref[...])
    scaled = [
        low[:, k : k + LANES] * scores for k in range(0, rank, LANES)
    ]
    lane = iota((2 * rows, LANES), 1)
    scaled.append(jnp.where(lane < 4, scores, 0.0))
    scaled = jnp.concatenate(scaled, axis=1).astype(BF16)
    grad_ref[...] = dot(both[...], scaled, TN)
    user_half_ref[:16, :] = dot(user_ref[...], half_ref[...])
    user_half_ref[16:, :] = dot(swap_ref[rows + 16 :, :], half_ref[...])
    here = iota((part, width), 1) == dp * part + iota((part, width), 0)
    tail_ref[:, :rank] = dot(here.astype(BF16), v_ref[...], NT)
    lane = iota((part, LANES), 1)
    w_col = jnp.sum(jnp.where(here, w_row, 0.0), axis=1, keepdims=True)
    b_col = jnp.sum(jnp.where(here, bias_ref[...], 0.0), axis=1, keepdims=True)
    tail_ref[:, rank:] = jnp.where(lane == 0, w_col, jnp.where(lane == 1, b_col, 0.0))


def pick_kernel(slots_ref, out_ref, wide):
    req = out_ref.shape[0]
    piece = slots_ref.shape[2] - LANES
    wide[...] = slots_ref[...].astype(F32)
    extra = wide[:, 0, piece:].astype(BF16)
    lane = iota(extra.shape, 1)
    order = jnp.where(lane < req, extra.astype(F32), 0.0).astype(BF16)[:, :req]
    for p in range(PIECES):
        got = wide[:, p, :piece].astype(BF16)
        out_ref[:, p * piece : (p + 1) * piece] = dot(order, got, TN).astype(BF16)
    out_ref[:, PIECES * piece :] = dot(order, extra, TN).astype(BF16)


def total_of(pack, width, req):
    at = width + req
    return pack[:, at : at + 1].astype(F32) + pack[:, at + 1 : at + 2].astype(F32)


def merge_kernel(grad_ref, own_ref, other_ref, user_ref, swap_ref, half_ref, user_half_ref, out_ref):
    req, width = user_ref.shape
    rank = half_ref.shape[1]
    peers = out_ref.shape[0]
    half = half_ref[...]
    lines, factors = [], []
    lane = iota((req, LANES), 1)
    for at, pack_ref, user in (
        (0, own_ref, user_ref[...]),
        (req, other_ref, swap_ref[...]),
    ):
        pack = pack_ref[...]
        sums = pack[:, :width]
        total = total_of(pack, width, req)
        user_half = user_half_ref[at : at + req, :]
        both = dot(sums, half) + total * user_half
        lines += [sums, user]
        factors += [
            jnp.concatenate([user_half, jnp.zeros((req, LANES), F32)], axis=1),
            jnp.concatenate([both, jnp.where(lane < 4, total, 0.0)], axis=1),
        ]
    lines = jnp.concatenate(lines, axis=0)
    factors = jnp.concatenate(factors, axis=0).astype(BF16)
    grad = grad_ref[...] + dot(lines, factors, TN)
    blocks = grad.reshape(peers, 4, 8, rank + LANES)
    lane = iota((peers, 8, LANES), 2)
    sums = jnp.zeros((peers, 8, LANES), F32)
    for q in range(4):
        out_ref[:, :, q * rank : (q + 1) * rank] = blocks[:, q, :, :rank].astype(BF16)
        sums = jnp.where(lane == q, blocks[:, q, :, rank:], sums)
    out_ref[:, :, 4 * rank :] = sums.astype(BF16)


def user_grad_kernel(pack_ref, user_ref, u_ref, v_ref, vw_ref, bias_ref, w_ref, out_ref):
    req, width = user_ref.shape
    pack = pack_ref[...]
    sums = pack[:, :width]
    total = total_of(pack, width, req)
    user = user_ref[...]
    u, vw = u_ref[...], vw_ref[...]
    low = dot(sums, u) + total * dot(user, u)
    grad_low = dot(sums, vw, NT) + total * dot(user, vw, NT)
    w_row = w_ref[...].astype(F32)
    out_ref[...] = (
        w_row * (dot(low.astype(BF16), v_ref[...]) + total * (bias_ref[...] + 1.0))
        + dot(grad_low.astype(BF16), u, NT)
    )


def sum_kernel(in_ref, out_ref):
    total = jnp.sum(in_ref[...].astype(F32), axis=0).astype(BF16)
    out_ref[...] = jnp.broadcast_to(total[None], out_ref.shape)


def last_kernel(factor, in_ref, tail_ref, grad_u_ref, grad_vt_ref, bias_ref, out_ref):
    part, rank = grad_u_ref.shape
    replicas = in_ref.shape[0]
    sums = [
        sum(in_ref[k].astype(F32) for k in range(core, replicas, 2)) * factor for core in (0, 1)
    ]
    low, grad_low = (
        jnp.concatenate([s[:, q * rank : (q + 1) * rank] for q in range(4)], axis=0) for s in sums
    )
    column = jnp.concatenate(
        [sums[0][:, 4 * rank + q : 4 * rank + q + 1] for q in range(4)], axis=0
    )
    tail = tail_ref[...]
    w_col, b_col = tail[:, rank : rank + 1], tail[:, rank + 1 : rank + 2]
    grad_u_ref[...] = grad_low
    grad_vt_ref[...] = w_col * low
    out_col = jnp.sum(tail[:, :rank] * low, axis=1, keepdims=True) + (b_col + 1.0) * column
    bias_ref[...] = jnp.transpose(jnp.broadcast_to(w_col * column, (part, LANES)))[0:1, :]
    out_ref[...] = jnp.transpose(jnp.broadcast_to(out_col, (part, LANES)))[0:1, :]


def call(kernel, out, *args, scratch=(), scalars=0):
    specs = [pl.BlockSpec(memory_space=pltpu.SMEM)] * scalars
    specs += [pl.BlockSpec(memory_space=pltpu.VMEM)] * (len(args) - scalars)
    return pl.pallas_call(
        kernel,
        out_shape=out,
        in_specs=specs,
        out_specs=jax.tree.map(lambda _: pl.BlockSpec(memory_space=pltpu.VMEM), out),
        scratch_shapes=list(scratch),
        compiler_params=PARAMS,
    )(*args)


def per_device(
    user_rows, user_row, segment, cand_feat, grad_score, u_weight, v_weight, bias, w_out
):
    user, feat, seg = user_rows[0], cand_feat[0], segment[0]
    peers, replicas = lax.axis_size("dp"), lax.axis_size("replica")
    req, width = user.shape
    rows = feat.shape[0]
    rank = u_weight.shape[1]
    part = width // peers
    piece = width // PIECES
    shape = jax.ShapeDtypeStruct
    bias, w_out = bias[None], w_out[None]
    pairs = [(i, i ^ 1) for i in range(replicas)]
    at = jnp.stack([lax.axis_index("dp"), lax.axis_index("replica") % 2]).astype(jnp.int32)

    slots, swap = call(
        request_kernel,
        (
            shape((peers, PIECES, piece + LANES), BF16),
            shape((rows + 16 + req, width), BF16),
        ),
        user_row, seg, grad_score, feat, user,
        scratch=[pltpu.VMEM((peers, PIECES, piece + LANES), F32)],
    )
    arrived = lax.all_to_all(slots, "dp", split_axis=0, concat_axis=0, tiled=True)
    swapped = lax.ppermute(swap, "replica", pairs)
    grad, half, vw, user_half, tail = call(
        main_kernel,
        (
            shape((width, rank + LANES), F32),
            shape((width, rank), BF16),
            shape((rank, width), BF16),
            shape((2 * req, rank), F32),
            shape((part, rank + LANES), F32),
        ),
        at, feat, grad_score, user, swapped, u_weight, v_weight, bias, w_out,
        scratch=[pltpu.VMEM((2 * rows, width), BF16)],
        scalars=1,
    )
    own = call(
        pick_kernel,
        shape((req, width + LANES), BF16),
        arrived,
        scratch=[pltpu.VMEM((peers, PIECES, piece + LANES), F32)],
    )
    other = lax.ppermute(own, "replica", pairs)
    parts = call(
        merge_kernel,
        shape((peers, 8, 4 * rank + LANES), BF16),
        grad, own, other, user, swapped[rows + 16 :], half, user_half,
    )
    received = lax.all_to_all(parts, "dp", split_axis=0, concat_axis=0, tiled=True)
    user_grad = call(
        user_grad_kernel,
        shape((req, width), F32),
        own, user, u_weight, v_weight, vw, bias, w_out,
    )
    copies = call(sum_kernel, shape((replicas, 8, 4 * rank + LANES), BF16), received)
    gathered = lax.all_to_all(copies, "replica", split_axis=0, concat_axis=0, tiled=True)
    factor = 1.0 / math.sqrt(rows * peers * replicas)
    grad_u, grad_vt, grad_bias, grad_out = call(
        functools.partial(last_kernel, factor),
        (
            shape((part, rank), F32),
            shape((part, rank), F32),
            shape((1, part), F32),
            shape((1, part), F32),
        ),
        gathered, tail,
    )
    return (user_grad[None], grad_u, grad_vt, grad_bias[0], grad_out[0])


def solution(mesh):
    placed = (
        P("replica", "dp", None),
        P("replica", "dp"),
        P("replica", "dp", None),
        P("replica", "dp", None),
        P("replica", "dp"),
        P(),
        P(),
        P(),
        P(),
    )
    return jax.shard_map(
        per_device,
        mesh=mesh,
        in_specs=placed,
        out_specs=(P("replica", "dp", None), P("dp", None), P("dp", None), P("dp"), P("dp")),
        check_vma=False,
    )
```

time: 531 us -> 122 us (0.23)
  blocking collectives: 318 us -> 36.7 us
  waiting for transfers between devices: 129 us -> 24.9 us
  other arithmetic: 17.6 us -> 0.08 us
  starting transfers between devices: 23.5 us -> 38.6 us
  between operations: 15 us -> 0.79 us
  local copies, waits for them, and re-layouts: 20.5 us -> 7.44 us
  Pallas kernels: 0 us -> 12.5 us
  matrix products: 6.66 us -> 0 us
    unnamed x1 -> x0, blocking collectives: 225 us -> none
    psum x1 -> x0, waiting for transfers between devices: 107 us -> none  [per_device(): summed, bias_sum, out_sum = lax.psum((summed, bias_sum, out_sum), 'replica')]
    psum x1 -> x0, blocking collectives: 93.6 us -> none  [per_device(): summed, bias_sum, out_sum = lax.psum((summed, bias_sum, out_sum), 'replica')]
    all_to_all x0 -> x1, blocking collectives: none -> 36.7 us  [per_device(): lax.all_to_all(parts, 'dp', split_axis=0, concat_axis=0, tiled=True)]
    ppermute x0 -> x2, starting transfers between devices: none -> 19.6 us  [the longest x1 16.1 us: per_device(): swapped = lax.ppermute(swap, 'replica', pairs)]
    pallas_call x0 -> x7, Pallas kernels: none -> 12.5 us  [call(): pl.pallas_call(kernel, out_shape=out, in_specs=specs, out_specs=jax.tree....]
    unnamed x25 -> x30, local copies, waits for them, and re-layouts: 13.3 us -> 6.58 us
    dot_general x8 -> x0, matrix products: 6.66 us -> none  [the longest x1 2.97 us: per_device(): jnp.dot(scores[None, :], crossed, precision=lax.Precision.HIGHEST, prefer...]
  transfers between devices with their start and end apart: 5 -> 4, of which waited for: 3 -> 2; matrix products, arithmetic and copies ran while one was open for 3% -> 1% of each run, Pallas kernels for 0% -> 7%
where the time goes in v1:
time: 122 us; the launch traced here: 121 us
  starting transfers between devices  38.6 us (32%)
  blocking collectives  36.7 us (30%)
  waiting for transfers between devices  24.9 us (20%)
  Pallas kernels  12.5 us (10%)
  local copies, waits for them, and re-layouts  7.44 us (6%)
    all_to_all x1, blocking collectives, per_device(): lax.all_to_all(parts, 'dp', split_axis=0, concat_axis=0, tiled=True)  36.7 us
    ppermute x1, starting transfers between devices, per_device(): swapped = lax.ppermute(swap, 'replica', pairs)  16.1 us
    all_to_all x1, waiting for transfers between devices, per_device(): lax.all_to_all(slots, 'dp', split_axis=0, concat_axis=0, tiled=True)  15.8 us
    all_to_all x1, starting transfers between devices, per_device(): lax.all_to_all(copies, 'replica', split_axis=0, concat_axis=0, tiled=True)  14.3 us
    pallas_call x7, Pallas kernels, call(): pl.pallas_call(kernel, out_shape=out, in_specs=specs, out_specs=jax.tree....  12.5 us
    all_to_all x1, waiting for transfers between devices, per_device(): lax.all_to_all(copies, 'replica', split_axis=0, concat_axis=0, tiled=True)  9.14 us
    unnamed x30, local copies, waits for them, and re-layouts  6.58 us
    all_to_all x1, starting transfers between devices, per_device(): lax.all_to_all(slots, 'dp', split_axis=0, concat_axis=0, tiled=True)  4.64 us
  transfers between devices with their start and end apart: 4, of which 2 were waited for; matrix products, arithmetic and copies ran while one was open for 1% of the time, Pallas kernels for 7%

profile of v1, /device:TPU:1, one launch (start us, length us, event | category | flops | bytes accessed | tf_op | source)
XLA Modules:
  0.0 121.0 jit_solution(5208015625508491765)
XLA Ops:
  0.7 1.2 %copy-done = bf16[1,256,2048]{2,1,0:T(8,128)(2,1)S(1)} copy-done((bf16[1,256,2048]{2,1,0:T(8,128)(2,1)S(1)}, bf16[1,256,2048]{2,1,0:T(8,128)(2,1)}, u32[]{:S(2)}) %copy-start) | copy-done | bytes 1048600
  1.9 0.8 copy-done.5
  2.7 0.7 copy-done.10
  3.4 0.7 copy-done.12
  4.1 0.7 copy-done.13
  4.8 1.7 %shard_map.128 = (bf16[64,8,384]{2,1,0:T(8,128)(2,1)}, bf16[288,2048]{1,0:T(8,128)(2,1)}) custom-call(s32[1,16]{1,0:T(1,128)S(1)} %copy-done.13, s32[1,256]{1,0:T(1,128)S(1)} %bitcast.17, f32[1,256]{1,0:T(1,128)S(1)} %copy-done.10, bf16[256,2048]{1,0:T(8,128)(2,1)S(1)} %bitcast.9, bf16[16,2048]{1,0:T(8,128)(2,1)S(1)} %bitcast.11), custom_call_target="tpu_custom_call" | custom-call | tf_op jit(solution)/shard_map/pallas_call | solution.py:214
  6.5 16.1 %collective-permute-start = (bf16[288,2048]{1,0:T(8,128)(2,1)}, bf16[288,2048]{1,0:T(8,128)(2,1)}, u32[]{:S(2)}, u32[]{:S(2)}) collective-permute-start(bf16[288,2048]{1,0:T(8,128)(2,1)} %get-tuple-element.17), channel_id=1, source_target_pairs={{0,1},{1,0},{2,3},{3,2},{4,5},{5,4},{6,7},{7,6},{8,9},{9,8},{10,11... | collective-permute-start | bytes 3538952 | tf_op jit(solution)/shard_map/ppermute | solution.py:249
  22.6 4.6 %all-to-all-start = ((bf16[64,8,384]{2,1,0:T(8,128)(2,1)}), bf16[64,8,384]{2,1,0:T(8,128)(2,1)S(1)}, u32[]{:S(2)}, u32[]{:S(2)}) async-start(bf16[64,8,384]{2,1,0:T(8,128)(2,1)} %get-tuple-element.16), calls=%async_computation | async-start | bytes 786432 | tf_op jit(solution)/shard_map/all_to_all | solution.py:248
  27.2 15.8 %all-to-all-done.slots_ref = bf16[64,8,384]{2,1,0:T(8,128)(2,1)S(1)} async-done(((bf16[64,8,384]{2,1,0:T(8,128)(2,1)}), bf16[64,8,384]{2,1,0:T(8,128)(2,1)S(1)}, u32[]{:S(2)}, u32[]{:S(2)}) %all-to-all-start) | async-done | bytes 393248 | tf_op jit(solution)/shard_map/all_to_all | solution.py:248
  43.0 0.7 shard_map.129.pack_ref.own_ref
  43.8 3.6 %collective-permute-start.1 = (bf16[16,2176]{1,0:T(8,128)(2,1)S(1)}, bf16[16,2176]{1,0:T(8,128)(2,1)S(1)}, u32[]{:S(2)}, u32[]{:S(2)}) collective-permute-start(bf16[16,2176]{1,0:T(8,128)(2,1)S(1)} %shard_map.129.pack_ref.own_ref), channel_id=1, source_target_pairs={{0,1},{1,0},{2,3},{3,2},{4,5},{5,4},{6,7},{7,6},{8,9},{9,8},{10,11... | collective-permute-start | bytes 208904 | tf_op jit(solution)/shard_map/ppermute | solution.py:269
  47.4 0.1 pad_add_fusion.at_ref
  47.4 0.8 slice.4.swap_ref
  48.3 1.2 %copy-done.3 = bf16[256,2048]{1,0:T(8,128)(2,1)S(1)} copy-done((bf16[256,2048]{1,0:T(8,128)(2,1)S(1)}, bf16[256,2048]{1,0:T(8,128)(2,1)}, u32[]{:S(2)}) %copy-start.3) | copy-done | bytes 1048600
  49.6 5.3 %shard_map.130 = (f32[2048,384]{1,0:T(8,128)S(1)}, bf16[2048,256]{1,0:T(8,128)(2,1)S(1)}, bf16[256,2048]{1,0:T(8,128)(2,1)S(1)}, f32[32,256]{1,0:T(8,128)S(1)}, f32[32,384]{1,0:T(8,128)S(1)}) custom-call(s32[2]{0:T(128)S(1)} %pad_add_fusion.at_ref, bf16[256,2048]{1,0:T(8,128)(2,1)S(1)} %bitcast.10, f32[1,256]{1,0:T(1,128)S(1)} %copy-done.11, ...), custom_call_target="tpu_custom_call" | custom-call | tf_op jit(solution)/shard_map/pallas_call | solution.py:214
  54.9 0.9 shard_map.132
  55.8 0.0 copy-done.7
  55.9 36.7 %all_to_all.15.in_ref = bf16[64,8,1152]{2,1,0:T(8,128)(2,1)S(1)} all-to-all(bf16[64,8,1152]{2,1,0:T(8,128)(2,1)S(1)} %shard_map.132), channel_id=1, replica_groups=mesh['dp'=64,'replica'=16] {'dp'}, dimensions={0} | all-to-all | bytes 2359296 | tf_op jit(solution)/shard_map/all_to_all | solution.py:275
  92.6 0.9 shard_map.133
  93.5 14.3 %all-to-all-start.2 = ((bf16[16,8,1152]{2,1,0:T(8,128)(2,1)}), bf16[16,8,1152]{2,1,0:T(8,128)(2,1)S(1)}, u32[]{:S(2)}, u32[]{:S(2)}) async-start(bf16[16,8,1152]{2,1,0:T(8,128)(2,1)} %shard_map.133), calls=%async_computation.2 | async-start | bytes 589824 | tf_op jit(solution)/shard_map/all_to_all | solution.py:282
  107.8 1.2 %copy-done.8 = bf16[256,2048]{1,0:T(8,128)(2,1)S(1)} copy-done((bf16[256,2048]{1,0:T(8,128)(2,1)S(1)}, bf16[256,2048]{1,0:T(8,128)(2,1)}, u32[]{:S(2)}) %copy-start.8) | copy-done | bytes 1048600
  109.0 2.0 %shard_map.131 = f32[16,2048]{1,0:T(8,128)} custom-call(bf16[16,2176]{1,0:T(8,128)(2,1)S(1)} %shard_map.129.pack_ref.own_ref, bf16[16,2048]{1,0:T(8,128)(2,1)S(1)} %bitcast.14, bf16[2048,256]{1,0:T(8,128)(2,1)S(1)} %copy-done.2, bf16[256,2048]{1,0:T(8,128)(2,1)S(1)} %copy-done.4, bf16[256,2048]{1,0:T(8,128)(2,1)S(1)} %copy-done.8, f32[1,2048]{1,0:T(1,128)S(1)} %bitcast.16, ...), custom_call_target="tpu_custom_call" | custom-call | tf_op jit(solution)/shard_map/pallas_call | solution.py:214
  111.0 9.1 %all-to-all-done.2.in_ref = bf16[16,8,1152]{2,1,0:T(8,128)(2,1)S(1)} async-done(((bf16[16,8,1152]{2,1,0:T(8,128)(2,1)}), bf16[16,8,1152]{2,1,0:T(8,128)(2,1)S(1)}, u32[]{:S(2)}, u32[]{:S(2)}) %all-to-all-start.2) | async-done | bytes 294944 | tf_op jit(solution)/shard_map/all_to_all | solution.py:282
  120.1 0.8 shard_map.134
  (25 shorter events, 0.1 us)
Async XLA Ops:
  0.6 26.6 %copy-start.14 = (bf16[2048]{0:T(1024)(128)(2,1)S(1)}, bf16[2048]{0:T(1024)(128)(2,1)}, u32[]{:S(2)}) copy-start(bf16[2048]{0:T(1024)(128)(2,1)} %param.17) | copy-start | bytes 12292
  0.6 1.2 %copy-start = (bf16[1,256,2048]{2,1,0:T(8,128)(2,1)S(1)}, bf16[1,256,2048]{2,1,0:T(8,128)(2,1)}, u32[]{:S(2)}) copy-start(bf16[1,256,2048]{2,1,0:T(8,128)(2,1)} %param.12) | copy-start | bytes 3145732
  1.9 0.8 copy-start.5
  2.7 0.7 copy-start.10
  3.4 0.7 copy-start.12
  4.1 0.7 copy-start.13
  4.7 43.6 %copy-start.1 = (bf16[1,256,2048]{2,1,0:T(8,128)(2,1)S(1)}, bf16[1,256,2048]{2,1,0:T(8,128)(2,1)}, u32[]{:S(2)}) copy-start(bf16[1,256,2048]{2,1,0:T(8,128)(2,1)} %param.12) | copy-start | bytes 3145732
  4.7 43.6 %copy-start.2 = (bf16[2048,256]{1,0:T(8,128)(2,1)S(1)}, bf16[2048,256]{1,0:T(8,128)(2,1)}, u32[]{:S(2)}) copy-start(bf16[2048,256]{1,0:T(8,128)(2,1)} %u_ref.3) | copy-start | bytes 3145732
  4.7 43.6 %copy-start.6 = (bf16[1,16,2048]{2,1,0:T(8,128)(2,1)S(1)}, bf16[1,16,2048]{2,1,0:T(8,128)(2,1)}, u32[]{:S(2)}) copy-start(bf16[1,16,2048]{2,1,0:T(8,128)(2,1)} %param.9) | copy-start | bytes 196612
  4.7 43.6 %copy-start.9 = (f32[2048]{0:T(1024)S(1)}, f32[2048]{0:T(1024)}, u32[]{:S(2)}) copy-start(f32[2048]{0:T(1024)} %param.16) | copy-start | bytes 24580
  4.7 43.6 %copy-start.11 = (f32[1,256]{1,0:T(1,128)S(1)}, f32[1,256]{1,0:T(1,128)}, u32[]{:S(2)}) copy-start(f32[1,256]{1,0:T(1,128)} %score_ref.3) | copy-start | bytes 3076
  6.5 41.0 %collective-permute-start = (bf16[288,2048]{1,0:T(8,128)(2,1)}, bf16[288,2048]{1,0:T(8,128)(2,1)}, u32[]{:S(2)}, u32[]{:S(2)}) collective-permute-start(bf16[288,2048]{1,0:T(8,128)(2,1)} %get-tuple-element.17), channel_id=1, source_target_pairs={{0,1},{1,0},{2,3},{3,2},{4,5},{5,4},{6,7},{7,6},{8,9},{9,8},{10,11... | collective-permute-start | bytes 3538952 | tf_op jit(solution)/shard_map/ppermute | solution.py:249
  22.6 20.5 %all-to-all-start = ((bf16[64,8,384]{2,1,0:T(8,128)(2,1)}), bf16[64,8,384]{2,1,0:T(8,128)(2,1)S(1)}, u32[]{:S(2)}, u32[]{:S(2)}) async-start(bf16[64,8,384]{2,1,0:T(8,128)(2,1)} %get-tuple-element.16), calls=%async_computation | async-start | bytes 786432 | tf_op jit(solution)/shard_map/all_to_all | solution.py:248
  43.8 11.1 %collective-permute-start.1 = (bf16[16,2176]{1,0:T(8,128)(2,1)S(1)}, bf16[16,2176]{1,0:T(8,128)(2,1)S(1)}, u32[]{:S(2)}, u32[]{:S(2)}) collective-permute-start(bf16[16,2176]{1,0:T(8,128)(2,1)S(1)} %shard_map.129.pack_ref.own_ref), channel_id=1, source_target_pairs={{0,1},{1,0},{2,3},{3,2},{4,5},{5,4},{6,7},{7,6},{8,9},{9,8},{10,11... | collective-permute-start | bytes 208904 | tf_op jit(solution)/shard_map/ppermute | solution.py:269
  48.3 1.2 %copy-start.3 = (bf16[256,2048]{1,0:T(8,128)(2,1)S(1)}, bf16[256,2048]{1,0:T(8,128)(2,1)}, u32[]{:S(2)}) copy-start(bf16[256,2048]{1,0:T(8,128)(2,1)} %v_ref.3) | copy-start | bytes 3145732
  54.9 1.0 copy-start.7
  92.6 15.2 %copy-start.4 = (bf16[256,2048]{1,0:T(8,128)(2,1)S(1)}, bf16[256,2048]{1,0:T(8,128)(2,1)}, u32[]{:S(2)}) copy-start(bf16[256,2048]{1,0:T(8,128)(2,1)} %v_ref.3) | copy-start | bytes 3145732
  93.5 26.6 %all-to-all-start.2 = ((bf16[16,8,1152]{2,1,0:T(8,128)(2,1)}), bf16[16,8,1152]{2,1,0:T(8,128)(2,1)S(1)}, u32[]{:S(2)}, u32[]{:S(2)}) async-start(bf16[16,8,1152]{2,1,0:T(8,128)(2,1)} %shard_map.133), calls=%async_computation.2 | async-start | bytes 589824 | tf_op jit(solution)/shard_map/all_to_all | solution.py:282
  107.8 1.2 %copy-start.8 = (bf16[256,2048]{1,0:T(8,128)(2,1)S(1)}, bf16[256,2048]{1,0:T(8,128)(2,1)}, u32[]{:S(2)}) copy-start(bf16[256,2048]{1,0:T(8,128)(2,1)} %copy-done.7) | copy-start | bytes 3145732

commit v2 on v1

--- a/solution.py
+++ b/solution.py
@@ -11,10 +11,9 @@
 F32 = jnp.float32
 BF16 = jnp.bfloat16
 LANES = 128
-PIECES = 8
+PIECES = 2
 NT = (((1,), (1,)), ((), ()))
 TN = (((0,), (0,)), ((), ()))
-PARAMS = pltpu.CompilerParams(vmem_limit_bytes=40 << 20)
 
 
 def dot(a, b, dims=(((1,), (0,)), ((), ()))):
@@ -34,10 +33,11 @@
     return jnp.transpose(jnp.broadcast_to(row, (LANES, row.shape[1])))
 
 
-def request_kernel(wanted_ref, seg_ref, score_ref, feat_ref, user_ref, slots_ref, swap_ref, wide):
+def request_kernel(wait, wanted_ref, seg_ref, score_ref, feat_ref, slots_ref, wide):
     peers, req = slots_ref.shape[0], wanted_ref.shape[1]
     rows, width = feat_ref.shape
     piece = width // PIECES
+    wait(0, 1, 2)
     wanted = wanted_ref[...]
     owner = lax.div(wanted, jnp.int32(req))
     local = wanted - owner * req
@@ -57,12 +57,19 @@
     extra = dot(to_owner, place, NT) + dot(to_owner, totals)
     weights = jnp.where(mine, scores, 0.0).astype(BF16)
     weights = dot(to_owner, weights).astype(BF16)
-    wide[:, :, piece:] = jnp.zeros((peers, PIECES, LANES), F32)
     wide[:, 0, piece:] = extra
+    for p in range(1, PIECES):
+        wide[:, p, piece:] = jnp.zeros((peers, LANES), F32)
+    wait(3)
     for p in range(PIECES):
         wide[:, p, :piece] = dot(weights, feat_ref[:, p * piece : (p + 1) * piece])
     slots_ref[...] = wide[...].astype(BF16)
-    score_high, score_low = split_in_two(scores)
+
+
+def swap_kernel(wait, slots_any, feat_ref, score_ref, user_ref, swap_ref):
+    wait(1, 2, 3)
+    rows, width = feat_ref.shape
+    score_high, score_low = split_in_two(score_ref[...])
     line = iota((16, rows), 0)
     swap_ref[:rows, :] = feat_ref[...]
     swap_ref[rows : rows + 16, :] = jnp.zeros((16, width), BF16)
@@ -74,10 +81,22 @@
     swap_ref[rows + 16 :, :] = user_ref[...]
 
 
+def lay_out(grad, out_ref, base, base_sums):
+    peers, rank = out_ref.shape[0], grad.shape[1] - LANES
+    blocks = grad.reshape(peers, 4, 8, rank + LANES)
+    lane = iota((peers, 8, LANES), 2)
+    sums = jnp.zeros((peers, 8, LANES), F32)
+    for q in range(4):
+        out_ref[:, :, q * rank : (q + 1) * rank] = (blocks[:, q, :, :rank] + base(q)).astype(BF16)
+        sums = jnp.where(lane == q, blocks[:, q, :, rank:], sums)
+    out_ref[:, :, 4 * rank :] = (sums + base_sums).astype(BF16)
+
+
 def main_kernel(
-    at_ref, feat_ref, score_ref, user_ref, swap_ref, u_ref, v_ref, bias_ref, w_ref,
-    grad_ref, half_ref, vw_ref, user_half_ref, tail_ref, both,
+    wait, at_ref, feat_ref, score_ref, user_ref, swap_ref, u_ref, v_ref, bias_ref, w_ref,
+    base_ref, half_ref, vw_ref, users_ref, user_half_ref, tail_ref, both,
 ):
+    wait(*range(1, 9))
     dp, core = at_ref[0], at_ref[1]
     rows, width = feat_ref.shape
     rank = v_ref.shape[0]
@@ -104,9 +123,10 @@
     lane = iota((2 * rows, LANES), 1)
     scaled.append(jnp.where(lane < 4, scores, 0.0))
     scaled = jnp.concatenate(scaled, axis=1).astype(BF16)
-    grad_ref[...] = dot(both[...], scaled, TN)
-    user_half_ref[:16, :] = dot(user_ref[...], half_ref[...])
-    user_half_ref[16:, :] = dot(swap_ref[rows + 16 :, :], half_ref[...])
+    lay_out(dot(both[...], scaled, TN), base_ref, lambda q: 0.0, 0.0)
+    users_ref[:16, :] = user_ref[...]
+    users_ref[16:, :] = swap_ref[rows + 16 :, :]
+    user_half_ref[...] = dot(users_ref[...], half_ref[...])
     here = iota((part, width), 1) == dp * part + iota((part, width), 0)
     tail_ref[:, :rank] = dot(here.astype(BF16), v_ref[...], NT)
     lane = iota((part, LANES), 1)
@@ -115,7 +135,7 @@
     tail_ref[:, rank:] = jnp.where(lane == 0, w_col, jnp.where(lane == 1, b_col, 0.0))
 
 
-def pick_kernel(slots_ref, out_ref, wide):
+def pick_kernel(wait, slots_ref, tail_any, out_ref, wide):
     req = out_ref.shape[0]
     piece = slots_ref.shape[2] - LANES
     wide[...] = slots_ref[...].astype(F32)
@@ -133,16 +153,16 @@
     return pack[:, at : at + 1].astype(F32) + pack[:, at + 1 : at + 2].astype(F32)
 
 
-def merge_kernel(grad_ref, own_ref, other_ref, user_ref, swap_ref, half_ref, user_half_ref, out_ref):
-    req, width = user_ref.shape
+def merge_kernel(wait, base_ref, own_ref, other_ref, users_ref, half_ref, user_half_ref, out_ref):
+    req, width = users_ref.shape[0] // 2, users_ref.shape[1]
     rank = half_ref.shape[1]
-    peers = out_ref.shape[0]
+    wait(3, 4, 5)
     half = half_ref[...]
     lines, factors = [], []
     lane = iota((req, LANES), 1)
     for at, pack_ref, user in (
-        (0, own_ref, user_ref[...]),
-        (req, other_ref, swap_ref[...]),
+        (0, own_ref, users_ref[:req, :]),
+        (req, other_ref, users_ref[req:, :]),
     ):
         pack = pack_ref[...]
         sums = pack[:, :width]
@@ -156,17 +176,17 @@
         ]
     lines = jnp.concatenate(lines, axis=0)
     factors = jnp.concatenate(factors, axis=0).astype(BF16)
-    grad = grad_ref[...] + dot(lines, factors, TN)
-    blocks = grad.reshape(peers, 4, 8, rank + LANES)
-    lane = iota((peers, 8, LANES), 2)
-    sums = jnp.zeros((peers, 8, LANES), F32)
-    for q in range(4):
-        out_ref[:, :, q * rank : (q + 1) * rank] = blocks[:, q, :, :rank].astype(BF16)
-        sums = jnp.where(lane == q, blocks[:, q, :, rank:], sums)
-    out_ref[:, :, 4 * rank :] = sums.astype(BF16)
-
-
-def user_grad_kernel(pack_ref, user_ref, u_ref, v_ref, vw_ref, bias_ref, w_ref, out_ref):
+    wait(0)
+    lay_out(
+        dot(lines, factors, TN),
+        out_ref,
+        lambda q: base_ref[:, :, q * rank : (q + 1) * rank].astype(F32),
+        base_ref[:, :, 4 * rank :].astype(F32),
+    )
+
+
+def user_grad_kernel(wait, pack_ref, user_ref, u_ref, v_ref, vw_ref, bias_ref, w_ref, out_ref):
+    wait(*range(1, 7))
     req, width = user_ref.shape
     pack = pack_ref[...]
     sums = pack[:, :width]
@@ -182,12 +202,13 @@
     )
 
 
-def sum_kernel(in_ref, out_ref):
+def sum_kernel(wait, in_ref, out_ref):
     total = jnp.sum(in_ref[...].astype(F32), axis=0).astype(BF16)
     out_ref[...] = jnp.broadcast_to(total[None], out_ref.shape)
 
 
-def last_kernel(factor, in_ref, tail_ref, grad_u_ref, grad_vt_ref, bias_ref, out_ref):
+def last_kernel(factor, wait, in_ref, tail_ref, grad_u_ref, grad_vt_ref, bias_ref, out_ref):
+    wait(1)
     part, rank = grad_u_ref.shape
     replicas = in_ref.shape[0]
     sums = [
@@ -208,16 +229,69 @@
     out_ref[...] = jnp.transpose(jnp.broadcast_to(out_col, (part, LANES)))[0:1, :]
 
 
-def call(kernel, out, *args, scratch=(), scalars=0):
-    specs = [pl.BlockSpec(memory_space=pltpu.SMEM)] * scalars
-    specs += [pl.BlockSpec(memory_space=pltpu.VMEM)] * (len(args) - scalars)
+def call(kernel, out, *args, places="", out_places="", scratch=(), room=24, cost=None):
+    spaces = {"s": pltpu.SMEM, "a": pl.ANY, "h": pltpu.HBM, "n": pl.ANY, "-": pltpu.VMEM}
+    several = isinstance(out, tuple)
+    outs = out if several else (out,)
+    places = places + "-" * (len(args) - len(places))
+    out_places = out_places + "-" * (len(outs) - len(out_places))
+    staged = [k for k, place in enumerate(places) if place in "hn"]
+    late = [k for k, place in enumerate(out_places) if place in "hn"]
+    args = [
+        pltpu.with_memory_space_constraint(arg, pltpu.HBM) if place == "h" else arg
+        for arg, place in zip(args, places)
+    ]
+    n_in, n_out, n_scratch = len(args), len(outs), len(scratch)
+
+    def body(*refs):
+        refs = list(refs)
+        ins, results = refs[:n_in], refs[n_in : n_in + n_out]
+        rest = refs[n_in + n_out :]
+        own, rest = rest[:n_scratch], rest[n_scratch:]
+        buffers, rest = rest[: len(staged)], rest[len(staged) :]
+        out_buffers, rest = rest[: len(late)], rest[len(late) :]
+        copies = {}
+        for at, k in enumerate(staged):
+            copies[k] = pltpu.make_async_copy(ins[k], buffers[at], rest[0].at[at])
+            copies[k].start()
+            ins[k] = buffers[at]
+        targets = {}
+        for at, k in enumerate(late):
+            targets[k] = results[k]
+            results[k] = out_buffers[at]
+
+        def wait(*which):
+            for k in which:
+                copies.pop(k).wait()
+
+        kernel(wait, *ins, *results, *own)
+        assert not copies
+        ends = [
+            pltpu.make_async_copy(results[k], targets[k], rest[-1].at[at])
+            for at, k in enumerate(late)
+        ]
+        for copy in ends:
+            copy.start()
+        for copy in ends:
+            copy.wait()
+
+    def like(x):
+        return pltpu.VMEM(x.shape, x.dtype)
+
+    extra = [like(args[k]) for k in staged] + [like(outs[k]) for k in late]
+    extra += [pltpu.SemaphoreType.DMA((len(group),)) for group in (staged, late) if group]
+    out_specs = tuple(pl.BlockSpec(memory_space=spaces[place]) for place in out_places)
+    pinned = tuple(
+        pltpu.HBM(x.shape, x.dtype) if place == "h" else x for x, place in zip(outs, out_places)
+    )
     return pl.pallas_call(
-        kernel,
-        out_shape=out,
-        in_specs=specs,
-        out_specs=jax.tree.map(lambda _: pl.BlockSpec(memory_space=pltpu.VMEM), out),
-        scratch_shapes=list(scratch),
-        compiler_params=PARAMS,
+        body,
+        out_shape=pinned if several else pinned[0],
+        in_specs=[pl.BlockSpec(memory_space=spaces[place]) for place in places],
+        out_specs=out_specs if several else out_specs[0],
+        scratch_shapes=list(scratch) + extra,
+        compiler_params=pltpu.CompilerParams(vmem_limit_bytes=room << 20),
+        cost_estimate=cost,
     )(*args)
 
 
@@ -236,47 +310,58 @@
     pairs = [(i, i ^ 1) for i in range(replicas)]
     at = jnp.stack([lax.axis_index("dp"), lax.axis_index("replica") % 2]).astype(jnp.int32)
 
-    slots, swap = call(
+    message = (peers, PIECES, piece + LANES)
+    slots = call(
         request_kernel,
-        (
-            shape((peers, PIECES, piece + LANES), BF16),
-            shape((rows + 16 + req, width), BF16),
-        ),
-        user_row, seg, grad_score, feat, user,
-        scratch=[pltpu.VMEM((peers, PIECES, piece + LANES), F32)],
+        shape(message, BF16),
+        user_row, seg, grad_score, feat,
+        places="hhhh",
+        scratch=[pltpu.VMEM(message, F32)],
+    )
+    swap = call(
+        swap_kernel,
+        shape((rows + 16 + req, width), BF16),
+        slots, feat, grad_score, user,
+        places="ahhh",
     )
     arrived = lax.all_to_all(slots, "dp", split_axis=0, concat_axis=0, tiled=True)
     swapped = lax.ppermute(swap, "replica", pairs)
-    grad, half, vw, user_half, tail = call(
+    base, half, vw, users, user_half, tail = call(
         main_kernel,
         (
-            shape((width, rank + LANES), F32),
+            shape((peers, 8, 4 * rank + LANES), BF16),
             shape((width, rank), BF16),
             shape((rank, width), BF16),
+            shape((2 * req, width), BF16),
             shape((2 * req, rank), F32),
             shape((part, rank + LANES), F32),
         ),
         at, feat, grad_score, user, swapped, u_weight, v_weight, bias, w_out,
         scratch=[pltpu.VMEM((2 * rows, width), BF16)],
-        scalars=1,
+        places="shhhnhhhh",
+        out_places="nhhnnn",
+        cost=pl.CostEstimate(flops=1, bytes_accessed=1, transcendentals=0),
     )
     own = call(
         pick_kernel,
         shape((req, width + LANES), BF16),
-        arrived,
-        scratch=[pltpu.VMEM((peers, PIECES, piece + LANES), F32)],
+        arrived, tail,
+        places="-a",
+        scratch=[pltpu.VMEM(message, F32)],
     )
     other = lax.ppermute(own, "replica", pairs)
     parts = call(
         merge_kernel,
         shape((peers, 8, 4 * rank + LANES), BF16),
-        grad, own, other, user, swapped[rows + 16 :], half, user_half,
+        base, own, other, users, half, user_half,
+        places="n--nnn",
     )
     received = lax.all_to_all(parts, "dp", split_axis=0, concat_axis=0, tiled=True)
     user_grad = call(
         user_grad_kernel,
         shape((req, width), F32),
         own, user, u_weight, v_weight, vw, bias, w_out,
+        places="-hhhnhh",
     )
     copies = call(sum_kernel, shape((replicas, 8, 4 * rank + LANES), BF16), received)
     gathered = lax.all_to_all(copies, "replica", split_axis=0, concat_axis=0, tiled=True)
@@ -290,6 +375,7 @@
             shape((1, part), F32),
         ),
         gathered, tail,
+        places="-n",
     )
     return (user_grad[None], grad_u, grad_vt, grad_bias[0], grad_out[0])
 

time: 122 us -> 114 us (0.934)
  waiting for transfers between devices: 24.9 us -> 15.2 us
  Pallas kernels: 12.5 us -> 19.7 us
  local copies, waits for them, and re-layouts: 7.44 us -> 1.84 us
    all_to_all x1, waiting for transfers between devices: 15.8 us -> 5.6 us  [per_device(): lax.all_to_all(slots, 'dp', split_axis=0, concat_axis=0, tiled=True)]
    pallas_call x7 -> x8, Pallas kernels: 12.5 us -> 19.7 us  [call(): pl.pallas_call(body, out_shape=pinned if several else pinned[0], in_specs...]
    unnamed x30 -> x6, local copies, waits for them, and re-layouts: 6.58 us -> 1.23 us
  transfers between devices with their start and end apart: 4 -> 4, of which waited for: 2 -> 3; matrix products, arithmetic and copies ran while one was open for 1% -> 1% of each run, Pallas kernels for 7% -> 10%
where the time goes in v2:
time: 114 us; the launch traced here: 113 us
  starting transfers between devices  39.5 us (35%)
  blocking collectives  36.1 us (32%)
  Pallas kernels  19.7 us (17%)
  waiting for transfers between devices  15.2 us (13%)
  local copies, waits for them, and re-layouts  1.84 us (2%)
    all_to_all x1, blocking collectives, per_device(): lax.all_to_all(parts, 'dp', split_axis=0, concat_axis=0, tiled=True)  36.1 us
    pallas_call x8, Pallas kernels, call(): pl.pallas_call(body, out_shape=pinned if several else pinned[0], in_specs...  19.7 us
    ppermute x1, starting transfers between devices, per_device(): swapped = lax.ppermute(swap, 'replica', pairs)  16.1 us
    all_to_all x1, starting transfers between devices, per_device(): lax.all_to_all(copies, 'replica', split_axis=0, concat_axis=0, tiled=True)  15.3 us
    all_to_all x1, waiting for transfers between devices, per_device(): lax.all_to_all(copies, 'replica', split_axis=0, concat_axis=0, tiled=True)  8.72 us
    all_to_all x1, waiting for transfers between devices, per_device(): lax.all_to_all(slots, 'dp', split_axis=0, concat_axis=0, tiled=True)  5.6 us
    all_to_all x1, starting transfers between devices, per_device(): lax.all_to_all(slots, 'dp', split_axis=0, concat_axis=0, tiled=True)  4.64 us
    ppermute x1, starting transfers between devices, per_device(): other = lax.ppermute(own, 'replica', pairs)  3.48 us
  transfers between devices with their start and end apart: 4, of which 3 were waited for; matrix products, arithmetic and copies ran while one was open for 1% of the time, Pallas kernels for 10%

profile of v2, /device:TPU:1, one launch (start us, length us, event | category | flops | bytes accessed | tf_op | source)
XLA Modules:
  0.0 113.1 jit_solution(1189241525902991067)
XLA Ops:
  0.6 2.6 %shard_map.128.refs_0_ = bf16[64,2,1152]{2,1,0:T(2,128)(2,1)} custom-call(s32[1,16]{1,0:T(1,128)} %refs_0_.1, s32[1,256]{1,0:T(1,128)} %bitcast.18, f32[1,256]{1,0:T(1,128)} %refs_2_.6, bf16[256,2048]{1,0:T(8,128)(2,1)} %bitcast.9), custom_call_target="tpu_custom_call" | custom-call | tf_op jit(solution)/shard_map/pallas_call | solution.py:287
  3.2 0.0 copy-start.2
  3.2 1.3 %shard_map.129 = bf16[288,2048]{1,0:T(8,128)(2,1)S(1)} custom-call(bf16[64,2,1152]{2,1,0:T(2,128)(2,1)} %shard_map.128.refs_0_, bf16[256,2048]{1,0:T(8,128)(2,1)} %bitcast.10, f32[1,256]{1,0:T(1,128)} %refs_2_.6, bf16[16,2048]{1,0:T(8,128)(2,1)} %bitcast.12), custom_call_target="tpu_custom_call" | custom-call | tf_op jit(solution)/shard_map/pallas_call | solution.py:287
  4.6 16.1 %collective-permute-start = (bf16[288,2048]{1,0:T(8,128)(2,1)S(1)}, bf16[288,2048]{1,0:T(8,128)(2,1)S(1)}, u32[]{:S(2)}, u32[]{:S(2)}) collective-permute-start(bf16[288,2048]{1,0:T(8,128)(2,1)S(1)} %shard_map.129), channel_id=1, source_target_pairs={{0,1},{1,0},{2,3},{3,2},{4,5},{5,4},{6,7},{7,6},{8,9},{9,8},{10,11... | collective-permute-start | bytes 3538952 | tf_op jit(solution)/shard_map/ppermute | solution.py:328
  20.7 4.6 %all-to-all-start = ((bf16[64,2,1152]{2,1,0:T(2,128)(2,1)}), bf16[64,2,1152]{2,1,0:T(2,128)(2,1)S(1)}, u32[]{:S(2)}, u32[]{:S(2)}) async-start(bf16[64,2,1152]{2,1,0:T(2,128)(2,1)} %shard_map.128.refs_0_), calls=%async_computation | async-start | bytes 589824 | tf_op jit(solution)/shard_map/all_to_all | solution.py:327
  25.3 0.0 copy-done.2
  25.3 0.6 broadcast_in_dim.10.refs_8_.refs_6_
  25.9 0.1 pad_add_fusion.refs_0_
  26.0 0.0 collective-permute-done.refs_4_
  26.0 8.1 %shard_map.130 = (bf16[64,8,1152]{2,1,0:T(8,128)(2,1)S(1)}, bf16[2048,256]{1,0:T(8,128)(2,1)}, bf16[256,2048]{1,0:T(8,128)(2,1)}, bf16[32,2048]{1,0:T(8,128)(2,1...) custom-call(s32[2]{0:T(128)S(1)} %pad_add_fusion.refs_0_, bf16[256,2048]{1,0:T(8,128)(2,1)} %bitcast.11, ...), custom_call_target="tpu_custom_call" | custom-call | flops 1 | bytes 1 | tf_op jit(solution)/shard_map/pallas_call | solution.py:287
  34.1 5.6 %all-to-all-done.refs_0_ = bf16[64,2,1152]{2,1,0:T(2,128)(2,1)S(1)} async-done(((bf16[64,2,1152]{2,1,0:T(2,128)(2,1)}), bf16[64,2,1152]{2,1,0:T(2,128)(2,1)S(1)}, u32[]{:S(2)}, u32[]{:S(2)}) %all-to-all-start) | async-done | bytes 294944 | tf_op jit(solution)/shard_map/all_to_all | solution.py:327
  39.7 0.7 shard_map.131.refs_0_.refs_1_
  40.4 3.5 %collective-permute-start.1 = (bf16[16,2176]{1,0:T(8,128)(2,1)S(1)}, bf16[16,2176]{1,0:T(8,128)(2,1)S(1)}, u32[]{:S(2)}, u32[]{:S(2)}) collective-permute-start(bf16[16,2176]{1,0:T(8,128)(2,1)S(1)} %shard_map.131.refs_0_.refs_1_), channel_id=1, source_target_pairs={{0,1},{1,0},{2,3},{3,2},{4,5},{5,4},{6,7},{7,6},{8,9},{9,8},{10,11... | collective-permute-start | bytes 208904 | tf_op jit(solution)/shard_map/ppermute | solution.py:352
  43.9 0.9 collective-permute-done.1.refs_2_
  44.8 0.0 copy-start
  44.8 1.2 %copy-done = bf16[2048,256]{1,0:T(8,128)(2,1)S(1)} copy-done((bf16[2048,256]{1,0:T(8,128)(2,1)S(1)}, bf16[2048,256]{1,0:T(8,128)(2,1)}, u32[]{:S(2)}) %copy-start) | copy-done | bytes 1048600
  46.0 1.6 %shard_map.133 = bf16[64,8,1152]{2,1,0:T(8,128)(2,1)S(1)} custom-call(bf16[64,8,1152]{2,1,0:T(8,128)(2,1)S(1)} %get-tuple-element.17.refs_0_, bf16[16,2176]{1,0:T(8,128)(2,1)S(1)} %shard_map.131.refs_0_.refs_1_, bf16[16,2176]{1,0:T(8,128)(2,1)S(1)} %collective-permute-done.1.refs_2_, bf16[32,2048]{1,0:T(8,128)(2,1)S(1)} %get-tuple-element.18.refs_3_, ...), custom_call_target="tpu_custom_call" | custom-call | tf_op jit(solution)/shard_map/pallas_call | solution.py:287
  47.6 36.1 %all_to_all.15.refs_0_ = bf16[64,8,1152]{2,1,0:T(8,128)(2,1)S(1)} all-to-all(bf16[64,8,1152]{2,1,0:T(8,128)(2,1)S(1)} %shard_map.133), channel_id=1, replica_groups=mesh['dp'=64,'replica'=16] {'dp'}, dimensions={0} | all-to-all | bytes 2359296 | tf_op jit(solution)/shard_map/all_to_all | solution.py:359
  83.6 0.9 shard_map.134
  84.6 15.3 %all-to-all-start.2 = ((bf16[16,8,1152]{2,1,0:T(8,128)(2,1)}), bf16[16,8,1152]{2,1,0:T(8,128)(2,1)S(1)}, u32[]{:S(2)}, u32[]{:S(2)}) async-start(bf16[16,8,1152]{2,1,0:T(8,128)(2,1)} %shard_map.134), calls=%async_computation.2 | async-start | bytes 589824 | tf_op jit(solution)/shard_map/all_to_all | solution.py:367
  99.9 0.0 copy-done.1
  99.9 3.6 %shard_map.132 = f32[16,2048]{1,0:T(8,128)} custom-call(bf16[16,2176]{1,0:T(8,128)(2,1)S(1)} %shard_map.131.refs_0_.refs_1_, bf16[16,2048]{1,0:T(8,128)(2,1)} %bitcast.14, bf16[2048,256]{1,0:T(8,128)(2,1)} %refs_2_.7, bf16[256,2048]{1,0:T(8,128)(2,1)} %refs_3_.1, bf16[256,2048]{1,0:T(8,128)(2,1)S(1)} %copy-done.1, f32[1,2048]{1,0:T(1,128)} %bitcast.17, ...), custom_call_target="tpu_custom_call" | custom-call | tf_op jit(solution)/shard_map/pallas_call | solution.py:287
  103.5 8.7 %all-to-all-done.2.refs_0_ = bf16[16,8,1152]{2,1,0:T(8,128)(2,1)S(1)} async-done(((bf16[16,8,1152]{2,1,0:T(8,128)(2,1)}), bf16[16,8,1152]{2,1,0:T(8,128)(2,1)S(1)}, u32[]{:S(2)}, u32[]{:S(2)}) %all-to-all-start.2) | async-done | bytes 294944 | tf_op jit(solution)/shard_map/all_to_all | solution.py:367
  112.2 0.9 shard_map.135
  (1 shorter events, 0.0 us)
Async XLA Ops:
  3.2 22.1 %copy-start.2 = (bf16[2048]{0:T(1024)(128)(2,1)S(1)}, bf16[2048]{0:T(1024)(128)(2,1)}, u32[]{:S(2)}) copy-start(bf16[2048]{0:T(1024)(128)(2,1)} %param.17) | copy-start | bytes 12292
  4.6 21.4 %collective-permute-start = (bf16[288,2048]{1,0:T(8,128)(2,1)S(1)}, bf16[288,2048]{1,0:T(8,128)(2,1)S(1)}, u32[]{:S(2)}, u32[]{:S(2)}) collective-permute-start(bf16[288,2048]{1,0:T(8,128)(2,1)S(1)} %shard_map.129), channel_id=1, source_target_pairs={{0,1},{1,0},{2,3},{3,2},{4,5},{5,4},{6,7},{7,6},{8,9},{9,8},{10,11... | collective-permute-start | bytes 3538952 | tf_op jit(solution)/shard_map/ppermute | solution.py:328
  20.7 19.0 %all-to-all-start = ((bf16[64,2,1152]{2,1,0:T(2,128)(2,1)}), bf16[64,2,1152]{2,1,0:T(2,128)(2,1)S(1)}, u32[]{:S(2)}, u32[]{:S(2)}) async-start(bf16[64,2,1152]{2,1,0:T(2,128)(2,1)} %shard_map.128.refs_0_), calls=%async_computation | async-start | bytes 589824 | tf_op jit(solution)/shard_map/all_to_all | solution.py:327
  40.4 4.4 %collective-permute-start.1 = (bf16[16,2176]{1,0:T(8,128)(2,1)S(1)}, bf16[16,2176]{1,0:T(8,128)(2,1)S(1)}, u32[]{:S(2)}, u32[]{:S(2)}) collective-permute-start(bf16[16,2176]{1,0:T(8,128)(2,1)S(1)} %shard_map.131.refs_0_.refs_1_), channel_id=1, source_target_pairs={{0,1},{1,0},{2,3},{3,2},{4,5},{5,4},{6,7},{7,6},{8,9},{9,8},{10,11... | collective-permute-start | bytes 208904 | tf_op jit(solution)/shard_map/ppermute | solution.py:352
  44.8 1.2 %copy-start = (bf16[2048,256]{1,0:T(8,128)(2,1)S(1)}, bf16[2048,256]{1,0:T(8,128)(2,1)}, u32[]{:S(2)}) copy-start(bf16[2048,256]{1,0:T(8,128)(2,1)} %get-tuple-element.19.refs_4_) | copy-start | bytes 3145732
  83.6 16.3 %copy-start.1 = (bf16[256,2048]{1,0:T(8,128)(2,1)S(1)}, bf16[256,2048]{1,0:T(8,128)(2,1)}, u32[]{:S(2)}) copy-start(bf16[256,2048]{1,0:T(8,128)(2,1)} %get-tuple-element.16.refs_4_) | copy-start | bytes 3145732
  84.6 27.7 %all-to-all-start.2 = ((bf16[16,8,1152]{2,1,0:T(8,128)(2,1)}), bf16[16,8,1152]{2,1,0:T(8,128)(2,1)S(1)}, u32[]{:S(2)}, u32[]{:S(2)}) async-start(bf16[16,8,1152]{2,1,0:T(8,128)(2,1)} %shard_map.134), calls=%async_computation.2 | async-start | bytes 589824 | tf_op jit(solution)/shard_map/all_to_all | solution.py:367

commit v3 on v2

--- a/solution.py
+++ b/solution.py
@@ -66,19 +66,18 @@
     slots_ref[...] = wide[...].astype(BF16)
 
 
-def swap_kernel(wait, slots_any, feat_ref, score_ref, user_ref, swap_ref):
-    wait(1, 2, 3)
-    rows, width = feat_ref.shape
+def swap_kernel(wait, slots_any, score_ref, user_ref, swap_ref):
+    wait(1, 2)
+    rows, width = score_ref.shape[1], user_ref.shape[1]
     score_high, score_low = split_in_two(score_ref[...])
     line = iota((16, rows), 0)
-    swap_ref[:rows, :] = feat_ref[...]
-    swap_ref[rows : rows + 16, :] = jnp.zeros((16, width), BF16)
-    swap_ref[rows : rows + 16, :rows] = jnp.where(
+    swap_ref[:16, :] = jnp.zeros((16, width), BF16)
+    swap_ref[:16, :rows] = jnp.where(
         line == 0,
         score_high.astype(F32),
         jnp.where(line == 1, score_low.astype(F32), 0.0),
     ).astype(BF16)
-    swap_ref[rows + 16 :, :] = user_ref[...]
+    swap_ref[16:, :] = user_ref[...]
 
 
 def lay_out(grad, out_ref, base, base_sums):
@@ -93,10 +92,10 @@
 
 
 def main_kernel(
-    wait, at_ref, feat_ref, score_ref, user_ref, swap_ref, u_ref, v_ref, bias_ref, w_ref,
+    wait, at_ref, feat_ref, score_ref, user_ref, other_ref, swap_ref, u_ref, v_ref, bias_ref, w_ref,
     base_ref, half_ref, vw_ref, users_ref, user_half_ref, tail_ref, both,
 ):
-    wait(*range(1, 9))
+    wait(*range(1, 10))
     dp, core = at_ref[0], at_ref[1]
     rows, width = feat_ref.shape
     rank = v_ref.shape[0]
@@ -111,8 +110,8 @@
         half_ref[...] = jnp.transpose(vw)
 
     both[:rows, :] = feat_ref[...]
-    both[rows:, :] = swap_ref[:rows, :]
-    marks = swap_ref[rows : rows + 16, :rows].astype(F32)
+    both[rows:, :] = other_ref[...]
+    marks = swap_ref[:16, :rows].astype(F32)
     scores = jnp.concatenate(
         [as_columns(score_ref[...]), as_columns(marks[0:1, :] + marks[1:2, :])], axis=0
     )
@@ -125,7 +124,7 @@
     scaled = jnp.concatenate(scaled, axis=1).astype(BF16)
     lay_out(dot(both[...], scaled, TN), base_ref, lambda q: 0.0, 0.0)
     users_ref[:16, :] = user_ref[...]
-    users_ref[16:, :] = swap_ref[rows + 16 :, :]
+    users_ref[16:, :] = swap_ref[16:, :]
     user_half_ref[...] = dot(users_ref[...], half_ref[...])
     here = iota((part, width), 1) == dp * part + iota((part, width), 0)
     tail_ref[:, :rank] = dot(here.astype(BF16), v_ref[...], NT)
@@ -320,11 +319,12 @@
     )
     swap = call(
         swap_kernel,
-        shape((rows + 16 + req, width), BF16),
-        slots, feat, grad_score, user,
-        places="ahhh",
+        shape((16 + req, width), BF16),
+        slots, grad_score, user,
+        places="ahh",
     )
     arrived = lax.all_to_all(slots, "dp", split_axis=0, concat_axis=0, tiled=True)
+    swapped_feat = lax.ppermute(feat, "replica", pairs)
     swapped = lax.ppermute(swap, "replica", pairs)
     base, half, vw, users, user_half, tail = call(
         main_kernel,
@@ -336,9 +336,9 @@
             shape((2 * req, rank), F32),
             shape((part, rank + LANES), F32),
         ),
-        at, feat, grad_score, user, swapped, u_weight, v_weight, bias, w_out,
+        at, feat, grad_score, user, swapped_feat, swapped, u_weight, v_weight, bias, w_out,
         scratch=[pltpu.VMEM((2 * rows, width), BF16)],
-        places="shhhnhhhh",
+        places="shhhnnhhhh",
         out_places="nhhnnn",
         cost=pl.CostEstimate(flops=1, bytes_accessed=1, transcendentals=0),
     )
@@ -354,7 +354,7 @@
         merge_kernel,
         shape((peers, 8, 4 * rank + LANES), BF16),
         base, own, other, users, half, user_half,
-        places="n--nnn",
+        places="n--nhn",
     )
     received = lax.all_to_all(parts, "dp", split_axis=0, concat_axis=0, tiled=True)
     user_grad = call(

time: 114 us -> 116 us (1.018)
  blocking collectives: 36.1 us -> 39.5 us
  waiting for transfers between devices: 15.2 us -> 12.4 us
  starting transfers between devices: 39.5 us -> 41.5 us
  local copies, waits for them, and re-layouts: 1.84 us -> 0.61 us
    ppermute x0 -> x1, starting transfers between devices: none -> 16.1 us  [per_device(): swapped_feat = lax.ppermute(feat, 'replica', pairs)]
    ppermute x1, starting transfers between devices: 16.1 us -> 1.92 us  [per_device(): swapped = lax.ppermute(swap, 'replica', pairs)]
    all_to_all x1, blocking collectives: 36.1 us -> 39.5 us  [per_device(): lax.all_to_all(parts, 'dp', split_axis=0, concat_axis=0, tiled=True)]
    all_to_all x1, waiting for transfers between devices: 5.6 us -> 2.15 us  [per_device(): lax.all_to_all(slots, 'dp', split_axis=0, concat_axis=0, tiled=True)]
    unnamed x6 -> x4, local copies, waits for them, and re-layouts: 1.23 us -> 0.01 us
  transfers between devices with their start and end apart: 4 -> 5, of which waited for: 3 -> 4; matrix products, arithmetic and copies ran while one was open for 1% -> 1% of each run, Pallas kernels for 10% -> 13%
where the time goes in v3:
time: 116 us; the launch traced here: 115 us
  starting transfers between devices  41.5 us (36%)
  blocking collectives  39.5 us (34%)
  Pallas kernels  20.4 us (18%)
  waiting for transfers between devices  12.4 us (11%)
    all_to_all x1, blocking collectives, per_device(): lax.all_to_all(parts, 'dp', split_axis=0, concat_axis=0, tiled=True)  39.5 us
    pallas_call x8, Pallas kernels, call(): pl.pallas_call(body, out_shape=pinned if several else pinned[0], in_specs...  20.4 us
    ppermute x1, starting transfers between devices, per_device(): swapped_feat = lax.ppermute(feat, 'replica', pairs)  16.1 us
    all_to_all x1, starting transfers between devices, per_device(): lax.all_to_all(copies, 'replica', split_axis=0, concat_axis=0, tiled=True)  15.4 us
    all_to_all x1, waiting for transfers between devices, per_device(): lax.all_to_all(copies, 'replica', split_axis=0, concat_axis=0, tiled=True)  8.72 us
    all_to_all x1, starting transfers between devices, per_device(): lax.all_to_all(slots, 'dp', split_axis=0, concat_axis=0, tiled=True)  4.63 us
    ppermute x1, starting transfers between devices, per_device(): other = lax.ppermute(own, 'replica', pairs)  3.48 us
  transfers between devices with their start and end apart: 5, of which 4 were waited for; matrix products, arithmetic and copies ran while one was open for 1% of the time, Pallas kernels for 13%

profile of v3, /device:TPU:1, one launch (start us, length us, event | category | flops | bytes accessed | tf_op | source)
XLA Modules:
  0.0 115.2 jit_solution(11770692676947795510)
XLA Ops:
  0.6 16.1 %collective-permute-start = (bf16[256,2048]{1,0:T(8,128)(2,1)}, bf16[256,2048]{1,0:T(8,128)(2,1)S(1)}, u32[]{:S(2)}, u32[]{:S(2)}) collective-permute-start(bf16[256,2048]{1,0:T(8,128)(2,1)} %bitcast.9), channel_id=1, source_target_pairs={{0,1},{1,0},{2,3},{3,2},{4,5},{5,4},{6,7},{7,6},{8,9},{9,8},{10,11... | collective-permute-start | bytes 3145736 | tf_op jit(solution)/shard_map/ppermute | solution.py:327
  16.7 0.0 copy-start.1
  16.7 2.6 %shard_map.128.refs_0_ = bf16[64,2,1152]{2,1,0:T(2,128)(2,1)} custom-call(s32[1,16]{1,0:T(1,128)} %refs_0_.1, s32[1,256]{1,0:T(1,128)} %bitcast.18, f32[1,256]{1,0:T(1,128)} %refs_2_.4, bf16[256,2048]{1,0:T(8,128)(2,1)} %bitcast.10), custom_call_target="tpu_custom_call" | custom-call | tf_op jit(solution)/shard_map/pallas_call | solution.py:286
  19.3 4.6 %all-to-all-start = ((bf16[64,2,1152]{2,1,0:T(2,128)(2,1)}), bf16[64,2,1152]{2,1,0:T(2,128)(2,1)S(1)}, u32[]{:S(2)}, u32[]{:S(2)}) async-start(bf16[64,2,1152]{2,1,0:T(2,128)(2,1)} %shard_map.128.refs_0_), calls=%async_computation | async-start | bytes 589824 | tf_op jit(solution)/shard_map/all_to_all | solution.py:326
  24.0 0.9 shard_map.129
  24.8 1.9 %collective-permute-start.1 = (bf16[32,2048]{1,0:T(8,128)(2,1)S(1)}, bf16[32,2048]{1,0:T(8,128)(2,1)S(1)}, u32[]{:S(2)}, u32[]{:S(2)}) collective-permute-start(bf16[32,2048]{1,0:T(8,128)(2,1)S(1)} %shard_map.129), channel_id=1, source_target_pairs={{0,1},{1,0},{2,3},{3,2},{4,5},{5,4},{6,7},{7,6},{8,9},{9,8},{10,11... | collective-permute-start | bytes 393224 | tf_op jit(solution)/shard_map/ppermute | solution.py:328
  26.8 0.0 copy-done.1
  26.8 0.6 broadcast_in_dim.10.refs_9_.refs_6_
  27.4 0.1 pad_add_fusion.refs_0_
  27.5 0.6 collective-permute-done.1.refs_5_
  28.1 0.0 collective-permute-done.refs_4_
  28.1 8.1 %shard_map.130 = (bf16[64,8,1152]{2,1,0:T(8,128)(2,1)S(1)}, bf16[2048,256]{1,0:T(8,128)(2,1)}, bf16[256,2048]{1,0:T(8,128)(2,1)}, bf16[32,2048]{1,0:T(8,128)(2,1...) custom-call(s32[2]{0:T(128)S(1)} %pad_add_fusion.refs_0_, bf16[256,2048]{1,0:T(8,128)(2,1)} %bitcast.11, ...), custom_call_target="tpu_custom_call" | custom-call | flops 1 | bytes 1 | tf_op jit(solution)/shard_map/pallas_call | solution.py:286
  36.2 2.1 %all-to-all-done.refs_0_ = bf16[64,2,1152]{2,1,0:T(2,128)(2,1)S(1)} async-done(((bf16[64,2,1152]{2,1,0:T(2,128)(2,1)}), bf16[64,2,1152]{2,1,0:T(2,128)(2,1)S(1)}, u32[]{:S(2)}, u32[]{:S(2)}) %all-to-all-start) | async-done | bytes 294944 | tf_op jit(solution)/shard_map/all_to_all | solution.py:326
  38.3 0.7 shard_map.131.refs_0_.refs_1_
  39.1 3.5 %collective-permute-start.2 = (bf16[16,2176]{1,0:T(8,128)(2,1)S(1)}, bf16[16,2176]{1,0:T(8,128)(2,1)S(1)}, u32[]{:S(2)}, u32[]{:S(2)}) collective-permute-start(bf16[16,2176]{1,0:T(8,128)(2,1)S(1)} %shard_map.131.refs_0_.refs_1_), channel_id=1, source_target_pairs={{0,1},{1,0},{2,3},{3,2},{4,5},{5,4},{6,7},{7,6},{8,9},{9,8},{10,11... | collective-permute-start | bytes 208904 | tf_op jit(solution)/shard_map/ppermute | solution.py:352
  42.6 0.9 collective-permute-done.2.refs_2_
  43.4 2.7 %shard_map.133 = bf16[64,8,1152]{2,1,0:T(8,128)(2,1)S(1)} custom-call(bf16[64,8,1152]{2,1,0:T(8,128)(2,1)S(1)} %get-tuple-element.17.refs_0_, bf16[16,2176]{1,0:T(8,128)(2,1)S(1)} %shard_map.131.refs_0_.refs_1_, bf16[16,2176]{1,0:T(8,128)(2,1)S(1)} %collective-permute-done.2.refs_2_, bf16[32,2048]{1,0:T(8,128)(2,1)S(1)} %get-tuple-element.18.refs_3_, ...), custom_call_target="tpu_custom_call" | custom-call | tf_op jit(solution)/shard_map/pallas_call | solution.py:286
  46.1 39.5 %all_to_all.15.refs_0_ = bf16[64,8,1152]{2,1,0:T(8,128)(2,1)S(1)} all-to-all(bf16[64,8,1152]{2,1,0:T(8,128)(2,1)S(1)} %shard_map.133), channel_id=1, replica_groups=mesh['dp'=64,'replica'=16] {'dp'}, dimensions={0} | all-to-all | bytes 2359296 | tf_op jit(solution)/shard_map/all_to_all | solution.py:359
  85.6 0.9 shard_map.134
  86.6 15.4 %all-to-all-start.2 = ((bf16[16,8,1152]{2,1,0:T(8,128)(2,1)}), bf16[16,8,1152]{2,1,0:T(8,128)(2,1)S(1)}, u32[]{:S(2)}, u32[]{:S(2)}) async-start(bf16[16,8,1152]{2,1,0:T(8,128)(2,1)} %shard_map.134), calls=%async_computation.2 | async-start | bytes 589824 | tf_op jit(solution)/shard_map/all_to_all | solution.py:367
  101.9 0.0 copy-done
  102.0 3.6 %shard_map.132 = f32[16,2048]{1,0:T(8,128)} custom-call(bf16[16,2176]{1,0:T(8,128)(2,1)S(1)} %shard_map.131.refs_0_.refs_1_, bf16[16,2048]{1,0:T(8,128)(2,1)} %bitcast.14, bf16[2048,256]{1,0:T(8,128)(2,1)} %refs_2_.5, bf16[256,2048]{1,0:T(8,128)(2,1)} %refs_3_.1, bf16[256,2048]{1,0:T(8,128)(2,1)S(1)} %copy-done, f32[1,2048]{1,0:T(1,128)} %bitcast.17, ...), custom_call_target="tpu_custom_call" | custom-call | tf_op jit(solution)/shard_map/pallas_call | solution.py:286
  105.6 8.7 %all-to-all-done.2.refs_0_ = bf16[16,8,1152]{2,1,0:T(8,128)(2,1)S(1)} async-done(((bf16[16,8,1152]{2,1,0:T(8,128)(2,1)}), bf16[16,8,1152]{2,1,0:T(8,128)(2,1)S(1)}, u32[]{:S(2)}, u32[]{:S(2)}) %all-to-all-start.2) | async-done | bytes 294944 | tf_op jit(solution)/shard_map/all_to_all | solution.py:367
  114.3 0.9 shard_map.135
  (1 shorter events, 0.0 us)
Async XLA Ops:
  0.6 27.5 %collective-permute-start = (bf16[256,2048]{1,0:T(8,128)(2,1)}, bf16[256,2048]{1,0:T(8,128)(2,1)S(1)}, u32[]{:S(2)}, u32[]{:S(2)}) collective-permute-start(bf16[256,2048]{1,0:T(8,128)(2,1)} %bitcast.9), channel_id=1, source_target_pairs={{0,1},{1,0},{2,3},{3,2},{4,5},{5,4},{6,7},{7,6},{8,9},{9,8},{10,11... | collective-permute-start | bytes 3145736 | tf_op jit(solution)/shard_map/ppermute | solution.py:327
  16.7 10.1 %copy-start.1 = (bf16[2048]{0:T(1024)(128)(2,1)S(1)}, bf16[2048]{0:T(1024)(128)(2,1)}, u32[]{:S(2)}) copy-start(bf16[2048]{0:T(1024)(128)(2,1)} %param.17) | copy-start | bytes 12292
  19.3 19.0 %all-to-all-start = ((bf16[64,2,1152]{2,1,0:T(2,128)(2,1)}), bf16[64,2,1152]{2,1,0:T(2,128)(2,1)S(1)}, u32[]{:S(2)}, u32[]{:S(2)}) async-start(bf16[64,2,1152]{2,1,0:T(2,128)(2,1)} %shard_map.128.refs_0_), calls=%async_computation | async-start | bytes 589824 | tf_op jit(solution)/shard_map/all_to_all | solution.py:326
  24.8 3.2 %collective-permute-start.1 = (bf16[32,2048]{1,0:T(8,128)(2,1)S(1)}, bf16[32,2048]{1,0:T(8,128)(2,1)S(1)}, u32[]{:S(2)}, u32[]{:S(2)}) collective-permute-start(bf16[32,2048]{1,0:T(8,128)(2,1)S(1)} %shard_map.129), channel_id=1, source_target_pairs={{0,1},{1,0},{2,3},{3,2},{4,5},{5,4},{6,7},{7,6},{8,9},{9,8},{10,11... | collective-permute-start | bytes 393224 | tf_op jit(solution)/shard_map/ppermute | solution.py:328
  39.1 4.4 %collective-permute-start.2 = (bf16[16,2176]{1,0:T(8,128)(2,1)S(1)}, bf16[16,2176]{1,0:T(8,128)(2,1)S(1)}, u32[]{:S(2)}, u32[]{:S(2)}) collective-permute-start(bf16[16,2176]{1,0:T(8,128)(2,1)S(1)} %shard_map.131.refs_0_.refs_1_), channel_id=1, source_target_pairs={{0,1},{1,0},{2,3},{3,2},{4,5},{5,4},{6,7},{7,6},{8,9},{9,8},{10,11... | collective-permute-start | bytes 208904 | tf_op jit(solution)/shard_map/ppermute | solution.py:352
  85.6 16.3 %copy-start = (bf16[256,2048]{1,0:T(8,128)(2,1)S(1)}, bf16[256,2048]{1,0:T(8,128)(2,1)}, u32[]{:S(2)}) copy-start(bf16[256,2048]{1,0:T(8,128)(2,1)} %get-tuple-element.16.refs_4_) | copy-start | bytes 3145732
  86.6 27.8 %all-to-all-start.2 = ((bf16[16,8,1152]{2,1,0:T(8,128)(2,1)}), bf16[16,8,1152]{2,1,0:T(8,128)(2,1)S(1)}, u32[]{:S(2)}, u32[]{:S(2)}) async-start(bf16[16,8,1152]{2,1,0:T(8,128)(2,1)} %shard_map.134), calls=%async_computation.2 | async-start | bytes 589824 | tf_op jit(solution)/shard_map/all_to_all | solution.py:367

commit v4 on v3

--- a/solution.py
+++ b/solution.py
@@ -33,7 +33,9 @@
     return jnp.transpose(jnp.broadcast_to(row, (LANES, row.shape[1])))
 
 
-def request_kernel(wait, wanted_ref, seg_ref, score_ref, feat_ref, slots_ref, wide):
+def request_kernel(
+    wait, wanted_ref, seg_ref, score_ref, user_ref, feat_ref, slots_ref, pack_ref, wide
+):
     peers, req = slots_ref.shape[0], wanted_ref.shape[1]
     rows, width = feat_ref.shape
     piece = width // PIECES
@@ -60,24 +62,20 @@
     wide[:, 0, piece:] = extra
     for p in range(1, PIECES):
         wide[:, p, piece:] = jnp.zeros((peers, LANES), F32)
-    wait(3)
-    for p in range(PIECES):
-        wide[:, p, :piece] = dot(weights, feat_ref[:, p * piece : (p + 1) * piece])
-    slots_ref[...] = wide[...].astype(BF16)
-
-
-def swap_kernel(wait, slots_any, score_ref, user_ref, swap_ref):
-    wait(1, 2)
-    rows, width = score_ref.shape[1], user_ref.shape[1]
-    score_high, score_low = split_in_two(score_ref[...])
+    score_high, score_low = split_in_two(scores)
     line = iota((16, rows), 0)
-    swap_ref[:16, :] = jnp.zeros((16, width), BF16)
-    swap_ref[:16, :rows] = jnp.where(
+    pack_ref[:16, :] = jnp.zeros((16, width), BF16)
+    pack_ref[:16, :rows] = jnp.where(
         line == 0,
         score_high.astype(F32),
         jnp.where(line == 1, score_low.astype(F32), 0.0),
     ).astype(BF16)
-    swap_ref[16:, :] = user_ref[...]
+    wait(3)
+    pack_ref[16:, :] = user_ref[...]
+    wait(4)
+    for p in range(PIECES):
+        wide[:, p, :piece] = dot(weights, feat_ref[:, p * piece : (p + 1) * piece])
+    slots_ref[...] = wide[...].astype(BF16)
 
 
 def lay_out(grad, out_ref, base, base_sums):
@@ -91,50 +89,61 @@
     out_ref[:, :, 4 * rank :] = (sums + base_sums).astype(BF16)
 
 
+def row_of(ref):
+    rows = ref[...].astype(F32)
+    return jnp.concatenate([rows[k : k + 1, :] for k in range(rows.shape[0])], axis=1)
+
+
+def my_core():
+    return lax.rem(lax.axis_index("replica"), 2)
+
+
 def main_kernel(
-    wait, at_ref, feat_ref, score_ref, user_ref, other_ref, swap_ref, u_ref, v_ref, bias_ref, w_ref,
-    base_ref, half_ref, vw_ref, users_ref, user_half_ref, tail_ref, both,
+    wait, feat_any, other_any, score_ref, user_ref, pack_ref, u_ref, v_ref, w_ref,
+    base_ref, user_half_ref, next_ref, both, low_ref, sems,
 ):
-    wait(*range(1, 10))
-    dp, core = at_ref[0], at_ref[1]
-    rows, width = feat_ref.shape
+    rows, width = feat_any.shape
     rank = v_ref.shape[0]
-    part = tail_ref.shape[0]
-    w_row = w_ref[...].astype(F32)
-    vw = (v_ref[...].astype(F32) * w_row).astype(BF16)
-    vw_ref[...] = vw
-    half_ref[...] = u_ref[...]
-
-    @pl.when(core == 1)
-    def _():
-        half_ref[...] = jnp.transpose(vw)
-
-    both[:rows, :] = feat_ref[...]
-    both[rows:, :] = other_ref[...]
-    marks = swap_ref[:16, :rows].astype(F32)
+    req = user_ref.shape[0]
+    copies = [
+        pltpu.make_async_copy(feat_any, both.at[:rows], sems.at[0]),
+        pltpu.make_async_copy(other_any, both.at[rows:], sems.at[1]),
+    ]
+    for copy in copies:
+        copy.start()
+    wait(2, 3, 4)
+    next_ref[...] = pack_ref[16:, :]
+    marks = pack_ref[:16, :rows].astype(F32)
     scores = jnp.concatenate(
         [as_columns(score_ref[...]), as_columns(marks[0:1, :] + marks[1:2, :])], axis=0
     )
-    low = dot(both[...], half_ref[...])
-    scaled = [
-        low[:, k : k + LANES] * scores for k in range(0, rank, LANES)
-    ]
+    wait(5, 6, 7)
+    for copy in copies:
+        copy.wait()
+    core = my_core()
+
+    @pl.when(core == 0)
+    def _():
+        u = u_ref[...]
+        low_ref[...] = dot(both[...], u)
+        user_half_ref[:req, :] = dot(user_ref[...], u)
+        user_half_ref[req:, :] = dot(pack_ref[16:, :], u)
+
+    @pl.when(core == 1)
+    def _():
+        vw = (v_ref[...].astype(F32) * row_of(w_ref)).astype(BF16)
+        low_ref[...] = dot(both[...], vw, NT)
+        user_half_ref[:req, :] = dot(user_ref[...], vw, NT)
+        user_half_ref[req:, :] = dot(pack_ref[16:, :], vw, NT)
+
+    scaled = [low_ref[:, k : k + LANES] * scores for k in range(0, rank, LANES)]
     lane = iota((2 * rows, LANES), 1)
     scaled.append(jnp.where(lane < 4, scores, 0.0))
     scaled = jnp.concatenate(scaled, axis=1).astype(BF16)
     lay_out(dot(both[...], scaled, TN), base_ref, lambda q: 0.0, 0.0)
-    users_ref[:16, :] = user_ref[...]
-    users_ref[16:, :] = swap_ref[16:, :]
-    user_half_ref[...] = dot(users_ref[...], half_ref[...])
-    here = iota((part, width), 1) == dp * part + iota((part, width), 0)
-    tail_ref[:, :rank] = dot(here.astype(BF16), v_ref[...], NT)
-    lane = iota((part, LANES), 1)
-    w_col = jnp.sum(jnp.where(here, w_row, 0.0), axis=1, keepdims=True)
-    b_col = jnp.sum(jnp.where(here, bias_ref[...], 0.0), axis=1, keepdims=True)
-    tail_ref[:, rank:] = jnp.where(lane == 0, w_col, jnp.where(lane == 1, b_col, 0.0))
-
-
-def pick_kernel(wait, slots_ref, tail_any, out_ref, wide):
+
+
+def pick_kernel(wait, slots_ref, after_any, out_ref, wide):
     req = out_ref.shape[0]
     piece = slots_ref.shape[2] - LANES
     wide[...] = slots_ref[...].astype(F32)
@@ -152,29 +161,51 @@
     return pack[:, at : at + 1].astype(F32) + pack[:, at + 1 : at + 2].astype(F32)
 
 
-def merge_kernel(wait, base_ref, own_ref, other_ref, users_ref, half_ref, user_half_ref, out_ref):
-    req, width = users_ref.shape[0] // 2, users_ref.shape[1]
-    rank = half_ref.shape[1]
-    wait(3, 4, 5)
-    half = half_ref[...]
-    lines, factors = [], []
-    lane = iota((req, LANES), 1)
-    for at, pack_ref, user in (
-        (0, own_ref, users_ref[:req, :]),
-        (req, other_ref, users_ref[req:, :]),
-    ):
-        pack = pack_ref[...]
-        sums = pack[:, :width]
-        total = total_of(pack, width, req)
-        user_half = user_half_ref[at : at + req, :]
-        both = dot(sums, half) + total * user_half
-        lines += [sums, user]
-        factors += [
-            jnp.concatenate([user_half, jnp.zeros((req, LANES), F32)], axis=1),
+def merge_kernel(
+    wait, base_ref, own_ref, other_ref, user_ref, next_ref, w_ref, user_half_ref, u_any, v_any,
+    out_ref, u_ref, v_ref, both_ref, sem,
+):
+    req, width = user_ref.shape
+    rank = user_half_ref.shape[1]
+    core = my_core()
+    get_u = pltpu.make_async_copy(u_any, u_ref, sem)
+    get_v = pltpu.make_async_copy(v_any, v_ref, sem)
+
+    @pl.when(core == 0)
+    def _():
+        get_u.start()
+
+    @pl.when(core == 1)
+    def _():
+        get_v.start()
+
+    own, other = own_ref[...], other_ref[...]
+    sums = jnp.concatenate([own[:, :width], other[:, :width]], axis=0)
+    total = jnp.concatenate([total_of(own, width, req), total_of(other, width, req)], axis=0)
+    wait(3, 4, 5, 6)
+
+    @pl.when(core == 0)
+    def _():
+        get_u.wait()
+        both_ref[...] = dot(sums, u_ref[...])
+
+    @pl.when(core == 1)
+    def _():
+        get_v.wait()
+        weighted = (sums.astype(F32) * row_of(w_ref)).astype(BF16)
+        both_ref[...] = dot(weighted, v_ref[...], NT)
+
+    user_half = user_half_ref[...]
+    both = both_ref[...] + total * user_half
+    lane = iota((2 * req, LANES), 1)
+    lines = jnp.concatenate([sums, user_ref[...], next_ref[...]], axis=0)
+    factors = jnp.concatenate(
+        [
+            jnp.concatenate([user_half, jnp.zeros((2 * req, LANES), F32)], axis=1),
             jnp.concatenate([both, jnp.where(lane < 4, total, 0.0)], axis=1),
-        ]
-    lines = jnp.concatenate(lines, axis=0)
-    factors = jnp.concatenate(factors, axis=0).astype(BF16)
+        ],
+        axis=0,
+    ).astype(BF16)
     wait(0)
     lay_out(
         dot(lines, factors, TN),
@@ -184,21 +215,30 @@
     )
 
 
-def user_grad_kernel(wait, pack_ref, user_ref, u_ref, v_ref, vw_ref, bias_ref, w_ref, out_ref):
-    wait(*range(1, 7))
+def user_grad_kernel(wait, pack_ref, user_ref, u_ref, v_ref, bias_ref, w_ref, out_ref, tail_ref):
+    wait(*range(1, 6))
     req, width = user_ref.shape
+    part, rank = tail_ref.shape[0], v_ref.shape[0]
     pack = pack_ref[...]
     sums = pack[:, :width]
     total = total_of(pack, width, req)
     user = user_ref[...]
-    u, vw = u_ref[...], vw_ref[...]
+    u, v = u_ref[...], v_ref[...]
+    w_row = row_of(w_ref)
     low = dot(sums, u) + total * dot(user, u)
-    grad_low = dot(sums, vw, NT) + total * dot(user, vw, NT)
-    w_row = w_ref[...].astype(F32)
+    both = (jnp.concatenate([sums, user], axis=0).astype(F32) * w_row).astype(BF16)
+    both = dot(both, v, NT)
+    grad_low = both[:req, :] + total * both[req:, :]
     out_ref[...] = (
-        w_row * (dot(low.astype(BF16), v_ref[...]) + total * (bias_ref[...] + 1.0))
+        w_row * (dot(low.astype(BF16), v) + total * (bias_ref[...] + 1.0))
         + dot(grad_low.astype(BF16), u, NT)
     )
+    here = iota((part, width), 1) == lax.axis_index("dp") * part + iota((part, width), 0)
+    tail_ref[:, :rank] = dot(here.astype(BF16), v, NT)
+    lane = iota((part, LANES), 1)
+    w_col = jnp.sum(jnp.where(here, w_row, 0.0), axis=1, keepdims=True)
+    b_col = jnp.sum(jnp.where(here, bias_ref[...], 0.0), axis=1, keepdims=True)
+    tail_ref[:, rank:] = jnp.where(lane == 0, w_col, jnp.where(lane == 1, b_col, 0.0))
 
 
 def sum_kernel(wait, in_ref, out_ref):
@@ -229,7 +269,7 @@
 
 
 def call(kernel, out, *args, places="", out_places="", scratch=(), room=24, cost=None):
-    spaces = {"s": pltpu.SMEM, "a": pl.ANY, "h": pltpu.HBM, "n": pl.ANY, "-": pltpu.VMEM}
+    spaces = {"s": pltpu.SMEM, "a": pl.ANY, "h": pltpu.HBM, "n": pl.ANY, "p": pltpu.HBM, "-": pltpu.VMEM}
     several = isinstance(out, tuple)
     outs = out if several else (out,)
     places = places + "-" * (len(args) - len(places))
@@ -237,7 +277,7 @@
     staged = [k for k, place in enumerate(places) if place in "hn"]
     late = [k for k, place in enumerate(out_places) if place in "hn"]
     args = [
-        pltpu.with_memory_space_constraint(arg, pltpu.HBM) if place == "h" else arg
+        pltpu.with_memory_space_constraint(arg, pltpu.HBM) if place in "hp" else arg
         for arg, place in zip(args, places)
     ]
     n_in, n_out, n_scratch = len(args), len(outs), len(scratch)
@@ -305,63 +345,62 @@
     part = width // peers
     piece = width // PIECES
     shape = jax.ShapeDtypeStruct
-    bias, w_out = bias[None], w_out[None]
+    bias, w_out = bias[None], w_out.reshape(width // LANES, LANES)
     pairs = [(i, i ^ 1) for i in range(replicas)]
-    at = jnp.stack([lax.axis_index("dp"), lax.axis_index("replica") % 2]).astype(jnp.int32)
-
     message = (peers, PIECES, piece + LANES)
-    slots = call(
+    slots, pack = call(
         request_kernel,
-        shape(message, BF16),
-        user_row, seg, grad_score, feat,
-        places="hhhh",
+        (shape(message, BF16), shape((16 + req, width), BF16)),
+        user_row, seg, grad_score, user, feat,
+        places="hhhhh",
         scratch=[pltpu.VMEM(message, F32)],
-    )
-    swap = call(
-        swap_kernel,
-        shape((16 + req, width), BF16),
-        slots, grad_score, user,
-        places="ahh",
     )
     arrived = lax.all_to_all(slots, "dp", split_axis=0, concat_axis=0, tiled=True)
     swapped_feat = lax.ppermute(feat, "replica", pairs)
-    swapped = lax.ppermute(swap, "replica", pairs)
-    base, half, vw, users, user_half, tail = call(
+    swapped = lax.ppermute(pack, "replica", pairs)
+    base, user_half, other_user = call(
         main_kernel,
         (
             shape((peers, 8, 4 * rank + LANES), BF16),
-            shape((width, rank), BF16),
-            shape((rank, width), BF16),
-            shape((2 * req, width), BF16),
             shape((2 * req, rank), F32),
-            shape((part, rank + LANES), F32),
+            shape((req, width), BF16),
         ),
-        at, feat, grad_score, user, swapped_feat, swapped, u_weight, v_weight, bias, w_out,
-        scratch=[pltpu.VMEM((2 * rows, width), BF16)],
-        places="shhhnnhhhh",
-        out_places="nhhnnn",
+        feat, swapped_feat, grad_score, user, swapped, u_weight, v_weight, w_out,
+        places="pahhnhhh",
+        out_places="hhh",
+        scratch=[
+            pltpu.VMEM((2 * rows, width), BF16),
+            pltpu.VMEM((2 * rows, rank), F32),
+            pltpu.SemaphoreType.DMA((2,)),
+        ],
         cost=pl.CostEstimate(flops=1, bytes_accessed=1, transcendentals=0),
     )
     own = call(
         pick_kernel,
         shape((req, width + LANES), BF16),
-        arrived, tail,
-        places="-a",
+        arrived, user_half,
+        places="-p",
         scratch=[pltpu.VMEM(message, F32)],
     )
     other = lax.ppermute(own, "replica", pairs)
     parts = call(
         merge_kernel,
         shape((peers, 8, 4 * rank + LANES), BF16),
-        base, own, other, users, half, user_half,
-        places="n--nhn",
+        base, own, other, user, other_user, w_out, user_half, u_weight, v_weight,
+        places="h--hhhhpp",
+        scratch=[
+            pltpu.VMEM((width, rank), BF16),
+            pltpu.VMEM((rank, width), BF16),
+            pltpu.VMEM((2 * req, rank), F32),
+            pltpu.SemaphoreType.DMA,
+        ],
     )
     received = lax.all_to_all(parts, "dp", split_axis=0, concat_axis=0, tiled=True)
-    user_grad = call(
+    user_grad, tail = call(
         user_grad_kernel,
-        shape((req, width), F32),
-        own, user, u_weight, v_weight, vw, bias, w_out,
-        places="-hhhnhh",
+        (shape((req, width), F32), shape((part, rank + LANES), F32)),
+        own, user, u_weight, v_weight, bias, w_out,
+        places="-hhhhh",
     )
     copies = call(sum_kernel, shape((replicas, 8, 4 * rank + LANES), BF16), received)
     gathered = lax.all_to_all(copies, "replica", split_axis=0, concat_axis=0, tiled=True)

time: 116 us -> 112 us (0.966)
  waiting for transfers between devices: 12.4 us -> 16.3 us
  blocking collectives: 39.5 us -> 36.3 us
  Pallas kernels: 20.4 us -> 17.4 us
    all_to_all x1, waiting for transfers between devices: 2.15 us -> 5.39 us  [per_device(): lax.all_to_all(slots, 'dp', split_axis=0, concat_axis=0, tiled=True)]
    all_to_all x1, blocking collectives: 39.5 us -> 36.3 us  [per_device(): lax.all_to_all(parts, 'dp', split_axis=0, concat_axis=0, tiled=True)]
    pallas_call x8 -> x7, Pallas kernels: 20.4 us -> 17.4 us  [call(): pl.pallas_call(body, out_shape=pinned if several else pinned[0], in_specs...]
  transfers between devices with their start and end apart: 5 -> 5, of which waited for: 4 -> 4; matrix products, arithmetic and copies ran while one was open for 1% -> 0% of each run, Pallas kernels for 13% -> 11%
where the time goes in v4:
time: 112 us
  starting transfers between devices  41.2 us (37%)
  blocking collectives  36.3 us (32%)
  Pallas kernels  17.4 us (16%)
  waiting for transfers between devices  16.3 us (15%)
    all_to_all x1, blocking collectives, per_device(): lax.all_to_all(parts, 'dp', split_axis=0, concat_axis=0, tiled=True)  36.3 us
    pallas_call x7, Pallas kernels, call(): pl.pallas_call(body, out_shape=pinned if several else pinned[0], in_specs...  17.4 us
    ppermute x1, starting transfers between devices, per_device(): swapped_feat = lax.ppermute(feat, 'replica', pairs)  16.1 us
    all_to_all x1, starting transfers between devices, per_device(): lax.all_to_all(copies, 'replica', split_axis=0, concat_axis=0, tiled=True)  15.1 us
    all_to_all x1, waiting for transfers between devices, per_device(): lax.all_to_all(copies, 'replica', split_axis=0, concat_axis=0, tiled=True)  8.7 us
    all_to_all x1, waiting for transfers between devices, per_device(): lax.all_to_all(slots, 'dp', split_axis=0, concat_axis=0, tiled=True)  5.39 us
    all_to_all x1, starting transfers between devices, per_device(): lax.all_to_all(slots, 'dp', split_axis=0, concat_axis=0, tiled=True)  4.63 us
    ppermute x1, starting transfers between devices, per_device(): other = lax.ppermute(own, 'replica', pairs)  3.48 us
  transfers between devices with their start and end apart: 5, of which 4 were waited for; matrix products, arithmetic and copies ran while one was open for 0% of the time, Pallas kernels for 11%

profile of v4, /device:TPU:1, one launch (start us, length us, event | category | flops | bytes accessed | tf_op | source)
XLA Modules:
  0.0 111.9 jit_solution(15513755088360096299)
XLA Ops:
  0.6 16.1 %collective-permute-start = (bf16[256,2048]{1,0:T(8,128)(2,1)}, bf16[256,2048]{1,0:T(8,128)(2,1)S(1)}, u32[]{:S(2)}, u32[]{:S(2)}) collective-permute-start(bf16[256,2048]{1,0:T(8,128)(2,1)} %bitcast.8), channel_id=1, source_target_pairs={{0,1},{1,0},{2,3},{3,2},{4,5},{5,4},{6,7},{7,6},{8,9},{9,8},{10,11... | collective-permute-start | bytes 3145736 | tf_op jit(solution)/shard_map/ppermute | solution.py:359
  16.7 2.7 %shard_map.128 = (bf16[64,2,1152]{2,1,0:T(2,128)(2,1)}, bf16[32,2048]{1,0:T(8,128)(2,1)S(1)}) custom-call(s32[1,16]{1,0:T(1,128)} %refs_0_.1, s32[1,256]{1,0:T(1,128)} %bitcast.19, f32[1,256]{1,0:T(1,128)} %refs_2_.4, bf16[16,2048]{1,0:T(8,128)(2,1)} %bitcast.11, bf16[256,2048]{1,0:T(8,128)(2,1)} %bitcast.9), custom_call_target="tpu_custom_call" | custom-call | tf_op jit(solution)/shard_map/pallas_call | solution.py:326
  19.4 4.6 %all-to-all-start = ((bf16[64,2,1152]{2,1,0:T(2,128)(2,1)}), bf16[64,2,1152]{2,1,0:T(2,128)(2,1)S(1)}, u32[]{:S(2)}, u32[]{:S(2)}) async-start(bf16[64,2,1152]{2,1,0:T(2,128)(2,1)} %get-tuple-element.16), calls=%async_computation | async-start | bytes 589824 | tf_op jit(solution)/shard_map/all_to_all | solution.py:358
  24.0 1.9 %collective-permute-start.1 = (bf16[32,2048]{1,0:T(8,128)(2,1)S(1)}, bf16[32,2048]{1,0:T(8,128)(2,1)S(1)}, u32[]{:S(2)}, u32[]{:S(2)}) collective-permute-start(bf16[32,2048]{1,0:T(8,128)(2,1)S(1)} %get-tuple-element.17), channel_id=1, source_target_pairs={{0,1},{1,0},{2,3},{3,2},{4,5},{5,4},{6,7},{7,6},{8,9},{9,8},{10,11... | collective-permute-start | bytes 393224 | tf_op jit(solution)/shard_map/ppermute | solution.py:360
  25.9 1.3 %collective-permute-done.1.refs_4_ = bf16[32,2048]{1,0:T(8,128)(2,1)S(1)} collective-permute-done((bf16[32,2048]{1,0:T(8,128)(2,1)S(1)}, bf16[32,2048]{1,0:T(8,128)(2,1)S(1)}, u32[]{:S(2)}, u32[]{:S(2)}) %collective-permute-start.1) | collective-permute-done | bytes 131104 | tf_op jit(solution)/shard_map/ppermute | solution.py:360
  27.2 0.0 collective-permute-done.refs_1_
  27.3 5.7 %shard_map.129 = (bf16[64,8,1152]{2,1,0:T(8,128)(2,1)}, f32[32,256]{1,0:T(8,128)}, bf16[16,2048]{1,0:T(8,128)(2,1)}) custom-call(bf16[256,2048]{1,0:T(8,128)(2,1)} %bitcast.10, bf16[256,2048]{1,0:T(8,128)(2,1)S(1)} %collective-permute-done.refs_1_, f32[1,256]{1,0:T(1,128)} %refs_2_.4, bf16[16,2048]{1,0:T(8,128)(2,1)} %bitcast.12, ...), custom_call_target="tpu_custom_call" | custom-call | flops 1 | bytes 1 | tf_op jit(solution)/shard_map/pallas_call | solution.py:326
  33.0 5.4 %all-to-all-done.refs_0_ = bf16[64,2,1152]{2,1,0:T(2,128)(2,1)S(1)} async-done(((bf16[64,2,1152]{2,1,0:T(2,128)(2,1)}), bf16[64,2,1152]{2,1,0:T(2,128)(2,1)S(1)}, u32[]{:S(2)}, u32[]{:S(2)}) %all-to-all-start) | async-done | bytes 294944 | tf_op jit(solution)/shard_map/all_to_all | solution.py:358
  38.4 0.7 shard_map.130.refs_0_.refs_1_
  39.1 3.5 %collective-permute-start.2 = (bf16[16,2176]{1,0:T(8,128)(2,1)S(1)}, bf16[16,2176]{1,0:T(8,128)(2,1)S(1)}, u32[]{:S(2)}, u32[]{:S(2)}) collective-permute-start(bf16[16,2176]{1,0:T(8,128)(2,1)S(1)} %shard_map.130.refs_0_.refs_1_), channel_id=1, source_target_pairs={{0,1},{1,0},{2,3},{3,2},{4,5},{5,4},{6,7},{7,6},{8,9},{9,8},{10,11... | collective-permute-start | bytes 208904 | tf_op jit(solution)/shard_map/ppermute | solution.py:385
  42.6 0.9 collective-permute-done.2.refs_2_
  43.5 2.8 %shard_map.132 = bf16[64,8,1152]{2,1,0:T(8,128)(2,1)S(1)} custom-call(bf16[64,8,1152]{2,1,0:T(8,128)(2,1)} %get-tuple-element.20.refs_0_, bf16[16,2176]{1,0:T(8,128)(2,1)S(1)} %shard_map.130.refs_0_.refs_1_, bf16[16,2176]{1,0:T(8,128)(2,1)S(1)} %collective-permute-done.2.refs_2_, bf16[16,2048]{1,0:T(8,128)(2,1)} %bitcast.13, ...), custom_call_target="tpu_custom_call" | custom-call | tf_op jit(solution)/shard_map/pallas_call | solution.py:326
  46.3 36.3 %all_to_all.15.refs_0_ = bf16[64,8,1152]{2,1,0:T(8,128)(2,1)S(1)} all-to-all(bf16[64,8,1152]{2,1,0:T(8,128)(2,1)S(1)} %shard_map.132), channel_id=1, replica_groups=mesh['dp'=64,'replica'=16] {'dp'}, dimensions={0} | all-to-all | bytes 2359296 | tf_op jit(solution)/shard_map/all_to_all | solution.py:398
  82.7 0.9 shard_map.133
  83.6 15.1 %all-to-all-start.2 = ((bf16[16,8,1152]{2,1,0:T(8,128)(2,1)}), bf16[16,8,1152]{2,1,0:T(8,128)(2,1)S(1)}, u32[]{:S(2)}, u32[]{:S(2)}) async-start(bf16[16,8,1152]{2,1,0:T(8,128)(2,1)} %shard_map.133), calls=%async_computation.2 | async-start | bytes 589824 | tf_op jit(solution)/shard_map/all_to_all | solution.py:406
  98.7 3.7 %shard_map.131 = (f32[16,2048]{1,0:T(8,128)}, f32[32,384]{1,0:T(8,128)S(1)}) custom-call(bf16[16,2176]{1,0:T(8,128)(2,1)S(1)} %shard_map.130.refs_0_.refs_1_, bf16[16,2048]{1,0:T(8,128)(2,1)} %bitcast.14, bf16[2048,256]{1,0:T(8,128)(2,1)} %refs_7_.1, bf16[256,2048]{1,0:T(8,128)(2,1)} %refs_8_.1, f32[1,2048]{1,0:T(1,128)} %bitcast.18, bf16[16,128]{1,0:T(8,128)(2,1)} %bitcast.17), custom_call_target="tpu_custom_call" | custom-call | tf_op jit(solution)/shard_map/pallas_call | solution.py:326
  102.3 8.7 %all-to-all-done.2.refs_0_ = bf16[16,8,1152]{2,1,0:T(8,128)(2,1)S(1)} async-done(((bf16[16,8,1152]{2,1,0:T(8,128)(2,1)}), bf16[16,8,1152]{2,1,0:T(8,128)(2,1)S(1)}, u32[]{:S(2)}, u32[]{:S(2)}) %all-to-all-start.2) | async-done | bytes 294944 | tf_op jit(solution)/shard_map/all_to_all | solution.py:406
  111.0 0.9 shard_map.134
Async XLA Ops:
  0.6 26.6 %collective-permute-start = (bf16[256,2048]{1,0:T(8,128)(2,1)}, bf16[256,2048]{1,0:T(8,128)(2,1)S(1)}, u32[]{:S(2)}, u32[]{:S(2)}) collective-permute-start(bf16[256,2048]{1,0:T(8,128)(2,1)} %bitcast.8), channel_id=1, source_target_pairs={{0,1},{1,0},{2,3},{3,2},{4,5},{5,4},{6,7},{7,6},{8,9},{9,8},{10,11... | collective-permute-start | bytes 3145736 | tf_op jit(solution)/shard_map/ppermute | solution.py:359
  19.4 19.0 %all-to-all-start = ((bf16[64,2,1152]{2,1,0:T(2,128)(2,1)}), bf16[64,2,1152]{2,1,0:T(2,128)(2,1)S(1)}, u32[]{:S(2)}, u32[]{:S(2)}) async-start(bf16[64,2,1152]{2,1,0:T(2,128)(2,1)} %get-tuple-element.16), calls=%async_computation | async-start | bytes 589824 | tf_op jit(solution)/shard_map/all_to_all | solution.py:358
  24.0 3.2 %collective-permute-start.1 = (bf16[32,2048]{1,0:T(8,128)(2,1)S(1)}, bf16[32,2048]{1,0:T(8,128)(2,1)S(1)}, u32[]{:S(2)}, u32[]{:S(2)}) collective-permute-start(bf16[32,2048]{1,0:T(8,128)(2,1)S(1)} %get-tuple-element.17), channel_id=1, source_target_pairs={{0,1},{1,0},{2,3},{3,2},{4,5},{5,4},{6,7},{7,6},{8,9},{9,8},{10,11... | collective-permute-start | bytes 393224 | tf_op jit(solution)/shard_map/ppermute | solution.py:360
  39.1 4.4 %collective-permute-start.2 = (bf16[16,2176]{1,0:T(8,128)(2,1)S(1)}, bf16[16,2176]{1,0:T(8,128)(2,1)S(1)}, u32[]{:S(2)}, u32[]{:S(2)}) collective-permute-start(bf16[16,2176]{1,0:T(8,128)(2,1)S(1)} %shard_map.130.refs_0_.refs_1_), channel_id=1, source_target_pairs={{0,1},{1,0},{2,3},{3,2},{4,5},{5,4},{6,7},{7,6},{8,9},{9,8},{10,11... | collective-permute-start | bytes 208904 | tf_op jit(solution)/shard_map/ppermute | solution.py:385
  83.6 27.4 %all-to-all-start.2 = ((bf16[16,8,1152]{2,1,0:T(8,128)(2,1)}), bf16[16,8,1152]{2,1,0:T(8,128)(2,1)S(1)}, u32[]{:S(2)}, u32[]{:S(2)}) async-start(bf16[16,8,1152]{2,1,0:T(8,128)(2,1)} %shard_map.133), calls=%async_computation.2 | async-start | bytes 589824 | tf_op jit(solution)/shard_map/all_to_all | solution.py:406

commit v5 on v4

--- a/solution.py
+++ b/solution.py
@@ -34,11 +34,18 @@
 
 
 def request_kernel(
-    wait, wanted_ref, seg_ref, score_ref, user_ref, feat_ref, slots_ref, pack_ref, wide
+    wait, wanted_ref, seg_ref, score_ref, user_ref, feat_any, slots_ref, pack_ref, wide, feat_ref, sems
 ):
     peers, req = slots_ref.shape[0], wanted_ref.shape[1]
     rows, width = feat_ref.shape
     piece = width // PIECES
+    parts = [pl.ds(p * piece, piece) for p in range(PIECES)]
+    copies = [
+        pltpu.make_async_copy(feat_any.at[:, part], feat_ref.at[:, part], sems.at[p])
+        for p, part in enumerate(parts)
+    ]
+    for copy in copies:
+        copy.start()
     wait(0, 1, 2)
     wanted = wanted_ref[...]
     owner = lax.div(wanted, jnp.int32(req))
@@ -72,21 +79,31 @@
     ).astype(BF16)
     wait(3)
     pack_ref[16:, :] = user_ref[...]
-    wait(4)
     for p in range(PIECES):
+        copies[p].wait()
         wide[:, p, :piece] = dot(weights, feat_ref[:, p * piece : (p + 1) * piece])
     slots_ref[...] = wide[...].astype(BF16)
 
 
-def lay_out(grad, out_ref, base, base_sums):
-    peers, rank = out_ref.shape[0], grad.shape[1] - LANES
-    blocks = grad.reshape(peers, 4, 8, rank + LANES)
-    lane = iota((peers, 8, LANES), 2)
-    sums = jnp.zeros((peers, 8, LANES), F32)
+def lay_out(grad, sums, out_ref, base):
+    peers, rank = out_ref.shape[0], grad.shape[1]
+    part = grad.shape[0] // peers
+    blocks = grad.reshape(peers, 4, 8, rank)
     for q in range(4):
-        out_ref[:, :, q * rank : (q + 1) * rank] = (blocks[:, q, :, :rank] + base(q)).astype(BF16)
-        sums = jnp.where(lane == q, blocks[:, q, :, rank:], sums)
-    out_ref[:, :, 4 * rank :] = (sums + base_sums).astype(BF16)
+        out_ref[:, :, q * rank : (q + 1) * rank] = (
+            blocks[:, q] + base(slice(q * rank, (q + 1) * rank))
+        ).astype(BF16)
+    each = LANES // part
+    turned = [sums] + [
+        jnp.concatenate([sums[:, k * part :], sums[:, : k * part]], axis=1) for k in range(1, each)
+    ]
+    lines = [
+        turned[j % each][:, j // each * LANES : (j // each + 1) * LANES] for j in range(peers)
+    ]
+    lines = jnp.concatenate([jnp.broadcast_to(line, (8, LANES)) for line in lines], axis=0)
+    out_ref[:, :, 4 * rank :] = (
+        lines.reshape(peers, 8, LANES) + base(slice(4 * rank, 4 * rank + LANES))
+    ).astype(BF16)
 
 
 def row_of(ref):
@@ -98,9 +115,20 @@
     return lax.rem(lax.axis_index("replica"), 2)
 
 
+def get_factor(u_any, v_any, u_ref, v_ref, sem):
+    copies = [
+        pltpu.make_async_copy(u_any, u_ref, sem),
+        pltpu.make_async_copy(v_any, v_ref, sem),
+    ]
+    core = my_core()
+    for k in (0, 1):
+        pl.when(core == k)(copies[k].start)
+    return copies
+
+
 def main_kernel(
-    wait, feat_any, other_any, score_ref, user_ref, pack_ref, u_ref, v_ref, w_ref,
-    base_ref, user_half_ref, next_ref, both, low_ref, sems,
+    wait, feat_any, other_any, score_ref, user_ref, pack_ref, w_ref, u_any, v_any,
+    base_ref, user_half_ref, next_ref, both, low_ref, u_ref, v_ref, sems,
 ):
     rows, width = feat_any.shape
     rank = v_ref.shape[0]
@@ -109,38 +137,49 @@
         pltpu.make_async_copy(feat_any, both.at[:rows], sems.at[0]),
         pltpu.make_async_copy(other_any, both.at[rows:], sems.at[1]),
     ]
+    factors = get_factor(u_any, v_any, u_ref, v_ref, sems.at[2])
     for copy in copies:
         copy.start()
-    wait(2, 3, 4)
+    wait(2, 3, 4, 5)
     next_ref[...] = pack_ref[16:, :]
     marks = pack_ref[:16, :rows].astype(F32)
     scores = jnp.concatenate(
         [as_columns(score_ref[...]), as_columns(marks[0:1, :] + marks[1:2, :])], axis=0
     )
-    wait(5, 6, 7)
+    users = jnp.concatenate([user_ref[...], pack_ref[16:, :]], axis=0)
+    core = my_core()
+
+    @pl.when(core == 0)
+    def _():
+        factors[0].wait()
+        user_half_ref[...] = dot(users, u_ref[...])
+
+    @pl.when(core == 1)
+    def _():
+        factors[1].wait()
+        v_ref[...] = (v_ref[...].astype(F32) * row_of(w_ref)).astype(BF16)
+        user_half_ref[...] = dot(users, v_ref[...], NT)
+
     for copy in copies:
         copy.wait()
-    core = my_core()
 
     @pl.when(core == 0)
     def _():
-        u = u_ref[...]
-        low_ref[...] = dot(both[...], u)
-        user_half_ref[:req, :] = dot(user_ref[...], u)
-        user_half_ref[req:, :] = dot(pack_ref[16:, :], u)
+        low_ref[...] = dot(both[...], u_ref[...])
 
     @pl.when(core == 1)
     def _():
-        vw = (v_ref[...].astype(F32) * row_of(w_ref)).astype(BF16)
-        low_ref[...] = dot(both[...], vw, NT)
-        user_half_ref[:req, :] = dot(user_ref[...], vw, NT)
-        user_half_ref[req:, :] = dot(pack_ref[16:, :], vw, NT)
+        low_ref[...] = dot(both[...], v_ref[...], NT)
 
     scaled = [low_ref[:, k : k + LANES] * scores for k in range(0, rank, LANES)]
-    lane = iota((2 * rows, LANES), 1)
-    scaled.append(jnp.where(lane < 4, scores, 0.0))
     scaled = jnp.concatenate(scaled, axis=1).astype(BF16)
-    lay_out(dot(both[...], scaled, TN), base_ref, lambda q: 0.0, 0.0)
+    sums = []
+    for k in range(0, width, LANES):
+        sums.append(
+            jnp.sum(both[:, k : k + LANES].astype(F32) * scores, axis=0, keepdims=True)
+        )
+    sums = jnp.concatenate(sums, axis=1)
+    lay_out(dot(both[...], scaled, TN), sums, base_ref, lambda part: 0.0)
 
 
 def pick_kernel(wait, slots_ref, after_any, out_ref, wide):
@@ -162,57 +201,41 @@
 
 
 def merge_kernel(
-    wait, base_ref, own_ref, other_ref, user_ref, next_ref, w_ref, user_half_ref, u_any, v_any,
-    out_ref, u_ref, v_ref, both_ref, sem,
+    wait, own_ref, other_ref, user_ref, next_ref, w_ref, user_half_ref, base_any, u_any, v_any,
+    out_ref, base_ref, u_ref, v_ref, both_ref, sems,
 ):
     req, width = user_ref.shape
-    rank = user_half_ref.shape[1]
-    core = my_core()
-    get_u = pltpu.make_async_copy(u_any, u_ref, sem)
-    get_v = pltpu.make_async_copy(v_any, v_ref, sem)
-
-    @pl.when(core == 0)
-    def _():
-        get_u.start()
-
-    @pl.when(core == 1)
-    def _():
-        get_v.start()
-
+    factors = get_factor(u_any, v_any, u_ref, v_ref, sems.at[0])
+    get_base = pltpu.make_async_copy(base_any, base_ref, sems.at[1])
+    get_base.start()
     own, other = own_ref[...], other_ref[...]
     sums = jnp.concatenate([own[:, :width], other[:, :width]], axis=0)
     total = jnp.concatenate([total_of(own, width, req), total_of(other, width, req)], axis=0)
-    wait(3, 4, 5, 6)
+    wait(2, 3, 4, 5)
+    users = jnp.concatenate([user_ref[...], next_ref[...]], axis=0)
+    core = my_core()
 
     @pl.when(core == 0)
     def _():
-        get_u.wait()
+        factors[0].wait()
         both_ref[...] = dot(sums, u_ref[...])
 
     @pl.when(core == 1)
     def _():
-        get_v.wait()
         weighted = (sums.astype(F32) * row_of(w_ref)).astype(BF16)
+        factors[1].wait()
         both_ref[...] = dot(weighted, v_ref[...], NT)
 
     user_half = user_half_ref[...]
     both = both_ref[...] + total * user_half
-    lane = iota((2 * req, LANES), 1)
-    lines = jnp.concatenate([sums, user_ref[...], next_ref[...]], axis=0)
-    factors = jnp.concatenate(
-        [
-            jnp.concatenate([user_half, jnp.zeros((2 * req, LANES), F32)], axis=1),
-            jnp.concatenate([both, jnp.where(lane < 4, total, 0.0)], axis=1),
-        ],
-        axis=0,
-    ).astype(BF16)
-    wait(0)
-    lay_out(
-        dot(lines, factors, TN),
-        out_ref,
-        lambda q: base_ref[:, :, q * rank : (q + 1) * rank].astype(F32),
-        base_ref[:, :, 4 * rank :].astype(F32),
-    )
+    grad = dot(
+        jnp.concatenate([sums, users], axis=0),
+        jnp.concatenate([user_half, both], axis=0).astype(BF16),
+        TN,
+    )
+    user_sums = jnp.sum(total * users.astype(F32), axis=0, keepdims=True)
+    get_base.wait()
+    lay_out(grad, user_sums, out_ref, lambda part: base_ref[:, :, part].astype(F32))
 
 
 def user_grad_kernel(wait, pack_ref, user_ref, u_ref, v_ref, bias_ref, w_ref, out_ref, tail_ref):
@@ -256,9 +279,7 @@
     low, grad_low = (
         jnp.concatenate([s[:, q * rank : (q + 1) * rank] for q in range(4)], axis=0) for s in sums
     )
-    column = jnp.concatenate(
-        [sums[0][:, 4 * rank + q : 4 * rank + q + 1] for q in range(4)], axis=0
-    )
+    column = as_columns(sums[0][0:1, 4 * rank :])[:part, 0:1]
     tail = tail_ref[...]
     w_col, b_col = tail[:, rank : rank + 1], tail[:, rank + 1 : rank + 2]
     grad_u_ref[...] = grad_low
@@ -352,26 +373,33 @@
         request_kernel,
         (shape(message, BF16), shape((16 + req, width), BF16)),
         user_row, seg, grad_score, user, feat,
-        places="hhhhh",
-        scratch=[pltpu.VMEM(message, F32)],
+        places="hhhhp",
+        scratch=[
+            pltpu.VMEM(message, F32),
+            pltpu.VMEM((rows, width), BF16),
+            pltpu.SemaphoreType.DMA((PIECES,)),
+        ],
     )
     arrived = lax.all_to_all(slots, "dp", split_axis=0, concat_axis=0, tiled=True)
     swapped_feat = lax.ppermute(feat, "replica", pairs)
     swapped = lax.ppermute(pack, "replica", pairs)
+    factor_buffers = [pltpu.VMEM((width, rank), BF16), pltpu.VMEM((rank, width), BF16)]
+    parts_shape = (peers, 8, 4 * rank + LANES)
     base, user_half, other_user = call(
         main_kernel,
         (
-            shape((peers, 8, 4 * rank + LANES), BF16),
+            shape(parts_shape, BF16),
             shape((2 * req, rank), F32),
             shape((req, width), BF16),
         ),
-        feat, swapped_feat, grad_score, user, swapped, u_weight, v_weight, w_out,
-        places="pahhnhhh",
+        feat, swapped_feat, grad_score, user, swapped, w_out, u_weight, v_weight,
+        places="pahhnhpp",
         out_places="hhh",
         scratch=[
             pltpu.VMEM((2 * rows, width), BF16),
             pltpu.VMEM((2 * rows, rank), F32),
-            pltpu.SemaphoreType.DMA((2,)),
+            *factor_buffers,
+            pltpu.SemaphoreType.DMA((3,)),
         ],
         cost=pl.CostEstimate(flops=1, bytes_accessed=1, transcendentals=0),
     )
@@ -385,14 +413,14 @@
     other = lax.ppermute(own, "replica", pairs)
     parts = call(
         merge_kernel,
-        shape((peers, 8, 4 * rank + LANES), BF16),
-        base, own, other, user, other_user, w_out, user_half, u_weight, v_weight,
-        places="h--hhhhpp",
+        shape(parts_shape, BF16),
+        own, other, user, other_user, w_out, user_half, base, u_weight, v_weight,
+        places="--hhhhppp",
         scratch=[
-            pltpu.VMEM((width, rank), BF16),
-            pltpu.VMEM((rank, width), BF16),
+            pltpu.VMEM(parts_shape, BF16),
+            *factor_buffers,
             pltpu.VMEM((2 * req, rank), F32),
-            pltpu.SemaphoreType.DMA,
+            pltpu.SemaphoreType.DMA((2,)),
         ],
     )
     received = lax.all_to_all(parts, "dp", split_axis=0, concat_axis=0, tiled=True)

time: 112 us -> 112 us (level)
  transfers between devices with their start and end apart: 5 -> 5, of which waited for: 4 -> 4; matrix products, arithmetic and copies ran while one was open for 0% -> 0% of each run, Pallas kernels for 11% -> 10%
where the time goes in v5:
time: 112 us; the launch traced here: 111 us
  starting transfers between devices  41.1 us (37%)
  blocking collectives  35.7 us (32%)
  waiting for transfers between devices  17 us (15%)
  Pallas kernels  16.6 us (15%)
    all_to_all x1, blocking collectives, per_device(): lax.all_to_all(parts, 'dp', split_axis=0, concat_axis=0, tiled=True)  35.7 us
    pallas_call x7, Pallas kernels, call(): pl.pallas_call(body, out_shape=pinned if several else pinned[0], in_specs...  16.6 us
    ppermute x1, starting transfers between devices, per_device(): swapped_feat = lax.ppermute(feat, 'replica', pairs)  16.1 us
    all_to_all x1, starting transfers between devices, per_device(): lax.all_to_all(copies, 'replica', split_axis=0, concat_axis=0, tiled=True)  15 us
    all_to_all x1, waiting for transfers between devices, per_device(): lax.all_to_all(copies, 'replica', split_axis=0, concat_axis=0, tiled=True)  8.7 us
    all_to_all x1, waiting for transfers between devices, per_device(): lax.all_to_all(slots, 'dp', split_axis=0, concat_axis=0, tiled=True)  6.08 us
    all_to_all x1, starting transfers between devices, per_device(): lax.all_to_all(slots, 'dp', split_axis=0, concat_axis=0, tiled=True)  4.63 us
    ppermute x1, starting transfers between devices, per_device(): other = lax.ppermute(own, 'replica', pairs)  3.48 us
  transfers between devices with their start and end apart: 5, of which 4 were waited for; matrix products, arithmetic and copies ran while one was open for 0% of the time, Pallas kernels for 10%

profile of v5, /device:TPU:1, one launch (start us, length us, event | category | flops | bytes accessed | tf_op | source)
XLA Modules:
  0.0 111.0 jit_solution(16989286261354824270)
XLA Ops:
  0.6 16.1 %collective-permute-start = (bf16[256,2048]{1,0:T(8,128)(2,1)}, bf16[256,2048]{1,0:T(8,128)(2,1)S(1)}, u32[]{:S(2)}, u32[]{:S(2)}) collective-permute-start(bf16[256,2048]{1,0:T(8,128)(2,1)} %bitcast.8), channel_id=1, source_target_pairs={{0,1},{1,0},{2,3},{3,2},{4,5},{5,4},{6,7},{7,6},{8,9},{9,8},{10,11... | collective-permute-start | bytes 3145736 | tf_op jit(solution)/shard_map/ppermute | solution.py:384
  16.7 2.6 %shard_map.128 = (bf16[64,2,1152]{2,1,0:T(2,128)(2,1)}, bf16[32,2048]{1,0:T(8,128)(2,1)S(1)}) custom-call(s32[1,16]{1,0:T(1,128)} %refs_0_.1, s32[1,256]{1,0:T(1,128)} %bitcast.19, f32[1,256]{1,0:T(1,128)} %refs_2_.4, bf16[16,2048]{1,0:T(8,128)(2,1)} %bitcast.11, bf16[256,2048]{1,0:T(8,128)(2,1)} %bitcast.9), custom_call_target="tpu_custom_call" | custom-call | tf_op jit(solution)/shard_map/pallas_call | solution.py:347
  19.3 4.6 %all-to-all-start = ((bf16[64,2,1152]{2,1,0:T(2,128)(2,1)}), bf16[64,2,1152]{2,1,0:T(2,128)(2,1)S(1)}, u32[]{:S(2)}, u32[]{:S(2)}) async-start(bf16[64,2,1152]{2,1,0:T(2,128)(2,1)} %get-tuple-element.16), calls=%async_computation | async-start | bytes 589824 | tf_op jit(solution)/shard_map/all_to_all | solution.py:383
  23.9 1.9 %collective-permute-start.1 = (bf16[32,2048]{1,0:T(8,128)(2,1)S(1)}, bf16[32,2048]{1,0:T(8,128)(2,1)S(1)}, u32[]{:S(2)}, u32[]{:S(2)}) collective-permute-start(bf16[32,2048]{1,0:T(8,128)(2,1)S(1)} %get-tuple-element.17), channel_id=1, source_target_pairs={{0,1},{1,0},{2,3},{3,2},{4,5},{5,4},{6,7},{7,6},{8,9},{9,8},{10,11... | collective-permute-start | bytes 393224 | tf_op jit(solution)/shard_map/ppermute | solution.py:385
  25.9 1.3 %collective-permute-done.1.refs_4_ = bf16[32,2048]{1,0:T(8,128)(2,1)S(1)} collective-permute-done((bf16[32,2048]{1,0:T(8,128)(2,1)S(1)}, bf16[32,2048]{1,0:T(8,128)(2,1)S(1)}, u32[]{:S(2)}, u32[]{:S(2)}) %collective-permute-start.1) | collective-permute-done | bytes 131104 | tf_op jit(solution)/shard_map/ppermute | solution.py:385
  27.2 0.0 collective-permute-done.refs_1_
  27.2 5.0 %shard_map.129 = (bf16[64,8,1152]{2,1,0:T(8,128)(2,1)}, f32[32,256]{1,0:T(8,128)}, bf16[16,2048]{1,0:T(8,128)(2,1)}) custom-call(bf16[256,2048]{1,0:T(8,128)(2,1)} %bitcast.10, bf16[256,2048]{1,0:T(8,128)(2,1)S(1)} %collective-permute-done.refs_1_, f32[1,256]{1,0:T(1,128)} %refs_2_.4, bf16[16,2048]{1,0:T(8,128)(2,1)} %bitcast.12, ...), custom_call_target="tpu_custom_call" | custom-call | flops 1 | bytes 1 | tf_op jit(solution)/shard_map/pallas_call | solution.py:347
  32.2 6.1 %all-to-all-done.refs_0_ = bf16[64,2,1152]{2,1,0:T(2,128)(2,1)S(1)} async-done(((bf16[64,2,1152]{2,1,0:T(2,128)(2,1)}), bf16[64,2,1152]{2,1,0:T(2,128)(2,1)S(1)}, u32[]{:S(2)}, u32[]{:S(2)}) %all-to-all-start) | async-done | bytes 294944 | tf_op jit(solution)/shard_map/all_to_all | solution.py:383
  38.3 0.7 shard_map.130.refs_0_
  39.0 3.5 %collective-permute-start.2 = (bf16[16,2176]{1,0:T(8,128)(2,1)S(1)}, bf16[16,2176]{1,0:T(8,128)(2,1)S(1)}, u32[]{:S(2)}, u32[]{:S(2)}) collective-permute-start(bf16[16,2176]{1,0:T(8,128)(2,1)S(1)} %shard_map.130.refs_0_), channel_id=1, source_target_pairs={{0,1},{1,0},{2,3},{3,2},{4,5},{5,4},{6,7},{7,6},{8,9},{9,8},{10,11... | collective-permute-start | bytes 208904 | tf_op jit(solution)/shard_map/ppermute | solution.py:413
  42.5 0.9 collective-permute-done.2.refs_1_
  43.4 2.7 %shard_map.132 = bf16[64,8,1152]{2,1,0:T(8,128)(2,1)S(1)} custom-call(bf16[16,2176]{1,0:T(8,128)(2,1)S(1)} %shard_map.130.refs_0_, bf16[16,2176]{1,0:T(8,128)(2,1)S(1)} %collective-permute-done.2.refs_1_, bf16[16,2048]{1,0:T(8,128)(2,1)} %bitcast.13, bf16[16,2048]{1,0:T(8,128)(2,1)} %get-tuple-element.20.refs_3_, bf16[16,128]{1,0:T(8,128)(2,1)} %bitcast.16, ...), custom_call_target="tpu_custom_call" | custom-call | tf_op jit(solution)/shard_map/pallas_call | solution.py:347
  46.2 35.7 %all_to_all.15.refs_0_ = bf16[64,8,1152]{2,1,0:T(8,128)(2,1)S(1)} all-to-all(bf16[64,8,1152]{2,1,0:T(8,128)(2,1)S(1)} %shard_map.132), channel_id=1, replica_groups=mesh['dp'=64,'replica'=16] {'dp'}, dimensions={0} | all-to-all | bytes 2359296 | tf_op jit(solution)/shard_map/all_to_all | solution.py:426
  81.8 0.9 shard_map.133
  82.7 15.0 %all-to-all-start.2 = ((bf16[16,8,1152]{2,1,0:T(8,128)(2,1)}), bf16[16,8,1152]{2,1,0:T(8,128)(2,1)S(1)}, u32[]{:S(2)}, u32[]{:S(2)}) async-start(bf16[16,8,1152]{2,1,0:T(8,128)(2,1)} %shard_map.133), calls=%async_computation.2 | async-start | bytes 589824 | tf_op jit(solution)/shard_map/all_to_all | solution.py:434
  97.7 3.7 %shard_map.131 = (f32[16,2048]{1,0:T(8,128)}, f32[32,384]{1,0:T(8,128)S(1)}) custom-call(bf16[16,2176]{1,0:T(8,128)(2,1)S(1)} %shard_map.130.refs_0_, bf16[16,2048]{1,0:T(8,128)(2,1)} %bitcast.14, bf16[2048,256]{1,0:T(8,128)(2,1)} %refs_7_.3, bf16[256,2048]{1,0:T(8,128)(2,1)} %refs_8_.1, f32[1,2048]{1,0:T(1,128)} %bitcast.18, bf16[16,128]{1,0:T(8,128)(2,1)} %bitcast.17), custom_call_target="tpu_custom_call" | custom-call | tf_op jit(solution)/shard_map/pallas_call | solution.py:347
  101.4 8.7 %all-to-all-done.2.refs_0_ = bf16[16,8,1152]{2,1,0:T(8,128)(2,1)S(1)} async-done(((bf16[16,8,1152]{2,1,0:T(8,128)(2,1)}), bf16[16,8,1152]{2,1,0:T(8,128)(2,1)S(1)}, u32[]{:S(2)}, u32[]{:S(2)}) %all-to-all-start.2) | async-done | bytes 294944 | tf_op jit(solution)/shard_map/all_to_all | solution.py:434
  110.1 0.9 shard_map.134
Async XLA Ops:
  0.6 26.5 %collective-permute-start = (bf16[256,2048]{1,0:T(8,128)(2,1)}, bf16[256,2048]{1,0:T(8,128)(2,1)S(1)}, u32[]{:S(2)}, u32[]{:S(2)}) collective-permute-start(bf16[256,2048]{1,0:T(8,128)(2,1)} %bitcast.8), channel_id=1, source_target_pairs={{0,1},{1,0},{2,3},{3,2},{4,5},{5,4},{6,7},{7,6},{8,9},{9,8},{10,11... | collective-permute-start | bytes 3145736 | tf_op jit(solution)/shard_map/ppermute | solution.py:384
  19.3 19.0 %all-to-all-start = ((bf16[64,2,1152]{2,1,0:T(2,128)(2,1)}), bf16[64,2,1152]{2,1,0:T(2,128)(2,1)S(1)}, u32[]{:S(2)}, u32[]{:S(2)}) async-start(bf16[64,2,1152]{2,1,0:T(2,128)(2,1)} %get-tuple-element.16), calls=%async_computation | async-start | bytes 589824 | tf_op jit(solution)/shard_map/all_to_all | solution.py:383
  23.9 3.2 %collective-permute-start.1 = (bf16[32,2048]{1,0:T(8,128)(2,1)S(1)}, bf16[32,2048]{1,0:T(8,128)(2,1)S(1)}, u32[]{:S(2)}, u32[]{:S(2)}) collective-permute-start(bf16[32,2048]{1,0:T(8,128)(2,1)S(1)} %get-tuple-element.17), channel_id=1, source_target_pairs={{0,1},{1,0},{2,3},{3,2},{4,5},{5,4},{6,7},{7,6},{8,9},{9,8},{10,11... | collective-permute-start | bytes 393224 | tf_op jit(solution)/shard_map/ppermute | solution.py:385
  39.0 4.4 %collective-permute-start.2 = (bf16[16,2176]{1,0:T(8,128)(2,1)S(1)}, bf16[16,2176]{1,0:T(8,128)(2,1)S(1)}, u32[]{:S(2)}, u32[]{:S(2)}) collective-permute-start(bf16[16,2176]{1,0:T(8,128)(2,1)S(1)} %shard_map.130.refs_0_), channel_id=1, source_target_pairs={{0,1},{1,0},{2,3},{3,2},{4,5},{5,4},{6,7},{7,6},{8,9},{9,8},{10,11... | collective-permute-start | bytes 208904 | tf_op jit(solution)/shard_map/ppermute | solution.py:413
  82.7 27.4 %all-to-all-start.2 = ((bf16[16,8,1152]{2,1,0:T(8,128)(2,1)}), bf16[16,8,1152]{2,1,0:T(8,128)(2,1)S(1)}, u32[]{:S(2)}, u32[]{:S(2)}) async-start(bf16[16,8,1152]{2,1,0:T(8,128)(2,1)} %shard_map.133), calls=%async_computation.2 | async-start | bytes 589824 | tf_op jit(solution)/shard_map/all_to_all | solution.py:434

commit v6 on v5

--- a/solution.py
+++ b/solution.py
@@ -115,71 +115,61 @@
     return lax.rem(lax.axis_index("replica"), 2)
 
 
-def get_factor(u_any, v_any, u_ref, v_ref, sem):
-    copies = [
-        pltpu.make_async_copy(u_any, u_ref, sem),
-        pltpu.make_async_copy(v_any, v_ref, sem),
-    ]
-    core = my_core()
-    for k in (0, 1):
-        pl.when(core == k)(copies[k].start)
-    return copies
-
-
 def main_kernel(
     wait, feat_any, other_any, score_ref, user_ref, pack_ref, w_ref, u_any, v_any,
-    base_ref, user_half_ref, next_ref, both, low_ref, u_ref, v_ref, sems,
+    base_ref, half_ref, user_half_ref, users_ref, both, v_ref, sems,
 ):
     rows, width = feat_any.shape
     rank = v_ref.shape[0]
     req = user_ref.shape[0]
+    core = my_core()
+    get_u = pltpu.make_async_copy(u_any, half_ref, sems.at[0])
+    get_v = pltpu.make_async_copy(v_any, v_ref, sems.at[0])
     copies = [
-        pltpu.make_async_copy(feat_any, both.at[:rows], sems.at[0]),
-        pltpu.make_async_copy(other_any, both.at[rows:], sems.at[1]),
-    ]
-    factors = get_factor(u_any, v_any, u_ref, v_ref, sems.at[2])
+        pltpu.make_async_copy(feat_any, both.at[:rows], sems.at[1]),
+        pltpu.make_async_copy(other_any, both.at[rows:], sems.at[2]),
+    ]
+    pl.when(core == 0)(get_u.start)
+    pl.when(core == 1)(get_v.start)
     for copy in copies:
         copy.start()
     wait(2, 3, 4, 5)
-    next_ref[...] = pack_ref[16:, :]
+    users_ref[:req, :] = user_ref[...]
+    users_ref[req:, :] = pack_ref[16:, :]
     marks = pack_ref[:16, :rows].astype(F32)
     scores = jnp.concatenate(
         [as_columns(score_ref[...]), as_columns(marks[0:1, :] + marks[1:2, :])], axis=0
     )
-    users = jnp.concatenate([user_ref[...], pack_ref[16:, :]], axis=0)
-    core = my_core()
-
-    @pl.when(core == 0)
-    def _():
-        factors[0].wait()
-        user_half_ref[...] = dot(users, u_ref[...])
+    pl.when(core == 0)(get_u.wait)
 
     @pl.when(core == 1)
     def _():
-        factors[1].wait()
-        v_ref[...] = (v_ref[...].astype(F32) * row_of(w_ref)).astype(BF16)
-        user_half_ref[...] = dot(users, v_ref[...], NT)
-
-    for copy in copies:
+        get_v.wait()
+        half_ref[...] = jnp.transpose((v_ref[...].astype(F32) * row_of(w_ref)).astype(BF16))
+
+    half = half_ref[...]
+    user_half_ref[...] = dot(users_ref[...], half)
+    scaled, sums = [], []
+    for at, copy in zip((0, rows), copies):
         copy.wait()
-
-    @pl.when(core == 0)
-    def _():
-        low_ref[...] = dot(both[...], u_ref[...])
-
-    @pl.when(core == 1)
-    def _():
-        low_ref[...] = dot(both[...], v_ref[...], NT)
-
-    scaled = [low_ref[:, k : k + LANES] * scores for k in range(0, rank, LANES)]
-    scaled = jnp.concatenate(scaled, axis=1).astype(BF16)
-    sums = []
-    for k in range(0, width, LANES):
+        here, weight = both[at : at + rows, :], scores[at : at + rows, :]
+        low = dot(here, half)
+        scaled.append(
+            jnp.concatenate(
+                [low[:, k : k + LANES] * weight for k in range(0, rank, LANES)], axis=1
+            ).astype(BF16)
+        )
         sums.append(
-            jnp.sum(both[:, k : k + LANES].astype(F32) * scores, axis=0, keepdims=True)
+            jnp.concatenate(
+                [
+                    jnp.sum(here[:, k : k + LANES].astype(F32) * weight, axis=0, keepdims=True)
+                    for k in range(0, width, LANES)
+                ],
+                axis=1,
+            )
         )
-    sums = jnp.concatenate(sums, axis=1)
-    lay_out(dot(both[...], scaled, TN), sums, base_ref, lambda part: 0.0)
+    grad = dot(both[...], jnp.concatenate(scaled, axis=0), TN)
+    lay_out(grad, sums[0] + sums[1], base_ref, lambda part: 0.0)
 
 
 def pick_kernel(wait, slots_ref, after_any, out_ref, wide):
@@ -200,41 +190,20 @@
     return pack[:, at : at + 1].astype(F32) + pack[:, at + 1 : at + 2].astype(F32)
 
 
-def merge_kernel(
-    wait, own_ref, other_ref, user_ref, next_ref, w_ref, user_half_ref, base_any, u_any, v_any,
-    out_ref, base_ref, u_ref, v_ref, both_ref, sems,
-):
-    req, width = user_ref.shape
-    factors = get_factor(u_any, v_any, u_ref, v_ref, sems.at[0])
-    get_base = pltpu.make_async_copy(base_any, base_ref, sems.at[1])
-    get_base.start()
+def merge_kernel(wait, own_ref, other_ref, users_ref, half_ref, user_half_ref, base_ref, out_ref):
+    req, width = users_ref.shape[0] // 2, users_ref.shape[1]
     own, other = own_ref[...], other_ref[...]
     sums = jnp.concatenate([own[:, :width], other[:, :width]], axis=0)
     total = jnp.concatenate([total_of(own, width, req), total_of(other, width, req)], axis=0)
-    wait(2, 3, 4, 5)
-    users = jnp.concatenate([user_ref[...], next_ref[...]], axis=0)
-    core = my_core()
-
-    @pl.when(core == 0)
-    def _():
-        factors[0].wait()
-        both_ref[...] = dot(sums, u_ref[...])
-
-    @pl.when(core == 1)
-    def _():
-        weighted = (sums.astype(F32) * row_of(w_ref)).astype(BF16)
-        factors[1].wait()
-        both_ref[...] = dot(weighted, v_ref[...], NT)
-
-    user_half = user_half_ref[...]
-    both = both_ref[...] + total * user_half
+    users, user_half = users_ref[...], user_half_ref[...]
+    both = dot(sums, half_ref[...]) + total * user_half
     grad = dot(
         jnp.concatenate([sums, users], axis=0),
         jnp.concatenate([user_half, both], axis=0).astype(BF16),
         TN,
     )
+    wait(5)
     user_sums = jnp.sum(total * users.astype(F32), axis=0, keepdims=True)
-    get_base.wait()
     lay_out(grad, user_sums, out_ref, lambda part: base_ref[:, :, part].astype(F32))
 
 
@@ -383,22 +352,21 @@
     arrived = lax.all_to_all(slots, "dp", split_axis=0, concat_axis=0, tiled=True)
     swapped_feat = lax.ppermute(feat, "replica", pairs)
     swapped = lax.ppermute(pack, "replica", pairs)
-    factor_buffers = [pltpu.VMEM((width, rank), BF16), pltpu.VMEM((rank, width), BF16)]
     parts_shape = (peers, 8, 4 * rank + LANES)
-    base, user_half, other_user = call(
+    base, half, user_half, users = call(
         main_kernel,
         (
             shape(parts_shape, BF16),
+            shape((width, rank), BF16),
             shape((2 * req, rank), F32),
-            shape((req, width), BF16),
+            shape((2 * req, width), BF16),
         ),
         feat, swapped_feat, grad_score, user, swapped, w_out, u_weight, v_weight,
         places="pahhnhpp",
-        out_places="hhh",
+        out_places="h",
         scratch=[
             pltpu.VMEM((2 * rows, width), BF16),
-            pltpu.VMEM((2 * rows, rank), F32),
-            *factor_buffers,
+            pltpu.VMEM((rank, width), BF16),
             pltpu.SemaphoreType.DMA((3,)),
         ],
         cost=pl.CostEstimate(flops=1, bytes_accessed=1, transcendentals=0),
@@ -407,21 +375,15 @@
         pick_kernel,
         shape((req, width + LANES), BF16),
         arrived, user_half,
-        places="-p",
+        places="-a",
         scratch=[pltpu.VMEM(message, F32)],
     )
     other = lax.ppermute(own, "replica", pairs)
     parts = call(
         merge_kernel,
         shape(parts_shape, BF16),
-        own, other, user, other_user, w_out, user_half, base, u_weight, v_weight,
-        places="--hhhhppp",
-        scratch=[
-            pltpu.VMEM(parts_shape, BF16),
-            *factor_buffers,
-            pltpu.VMEM((2 * req, rank), F32),
-            pltpu.SemaphoreType.DMA((2,)),
-        ],
+        own, other, users, half, user_half, base,
+        places="-----h",
     )
     received = lax.all_to_all(parts, "dp", split_axis=0, concat_axis=0, tiled=True)
     user_grad, tail = call(

time: 112 us -> 112 us (level)
  no operation moved by 1% of the time
where the time goes in v6:
time: 112 us; the launch traced here: 111 us
  starting transfers between devices  41.5 us (37%)
  blocking collectives  35.8 us (32%)
  waiting for transfers between devices  16.7 us (15%)
  Pallas kernels  16.4 us (15%)
    all_to_all x1, blocking collectives, per_device(): lax.all_to_all(parts, 'dp', split_axis=0, concat_axis=0, tiled=True)  35.8 us
    pallas_call x7, Pallas kernels, call(): pl.pallas_call(body, out_shape=pinned if several else pinned[0], in_specs...  16.4 us
    ppermute x1, starting transfers between devices, per_device(): swapped_feat = lax.ppermute(feat, 'replica', pairs)  16.1 us
    all_to_all x1, starting transfers between devices, per_device(): lax.all_to_all(copies, 'replica', split_axis=0, concat_axis=0, tiled=True)  15.4 us
    all_to_all x1, waiting for transfers between devices, per_device(): lax.all_to_all(copies, 'replica', split_axis=0, concat_axis=0, tiled=True)  8.7 us
    all_to_all x1, waiting for transfers between devices, per_device(): lax.all_to_all(slots, 'dp', split_axis=0, concat_axis=0, tiled=True)  5.83 us
    all_to_all x1, starting transfers between devices, per_device(): lax.all_to_all(slots, 'dp', split_axis=0, concat_axis=0, tiled=True)  4.63 us
    ppermute x1, starting transfers between devices, per_device(): other = lax.ppermute(own, 'replica', pairs)  3.48 us
  transfers between devices with their start and end apart: 5, of which 4 were waited for; matrix products, arithmetic and copies ran while one was open for 0% of the time, Pallas kernels for 10%

profile of v6, /device:TPU:1, one launch (start us, length us, event | category | flops | bytes accessed | tf_op | source)
XLA Modules:
  0.0 111.2 jit_solution(1805733784056827438)
XLA Ops:
  0.6 16.1 %collective-permute-start = (bf16[256,2048]{1,0:T(8,128)(2,1)}, bf16[256,2048]{1,0:T(8,128)(2,1)S(1)}, u32[]{:S(2)}, u32[]{:S(2)}) collective-permute-start(bf16[256,2048]{1,0:T(8,128)(2,1)} %bitcast.8), channel_id=1, source_target_pairs={{0,1},{1,0},{2,3},{3,2},{4,5},{5,4},{6,7},{7,6},{8,9},{9,8},{10,11... | collective-permute-start | bytes 3145736 | tf_op jit(solution)/shard_map/ppermute | solution.py:353
  16.7 2.6 %shard_map.128 = (bf16[64,2,1152]{2,1,0:T(2,128)(2,1)}, bf16[32,2048]{1,0:T(8,128)(2,1)S(1)}) custom-call(s32[1,16]{1,0:T(1,128)} %refs_0_.1, s32[1,256]{1,0:T(1,128)} %bitcast.17, f32[1,256]{1,0:T(1,128)} %refs_2_.4, bf16[16,2048]{1,0:T(8,128)(2,1)} %bitcast.11, bf16[256,2048]{1,0:T(8,128)(2,1)} %bitcast.9), custom_call_target="tpu_custom_call" | custom-call | tf_op jit(solution)/shard_map/pallas_call | solution.py:316
  19.3 4.6 %all-to-all-start = ((bf16[64,2,1152]{2,1,0:T(2,128)(2,1)}), bf16[64,2,1152]{2,1,0:T(2,128)(2,1)S(1)}, u32[]{:S(2)}, u32[]{:S(2)}) async-start(bf16[64,2,1152]{2,1,0:T(2,128)(2,1)} %get-tuple-element.17), calls=%async_computation | async-start | bytes 589824 | tf_op jit(solution)/shard_map/all_to_all | solution.py:352
  23.9 1.9 %collective-permute-start.1 = (bf16[32,2048]{1,0:T(8,128)(2,1)S(1)}, bf16[32,2048]{1,0:T(8,128)(2,1)S(1)}, u32[]{:S(2)}, u32[]{:S(2)}) collective-permute-start(bf16[32,2048]{1,0:T(8,128)(2,1)S(1)} %get-tuple-element.18), channel_id=1, source_target_pairs={{0,1},{1,0},{2,3},{3,2},{4,5},{5,4},{6,7},{7,6},{8,9},{9,8},{10,11... | collective-permute-start | bytes 393224 | tf_op jit(solution)/shard_map/ppermute | solution.py:354
  25.9 1.3 %collective-permute-done.1.refs_4_ = bf16[32,2048]{1,0:T(8,128)(2,1)S(1)} collective-permute-done((bf16[32,2048]{1,0:T(8,128)(2,1)S(1)}, bf16[32,2048]{1,0:T(8,128)(2,1)S(1)}, u32[]{:S(2)}, u32[]{:S(2)}) %collective-permute-start.1) | collective-permute-done | bytes 131104 | tf_op jit(solution)/shard_map/ppermute | solution.py:354
  27.2 0.0 collective-permute-done.refs_1_
  27.2 5.3 %shard_map.129 = (bf16[64,8,1152]{2,1,0:T(8,128)(2,1)}, bf16[2048,256]{1,0:T(8,128)(2,1)S(1)}, f32[32,256]{1,0:T(8,128)S(1)}, bf16[32,2048]{1,0:T(8,128)(2,1)S(1)}) custom-call(bf16[256,2048]{1,0:T(8,128)(2,1)} %bitcast.10, bf16[256,2048]{1,0:T(8,128)(2,1)S(1)} %collective-permute-done.refs_1_, f32[1,256]{1,0:T(1,128)} %refs_2_.4, ...), custom_call_target="tpu_custom_call" | custom-call | flops 1 | bytes 1 | tf_op jit(solution)/shard_map/pallas_call | solution.py:316
  32.5 5.8 %all-to-all-done.refs_0_ = bf16[64,2,1152]{2,1,0:T(2,128)(2,1)S(1)} async-done(((bf16[64,2,1152]{2,1,0:T(2,128)(2,1)}), bf16[64,2,1152]{2,1,0:T(2,128)(2,1)S(1)}, u32[]{:S(2)}, u32[]{:S(2)}) %all-to-all-start) | async-done | bytes 294944 | tf_op jit(solution)/shard_map/all_to_all | solution.py:352
  38.3 0.7 shard_map.130.refs_0_
  39.0 3.5 %collective-permute-start.2 = (bf16[16,2176]{1,0:T(8,128)(2,1)S(1)}, bf16[16,2176]{1,0:T(8,128)(2,1)S(1)}, u32[]{:S(2)}, u32[]{:S(2)}) collective-permute-start(bf16[16,2176]{1,0:T(8,128)(2,1)S(1)} %shard_map.130.refs_0_), channel_id=1, source_target_pairs={{0,1},{1,0},{2,3},{3,2},{4,5},{5,4},{6,7},{7,6},{8,9},{9,8},{10,11... | collective-permute-start | bytes 208904 | tf_op jit(solution)/shard_map/ppermute | solution.py:381
  42.5 0.9 collective-permute-done.2.refs_1_
  43.4 2.3 %shard_map.132 = bf16[64,8,1152]{2,1,0:T(8,128)(2,1)S(1)} custom-call(bf16[16,2176]{1,0:T(8,128)(2,1)S(1)} %shard_map.130.refs_0_, bf16[16,2176]{1,0:T(8,128)(2,1)S(1)} %collective-permute-done.2.refs_1_, bf16[32,2048]{1,0:T(8,128)(2,1)S(1)} %get-tuple-element.21.refs_2_, bf16[2048,256]{1,0:T(8,128)(2,1)S(1)} %get-tuple-element.22.refs_3_, ...), custom_call_target="tpu_custom_call" | custom-call | tf_op jit(solution)/shard_map/pallas_call | solution.py:316
  45.8 35.8 %all_to_all.15.refs_0_ = bf16[64,8,1152]{2,1,0:T(8,128)(2,1)S(1)} all-to-all(bf16[64,8,1152]{2,1,0:T(8,128)(2,1)S(1)} %shard_map.132), channel_id=1, replica_groups=mesh['dp'=64,'replica'=16] {'dp'}, dimensions={0} | all-to-all | bytes 2359296 | tf_op jit(solution)/shard_map/all_to_all | solution.py:388
  81.6 0.9 shard_map.133
  82.5 15.4 %all-to-all-start.2 = ((bf16[16,8,1152]{2,1,0:T(8,128)(2,1)}), bf16[16,8,1152]{2,1,0:T(8,128)(2,1)S(1)}, u32[]{:S(2)}, u32[]{:S(2)}) async-start(bf16[16,8,1152]{2,1,0:T(8,128)(2,1)} %shard_map.133), calls=%async_computation.2 | async-start | bytes 589824 | tf_op jit(solution)/shard_map/all_to_all | solution.py:396
  97.9 3.7 %shard_map.131 = (f32[16,2048]{1,0:T(8,128)}, f32[32,384]{1,0:T(8,128)S(1)}) custom-call(bf16[16,2176]{1,0:T(8,128)(2,1)S(1)} %shard_map.130.refs_0_, bf16[16,2048]{1,0:T(8,128)(2,1)} %bitcast.13, bf16[2048,256]{1,0:T(8,128)(2,1)} %refs_2_.5, bf16[256,2048]{1,0:T(8,128)(2,1)} %refs_3_.1, f32[1,2048]{1,0:T(1,128)} %bitcast.16, bf16[16,128]{1,0:T(8,128)(2,1)} %bitcast.15), custom_call_target="tpu_custom_call" | custom-call | tf_op jit(solution)/shard_map/pallas_call | solution.py:316
  101.6 8.7 %all-to-all-done.2.refs_0_ = bf16[16,8,1152]{2,1,0:T(8,128)(2,1)S(1)} async-done(((bf16[16,8,1152]{2,1,0:T(8,128)(2,1)}), bf16[16,8,1152]{2,1,0:T(8,128)(2,1)S(1)}, u32[]{:S(2)}, u32[]{:S(2)}) %all-to-all-start.2) | async-done | bytes 294944 | tf_op jit(solution)/shard_map/all_to_all | solution.py:396
  110.3 0.9 shard_map.134
Async XLA Ops:
  0.6 26.5 %collective-permute-start = (bf16[256,2048]{1,0:T(8,128)(2,1)}, bf16[256,2048]{1,0:T(8,128)(2,1)S(1)}, u32[]{:S(2)}, u32[]{:S(2)}) collective-permute-start(bf16[256,2048]{1,0:T(8,128)(2,1)} %bitcast.8), channel_id=1, source_target_pairs={{0,1},{1,0},{2,3},{3,2},{4,5},{5,4},{6,7},{7,6},{8,9},{9,8},{10,11... | collective-permute-start | bytes 3145736 | tf_op jit(solution)/shard_map/ppermute | solution.py:353
  19.3 19.0 %all-to-all-start = ((bf16[64,2,1152]{2,1,0:T(2,128)(2,1)}), bf16[64,2,1152]{2,1,0:T(2,128)(2,1)S(1)}, u32[]{:S(2)}, u32[]{:S(2)}) async-start(bf16[64,2,1152]{2,1,0:T(2,128)(2,1)} %get-tuple-element.17), calls=%async_computation | async-start | bytes 589824 | tf_op jit(solution)/shard_map/all_to_all | solution.py:352
  23.9 3.2 %collective-permute-start.1 = (bf16[32,2048]{1,0:T(8,128)(2,1)S(1)}, bf16[32,2048]{1,0:T(8,128)(2,1)S(1)}, u32[]{:S(2)}, u32[]{:S(2)}) collective-permute-start(bf16[32,2048]{1,0:T(8,128)(2,1)S(1)} %get-tuple-element.18), channel_id=1, source_target_pairs={{0,1},{1,0},{2,3},{3,2},{4,5},{5,4},{6,7},{7,6},{8,9},{9,8},{10,11... | collective-permute-start | bytes 393224 | tf_op jit(solution)/shard_map/ppermute | solution.py:354
  39.0 4.4 %collective-permute-start.2 = (bf16[16,2176]{1,0:T(8,128)(2,1)S(1)}, bf16[16,2176]{1,0:T(8,128)(2,1)S(1)}, u32[]{:S(2)}, u32[]{:S(2)}) collective-permute-start(bf16[16,2176]{1,0:T(8,128)(2,1)S(1)} %shard_map.130.refs_0_), channel_id=1, source_target_pairs={{0,1},{1,0},{2,3},{3,2},{4,5},{5,4},{6,7},{7,6},{8,9},{9,8},{10,11... | collective-permute-start | bytes 208904 | tf_op jit(solution)/shard_map/ppermute | solution.py:381
  82.5 27.8 %all-to-all-start.2 = ((bf16[16,8,1152]{2,1,0:T(8,128)(2,1)}), bf16[16,8,1152]{2,1,0:T(8,128)(2,1)S(1)}, u32[]{:S(2)}, u32[]{:S(2)}) async-start(bf16[16,8,1152]{2,1,0:T(8,128)(2,1)} %shard_map.133), calls=%async_computation.2 | async-start | bytes 589824 | tf_op jit(solution)/shard_map/all_to_all | solution.py:396

commit v7 on v6

--- a/solution.py
+++ b/solution.py
@@ -12,6 +12,7 @@
 BF16 = jnp.bfloat16
 LANES = 128
 PIECES = 2
+TURN = 36 / 64
 NT = (((1,), (1,)), ((), ()))
 TN = (((0,), (0,)), ((), ()))
 
@@ -51,7 +52,8 @@
     owner = lax.div(wanted, jnp.int32(req))
     local = wanted - owner * req
     scores = score_ref[...]
-    to_owner = (iota((peers, req), 0) == owner).astype(BF16)
+    turn = round(TURN * peers)
+    to_owner = (iota((peers, req), 0) == lax.rem(owner + (peers - turn), peers)).astype(BF16)
     place = (iota((LANES, req), 0) == local).astype(BF16)
     mine = iota((req, rows), 0) == seg_ref[...]
     total_high, total_low = split_in_two(
@@ -88,7 +90,10 @@
 def lay_out(grad, sums, out_ref, base):
     peers, rank = out_ref.shape[0], grad.shape[1]
     part = grad.shape[0] // peers
+    turn = round(TURN * peers)
+    order = [(j + turn) % peers for j in range(peers)]
     blocks = grad.reshape(peers, 4, 8, rank)
+    blocks = jnp.concatenate([blocks[turn:], blocks[:turn]], axis=0)
     for q in range(4):
         out_ref[:, :, q * rank : (q + 1) * rank] = (
             blocks[:, q] + base(slice(q * rank, (q + 1) * rank))
@@ -98,7 +103,7 @@
         jnp.concatenate([sums[:, k * part :], sums[:, : k * part]], axis=1) for k in range(1, each)
     ]
     lines = [
-        turned[j % each][:, j // each * LANES : (j // each + 1) * LANES] for j in range(peers)
+        turned[j % each][:, j // each * LANES : (j // each + 1) * LANES] for j in order
     ]
     lines = jnp.concatenate([jnp.broadcast_to(line, (8, LANES)) for line in lines], axis=0)
     out_ref[:, :, 4 * rank :] = (
@@ -337,6 +342,9 @@
     shape = jax.ShapeDtypeStruct
     bias, w_out = bias[None], w_out.reshape(width // LANES, LANES)
     pairs = [(i, i ^ 1) for i in range(replicas)]
+    turn = round(TURN * peers)
+    plane = [[(j + turn) % peers for j in range(peers)]]
+    column = [[(j + replicas - 2) % replicas for j in range(replicas)]]
     message = (peers, PIECES, piece + LANES)
     slots, pack = call(
         request_kernel,
@@ -349,7 +357,9 @@
             pltpu.SemaphoreType.DMA((PIECES,)),
         ],
     )
-    arrived = lax.all_to_all(slots, "dp", split_axis=0, concat_axis=0, tiled=True)
+    arrived = lax.all_to_all(
+        slots, "dp", split_axis=0, concat_axis=0, tiled=True, axis_index_groups=plane
+    )
     swapped_feat = lax.ppermute(feat, "replica", pairs)
     swapped = lax.ppermute(pack, "replica", pairs)
     parts_shape = (peers, 8, 4 * rank + LANES)
@@ -385,7 +395,9 @@
         own, other, users, half, user_half, base,
         places="-----h",
     )
-    received = lax.all_to_all(parts, "dp", split_axis=0, concat_axis=0, tiled=True)
+    received = lax.all_to_all(
+        parts, "dp", split_axis=0, concat_axis=0, tiled=True, axis_index_groups=plane
+    )
     user_grad, tail = call(
         user_grad_kernel,
         (shape((req, width), F32), shape((part, rank + LANES), F32)),
@@ -393,7 +405,9 @@
         places="-hhhhh",
     )
     copies = call(sum_kernel, shape((replicas, 8, 4 * rank + LANES), BF16), received)
-    gathered = lax.all_to_all(copies, "replica", split_axis=0, concat_axis=0, tiled=True)
+    gathered = lax.all_to_all(
+        copies, "replica", split_axis=0, concat_axis=0, tiled=True, axis_index_groups=column
+    )
     factor = 1.0 / math.sqrt(rows * peers * replicas)
     grad_u, grad_vt, grad_bias, grad_out = call(
         functools.partial(last_kernel, factor),

time: 112 us -> 107 us (0.955)
  waiting for transfers between devices: 16.7 us -> 8.4 us
  blocking collectives: 35.8 us -> 37.9 us
  starting transfers between devices: 41.5 us -> 43.1 us
    all_to_all x2, waiting for transfers between devices: 14.5 us -> 6.23 us  [the longest x1 6.23 us: per_device(): lax.all_to_all(copies, 'replica', split_axis=0, concat_axis=0, tiled=True...]
    all_to_all x2, starting transfers between devices: 20 us -> 22.6 us  [the longest x1 12.1 us: per_device(): lax.all_to_all(slots, 'dp', split_axis=0, concat_axis=0, tiled=True, axis...]
    all_to_all x1, blocking collectives: 35.8 us -> 37.9 us  [per_device(): lax.all_to_all(parts, 'dp', split_axis=0, concat_axis=0, tiled=True, axis...]
    ppermute x1, starting transfers between devices: 3.48 us -> 1.94 us  [per_device(): other = lax.ppermute(own, 'replica', pairs)]
  transfers between devices with their start and end apart: 5 -> 5, of which waited for: 4 -> 3; matrix products, arithmetic and copies ran while one was open for 0% -> 0% of each run, Pallas kernels for 10% -> 11%
where the time goes in v7:
time: 107 us
  starting transfers between devices  43.1 us (40%)
  blocking collectives  37.9 us (35%)
  Pallas kernels  16.4 us (15%)
  waiting for transfers between devices  8.4 us (8%)
    all_to_all x1, blocking collectives, per_device(): lax.all_to_all(parts, 'dp', split_axis=0, concat_axis=0, tiled=True, axis...  37.9 us
    pallas_call x7, Pallas kernels, call(): pl.pallas_call(body, out_shape=pinned if several else pinned[0], in_specs...  16.4 us
    ppermute x1, starting transfers between devices, per_device(): swapped_feat = lax.ppermute(feat, 'replica', pairs)  16.1 us
    all_to_all x1, starting transfers between devices, per_device(): lax.all_to_all(slots, 'dp', split_axis=0, concat_axis=0, tiled=True, axis...  12.1 us
    all_to_all x1, starting transfers between devices, per_device(): lax.all_to_all(copies, 'replica', split_axis=0, concat_axis=0, tiled=True...  10.5 us
    all_to_all x1, waiting for transfers between devices, per_device(): lax.all_to_all(copies, 'replica', split_axis=0, concat_axis=0, tiled=True...  6.23 us
    ppermute x1, starting transfers between devices, per_device(): swapped = lax.ppermute(pack, 'replica', pairs)  2.48 us
  transfers between devices with their start and end apart: 5, of which 3 were waited for; matrix products, arithmetic and copies ran while one was open for 0% of the time, Pallas kernels for 11%

profile of v7, /device:TPU:1, one launch (start us, length us, event | category | flops | bytes accessed | tf_op | source)
XLA Modules:
  0.0 106.6 jit_solution(15294071088877197875)
XLA Ops:
  0.6 16.1 %collective-permute-start = (bf16[256,2048]{1,0:T(8,128)(2,1)}, bf16[256,2048]{1,0:T(8,128)(2,1)S(1)}, u32[]{:S(2)}, u32[]{:S(2)}) collective-permute-start(bf16[256,2048]{1,0:T(8,128)(2,1)} %bitcast.8), channel_id=1, source_target_pairs={{0,1},{1,0},{2,3},{3,2},{4,5},{5,4},{6,7},{7,6},{8,9},{9,8},{10,11... | collective-permute-start | bytes 3145736 | tf_op jit(solution)/shard_map/ppermute | solution.py:363
  16.7 2.6 %shard_map.128 = (bf16[64,2,1152]{2,1,0:T(2,128)(2,1)}, bf16[32,2048]{1,0:T(8,128)(2,1)S(1)}) custom-call(s32[1,16]{1,0:T(1,128)} %refs_0_.1, s32[1,256]{1,0:T(1,128)} %bitcast.17, f32[1,256]{1,0:T(1,128)} %refs_2_.4, bf16[16,2048]{1,0:T(8,128)(2,1)} %bitcast.11, bf16[256,2048]{1,0:T(8,128)(2,1)} %bitcast.9), custom_call_target="tpu_custom_call" | custom-call | tf_op jit(solution)/shard_map/pallas_call | solution.py:321
  19.3 12.1 %all-to-all-start = ((bf16[64,2,1152]{2,1,0:T(2,128)(2,1)}), bf16[64,2,1152]{2,1,0:T(2,128)(2,1)S(1)}, u32[]{:S(2)}, u32[]{:S(2)}) async-start(bf16[64,2,1152]{2,1,0:T(2,128)(2,1)} %get-tuple-element.17), calls=%async_computation | async-start | bytes 589824 | tf_op jit(solution)/shard_map/all_to_all | solution.py:360
  31.4 2.5 %collective-permute-start.1 = (bf16[32,2048]{1,0:T(8,128)(2,1)S(1)}, bf16[32,2048]{1,0:T(8,128)(2,1)S(1)}, u32[]{:S(2)}, u32[]{:S(2)}) collective-permute-start(bf16[32,2048]{1,0:T(8,128)(2,1)S(1)} %get-tuple-element.18), channel_id=1, source_target_pairs={{0,1},{1,0},{2,3},{3,2},{4,5},{5,4},{6,7},{7,6},{8,9},{9,8},{10,11... | collective-permute-start | bytes 393224 | tf_op jit(solution)/shard_map/ppermute | solution.py:364
  33.9 1.0 collective-permute-done.1.refs_4_
  34.8 0.0 collective-permute-done.refs_1_
  34.8 5.3 %shard_map.129 = (bf16[64,8,1152]{2,1,0:T(8,128)(2,1)}, bf16[2048,256]{1,0:T(8,128)(2,1)S(1)}, f32[32,256]{1,0:T(8,128)S(1)}, bf16[32,2048]{1,0:T(8,128)(2,1)S(1)}) custom-call(bf16[256,2048]{1,0:T(8,128)(2,1)} %bitcast.10, bf16[256,2048]{1,0:T(8,128)(2,1)S(1)} %collective-permute-done.refs_1_, f32[1,256]{1,0:T(1,128)} %refs_2_.4, ...), custom_call_target="tpu_custom_call" | custom-call | flops 1 | bytes 1 | tf_op jit(solution)/shard_map/pallas_call | solution.py:321
  40.1 0.0 all-to-all-done.refs_0_
  40.2 0.7 shard_map.130.refs_0_
  40.9 1.9 %collective-permute-start.2 = (bf16[16,2176]{1,0:T(8,128)(2,1)S(1)}, bf16[16,2176]{1,0:T(8,128)(2,1)S(1)}, u32[]{:S(2)}, u32[]{:S(2)}) collective-permute-start(bf16[16,2176]{1,0:T(8,128)(2,1)S(1)} %shard_map.130.refs_0_), channel_id=1, source_target_pairs={{0,1},{1,0},{2,3},{3,2},{4,5},{5,4},{6,7},{7,6},{8,9},{9,8},{10,11... | collective-permute-start | bytes 208904 | tf_op jit(solution)/shard_map/ppermute | solution.py:391
  42.8 1.2 %collective-permute-done.2.refs_1_ = bf16[16,2176]{1,0:T(8,128)(2,1)S(1)} collective-permute-done((bf16[16,2176]{1,0:T(8,128)(2,1)S(1)}, bf16[16,2176]{1,0:T(8,128)(2,1)S(1)}, u32[]{:S(2)}, u32[]{:S(2)}) %collective-permute-start.2) | collective-permute-done | bytes 69664 | tf_op jit(solution)/shard_map/ppermute | solution.py:391
  44.1 2.3 %shard_map.132 = bf16[64,8,1152]{2,1,0:T(8,128)(2,1)S(1)} custom-call(bf16[16,2176]{1,0:T(8,128)(2,1)S(1)} %shard_map.130.refs_0_, bf16[16,2176]{1,0:T(8,128)(2,1)S(1)} %collective-permute-done.2.refs_1_, bf16[32,2048]{1,0:T(8,128)(2,1)S(1)} %get-tuple-element.21.refs_2_, bf16[2048,256]{1,0:T(8,128)(2,1)S(1)} %get-tuple-element.22.refs_3_, ...), custom_call_target="tpu_custom_call" | custom-call | tf_op jit(solution)/shard_map/pallas_call | solution.py:321
  46.4 37.9 %all_to_all.15.refs_0_ = bf16[64,8,1152]{2,1,0:T(8,128)(2,1)S(1)} all-to-all(bf16[64,8,1152]{2,1,0:T(8,128)(2,1)S(1)} %shard_map.132), channel_id=1, replica_groups={{576,592,608,624,640,656,672,688,704,720,736,752,768,784,800,816,832,84..., dimensions={0} | all-to-all | bytes 2359296 | tf_op jit(solution)/shard_map/all_to_all | solution.py:398
  84.3 0.9 shard_map.133
  85.2 10.5 %all-to-all-start.2 = ((bf16[16,8,1152]{2,1,0:T(8,128)(2,1)}), bf16[16,8,1152]{2,1,0:T(8,128)(2,1)S(1)}, u32[]{:S(2)}, u32[]{:S(2)}) async-start(bf16[16,8,1152]{2,1,0:T(8,128)(2,1)} %shard_map.133), calls=%async_computation.2 | async-start | bytes 589824 | tf_op jit(solution)/shard_map/all_to_all | solution.py:408
  95.7 3.7 %shard_map.131 = (f32[16,2048]{1,0:T(8,128)}, f32[32,384]{1,0:T(8,128)S(1)}) custom-call(bf16[16,2176]{1,0:T(8,128)(2,1)S(1)} %shard_map.130.refs_0_, bf16[16,2048]{1,0:T(8,128)(2,1)} %bitcast.13, bf16[2048,256]{1,0:T(8,128)(2,1)} %refs_2_.5, bf16[256,2048]{1,0:T(8,128)(2,1)} %refs_3_.1, f32[1,2048]{1,0:T(1,128)} %bitcast.16, bf16[16,128]{1,0:T(8,128)(2,1)} %bitcast.15), custom_call_target="tpu_custom_call" | custom-call | tf_op jit(solution)/shard_map/pallas_call | solution.py:321
  99.4 6.2 %all-to-all-done.2.refs_0_ = bf16[16,8,1152]{2,1,0:T(8,128)(2,1)S(1)} async-done(((bf16[16,8,1152]{2,1,0:T(8,128)(2,1)}), bf16[16,8,1152]{2,1,0:T(8,128)(2,1)S(1)}, u32[]{:S(2)}, u32[]{:S(2)}) %all-to-all-start.2) | async-done | bytes 294944 | tf_op jit(solution)/shard_map/all_to_all | solution.py:408
  105.6 0.9 shard_map.134
Async XLA Ops:
  0.6 34.2 %collective-permute-start = (bf16[256,2048]{1,0:T(8,128)(2,1)}, bf16[256,2048]{1,0:T(8,128)(2,1)S(1)}, u32[]{:S(2)}, u32[]{:S(2)}) collective-permute-start(bf16[256,2048]{1,0:T(8,128)(2,1)} %bitcast.8), channel_id=1, source_target_pairs={{0,1},{1,0},{2,3},{3,2},{4,5},{5,4},{6,7},{7,6},{8,9},{9,8},{10,11... | collective-permute-start | bytes 3145736 | tf_op jit(solution)/shard_map/ppermute | solution.py:363
  19.3 20.9 %all-to-all-start = ((bf16[64,2,1152]{2,1,0:T(2,128)(2,1)}), bf16[64,2,1152]{2,1,0:T(2,128)(2,1)S(1)}, u32[]{:S(2)}, u32[]{:S(2)}) async-start(bf16[64,2,1152]{2,1,0:T(2,128)(2,1)} %get-tuple-element.17), calls=%async_computation | async-start | bytes 589824 | tf_op jit(solution)/shard_map/all_to_all | solution.py:360
  31.4 3.5 %collective-permute-start.1 = (bf16[32,2048]{1,0:T(8,128)(2,1)S(1)}, bf16[32,2048]{1,0:T(8,128)(2,1)S(1)}, u32[]{:S(2)}, u32[]{:S(2)}) collective-permute-start(bf16[32,2048]{1,0:T(8,128)(2,1)S(1)} %get-tuple-element.18), channel_id=1, source_target_pairs={{0,1},{1,0},{2,3},{3,2},{4,5},{5,4},{6,7},{7,6},{8,9},{9,8},{10,11... | collective-permute-start | bytes 393224 | tf_op jit(solution)/shard_map/ppermute | solution.py:364
  40.9 3.1 %collective-permute-start.2 = (bf16[16,2176]{1,0:T(8,128)(2,1)S(1)}, bf16[16,2176]{1,0:T(8,128)(2,1)S(1)}, u32[]{:S(2)}, u32[]{:S(2)}) collective-permute-start(bf16[16,2176]{1,0:T(8,128)(2,1)S(1)} %shard_map.130.refs_0_), channel_id=1, source_target_pairs={{0,1},{1,0},{2,3},{3,2},{4,5},{5,4},{6,7},{7,6},{8,9},{9,8},{10,11... | collective-permute-start | bytes 208904 | tf_op jit(solution)/shard_map/ppermute | solution.py:391
  85.2 20.4 %all-to-all-start.2 = ((bf16[16,8,1152]{2,1,0:T(8,128)(2,1)}), bf16[16,8,1152]{2,1,0:T(8,128)(2,1)S(1)}, u32[]{:S(2)}, u32[]{:S(2)}) async-start(bf16[16,8,1152]{2,1,0:T(8,128)(2,1)} %shard_map.133), calls=%async_computation.2 | async-start | bytes 589824 | tf_op jit(solution)/shard_map/all_to_all | solution.py:408

commit v8 on v7

--- a/solution.py
+++ b/solution.py
@@ -87,28 +87,40 @@
     slots_ref[...] = wide[...].astype(BF16)
 
 
-def lay_out(grad, sums, out_ref, base):
+def lay_out(grad, first, out_ref, base_ref=None):
     peers, rank = out_ref.shape[0], grad.shape[1]
-    part = grad.shape[0] // peers
+    chunks = grad.shape[0] // 32
+    at = (first - round(TURN * peers)) % peers
+    blocks = grad.reshape(chunks, 4, 8, rank)
+    written, done = [], 0
+    while done < chunks:
+        count = min(chunks - done, peers - at)
+        place = slice(at, at + count)
+        for q in range(4):
+            part = slice(q * rank, (q + 1) * rank)
+            block = blocks[done : done + count, q]
+            if base_ref is not None:
+                block = block + base_ref[place, :, part].astype(F32)
+            out_ref[place, :, part] = block.astype(BF16)
+        written.append(place)
+        done, at = done + count, (at + count) % peers
+    return written
+
+
+def lay_sums(sums, out_ref):
+    peers = out_ref.shape[0]
+    part = sums.shape[1] // peers
     turn = round(TURN * peers)
-    order = [(j + turn) % peers for j in range(peers)]
-    blocks = grad.reshape(peers, 4, 8, rank)
-    blocks = jnp.concatenate([blocks[turn:], blocks[:turn]], axis=0)
-    for q in range(4):
-        out_ref[:, :, q * rank : (q + 1) * rank] = (
-            blocks[:, q] + base(slice(q * rank, (q + 1) * rank))
-        ).astype(BF16)
     each = LANES // part
     turned = [sums] + [
         jnp.concatenate([sums[:, k * part :], sums[:, : k * part]], axis=1) for k in range(1, each)
     ]
+    order = [(j + turn) % peers for j in range(peers)]
     lines = [
         turned[j % each][:, j // each * LANES : (j // each + 1) * LANES] for j in order
     ]
     lines = jnp.concatenate([jnp.broadcast_to(line, (8, LANES)) for line in lines], axis=0)
-    out_ref[:, :, 4 * rank :] = (
-        lines.reshape(peers, 8, LANES) + base(slice(4 * rank, 4 * rank + LANES))
-    ).astype(BF16)
+    out_ref[:, :, out_ref.shape[2] - LANES :] = lines.reshape(peers, 8, LANES).astype(BF16)
 
 
 def row_of(ref):
@@ -122,11 +134,12 @@
 
 def main_kernel(
     wait, feat_any, other_any, score_ref, user_ref, pack_ref, w_ref, u_any, v_any,
-    base_ref, half_ref, user_half_ref, users_ref, both, v_ref, sems,
+    base_hbm, half_ref, user_half_ref, users_ref, both, v_ref, base_ref, sems,
 ):
     rows, width = feat_any.shape
     rank = v_ref.shape[0]
     req = user_ref.shape[0]
+    peers = base_ref.shape[0]
     core = my_core()
     get_u = pltpu.make_async_copy(u_any, half_ref, sems.at[0])
     get_v = pltpu.make_async_copy(v_any, v_ref, sems.at[0])
@@ -153,28 +166,31 @@
         half_ref[...] = jnp.transpose((v_ref[...].astype(F32) * row_of(w_ref)).astype(BF16))
 
     half = half_ref[...]
-    user_half_ref[...] = dot(users_ref[...], half)
-    scaled, sums = [], []
+    scaled = []
     for at, copy in zip((0, rows), copies):
         copy.wait()
-        here, weight = both[at : at + rows, :], scores[at : at + rows, :]
-        low = dot(here, half)
+        weight = scores[at : at + rows, :]
+        low = dot(both[at : at + rows, :], half)
         scaled.append(
             jnp.concatenate(
                 [low[:, k : k + LANES] * weight for k in range(0, rank, LANES)], axis=1
             ).astype(BF16)
         )
-        sums.append(
-            jnp.concatenate(
-                [
-                    jnp.sum(here[:, k : k + LANES].astype(F32) * weight, axis=0, keepdims=True)
-                    for k in range(0, width, LANES)
-                ],
-                axis=1,
+    scaled = jnp.concatenate(scaled, axis=0)
+    ends = []
+    for k in range(2):
+        at = k * (width // 2)
+        grad = dot(both[:, at : at + width // 2], scaled, TN)
+        for place in lay_out(grad, k * (peers // 2), base_ref):
+            ends.append(
+                pltpu.make_async_copy(
+                    base_ref.at[place], base_hbm.at[place], sems.at[3 + len(ends)]
+                )
             )
-        )
-    grad = dot(both[...], jnp.concatenate(scaled, axis=0), TN)
-    lay_out(grad, sums[0] + sums[1], base_ref, lambda part: 0.0)
+            ends[-1].start()
+    user_half_ref[...] = dot(users_ref[...], half)
+    for copy in ends:
+        copy.wait()
 
 
 def pick_kernel(wait, slots_ref, after_any, out_ref, wide):
@@ -207,9 +223,11 @@
         jnp.concatenate([user_half, both], axis=0).astype(BF16),
         TN,
     )
+    lay_sums(
+        jnp.sum(sums.astype(F32) + total * users.astype(F32), axis=0, keepdims=True), out_ref
+    )
     wait(5)
-    user_sums = jnp.sum(total * users.astype(F32), axis=0, keepdims=True)
-    lay_out(grad, user_sums, out_ref, lambda part: base_ref[:, :, part].astype(F32))
+    lay_out(grad, 0, out_ref, base_ref)
 
 
 def user_grad_kernel(wait, pack_ref, user_ref, u_ref, v_ref, bias_ref, w_ref, out_ref, tail_ref):
@@ -316,7 +334,7 @@
     extra += [pltpu.SemaphoreType.DMA((len(group),)) for group in (staged, late) if group]
     out_specs = tuple(pl.BlockSpec(memory_space=spaces[place]) for place in out_places)
     pinned = tuple(
-        pltpu.HBM(x.shape, x.dtype) if place == "h" else x for x, place in zip(outs, out_places)
+        pltpu.HBM(x.shape, x.dtype) if place in "hp" else x for x, place in zip(outs, out_places)
     )
     return pl.pallas_call(
         body,
@@ -366,18 +384,19 @@
     base, half, user_half, users = call(
         main_kernel,
         (
-            shape(parts_shape, BF16),
+            shape((peers, 8, 4 * rank), BF16),
             shape((width, rank), BF16),
             shape((2 * req, rank), F32),
             shape((2 * req, width), BF16),
         ),
         feat, swapped_feat, grad_score, user, swapped, w_out, u_weight, v_weight,
         places="pahhnhpp",
-        out_places="h",
+        out_places="p",
         scratch=[
             pltpu.VMEM((2 * rows, width), BF16),
             pltpu.VMEM((rank, width), BF16),
-            pltpu.SemaphoreType.DMA((3,)),
+            pltpu.VMEM((peers, 8, 4 * rank), BF16),
+            pltpu.SemaphoreType.DMA((6,)),
         ],
         cost=pl.CostEstimate(flops=1, bytes_accessed=1, transcendentals=0),
     )

time: 107 us -> 106 us (level)
  Pallas kernels: 16.4 us -> 15 us
    pallas_call x7, Pallas kernels: 16.4 us -> 15 us  [call(): pl.pallas_call(body, out_shape=pinned if several else pinned[0], in_specs...]
  transfers between devices with their start and end apart: 5 -> 5, of which waited for: 3 -> 3; matrix products, arithmetic and copies ran while one was open for 0% -> 0% of each run, Pallas kernels for 11% -> 10%
where the time goes in v8:
time: 106 us; the launch traced here: 105 us
  starting transfers between devices  43.8 us (41%)
  blocking collectives  37.4 us (35%)
  Pallas kernels  15 us (14%)
  waiting for transfers between devices  8.15 us (8%)
    all_to_all x1, blocking collectives, per_device(): lax.all_to_all(parts, 'dp', split_axis=0, concat_axis=0, tiled=True, axis...  37.4 us
    ppermute x1, starting transfers between devices, per_device(): swapped_feat = lax.ppermute(feat, 'replica', pairs)  16.1 us
    pallas_call x7, Pallas kernels, call(): pl.pallas_call(body, out_shape=pinned if several else pinned[0], in_specs...  15 us
    all_to_all x1, starting transfers between devices, per_device(): lax.all_to_all(slots, 'dp', split_axis=0, concat_axis=0, tiled=True, axis...  12.1 us
    all_to_all x1, starting transfers between devices, per_device(): lax.all_to_all(copies, 'replica', split_axis=0, concat_axis=0, tiled=True...  11 us
    all_to_all x1, waiting for transfers between devices, per_device(): lax.all_to_all(copies, 'replica', split_axis=0, concat_axis=0, tiled=True...  6.23 us
    ppermute x1, starting transfers between devices, per_device(): swapped = lax.ppermute(pack, 'replica', pairs)  2.48 us
    ppermute x1, starting transfers between devices, per_device(): other = lax.ppermute(own, 'replica', pairs)  2.19 us
  transfers between devices with their start and end apart: 5, of which 3 were waited for; matrix products, arithmetic and copies ran while one was open for 0% of the time, Pallas kernels for 10%

profile of v8, /device:TPU:1, one launch (start us, length us, event | category | flops | bytes accessed | tf_op | source)
XLA Modules:
  0.0 105.1 jit_solution(8265337041216653802)
XLA Ops:
  0.6 16.1 %collective-permute-start = (bf16[256,2048]{1,0:T(8,128)(2,1)}, bf16[256,2048]{1,0:T(8,128)(2,1)S(1)}, u32[]{:S(2)}, u32[]{:S(2)}) collective-permute-start(bf16[256,2048]{1,0:T(8,128)(2,1)} %bitcast.8), channel_id=1, source_target_pairs={{0,1},{1,0},{2,3},{3,2},{4,5},{5,4},{6,7},{7,6},{8,9},{9,8},{10,11... | collective-permute-start | bytes 3145736 | tf_op jit(solution)/shard_map/ppermute | solution.py:381
  16.7 2.6 %shard_map.128 = (bf16[64,2,1152]{2,1,0:T(2,128)(2,1)}, bf16[32,2048]{1,0:T(8,128)(2,1)S(1)}) custom-call(s32[1,16]{1,0:T(1,128)} %refs_0_.1, s32[1,256]{1,0:T(1,128)} %bitcast.17, f32[1,256]{1,0:T(1,128)} %refs_2_.4, bf16[16,2048]{1,0:T(8,128)(2,1)} %bitcast.11, bf16[256,2048]{1,0:T(8,128)(2,1)} %bitcast.9), custom_call_target="tpu_custom_call" | custom-call | tf_op jit(solution)/shard_map/pallas_call | solution.py:339
  19.3 12.1 %all-to-all-start = ((bf16[64,2,1152]{2,1,0:T(2,128)(2,1)}), bf16[64,2,1152]{2,1,0:T(2,128)(2,1)S(1)}, u32[]{:S(2)}, u32[]{:S(2)}) async-start(bf16[64,2,1152]{2,1,0:T(2,128)(2,1)} %get-tuple-element.17), calls=%async_computation | async-start | bytes 589824 | tf_op jit(solution)/shard_map/all_to_all | solution.py:378
  31.4 2.5 %collective-permute-start.1 = (bf16[32,2048]{1,0:T(8,128)(2,1)S(1)}, bf16[32,2048]{1,0:T(8,128)(2,1)S(1)}, u32[]{:S(2)}, u32[]{:S(2)}) collective-permute-start(bf16[32,2048]{1,0:T(8,128)(2,1)S(1)} %get-tuple-element.18), channel_id=1, source_target_pairs={{0,1},{1,0},{2,3},{3,2},{4,5},{5,4},{6,7},{7,6},{8,9},{9,8},{10,11... | collective-permute-start | bytes 393224 | tf_op jit(solution)/shard_map/ppermute | solution.py:382
  33.9 1.0 collective-permute-done.1.refs_4_
  34.9 0.0 collective-permute-done.refs_1_
  34.9 4.8 %shard_map.129 = (bf16[64,8,1024]{2,1,0:T(8,128)(2,1)}, bf16[2048,256]{1,0:T(8,128)(2,1)S(1)}, f32[32,256]{1,0:T(8,128)S(1)}, bf16[32,2048]{1,0:T(8,128)(2,1)S(1)}) custom-call(bf16[256,2048]{1,0:T(8,128)(2,1)} %bitcast.10, bf16[256,2048]{1,0:T(8,128)(2,1)S(1)} %collective-permute-done.refs_1_, f32[1,256]{1,0:T(1,128)} %refs_2_.4, ...), custom_call_target="tpu_custom_call" | custom-call | flops 1 | bytes 1 | tf_op jit(solution)/shard_map/pallas_call | solution.py:339
  39.6 0.0 all-to-all-done.refs_0_
  39.6 0.7 shard_map.130.refs_0_
  40.4 2.2 %collective-permute-start.2 = (bf16[16,2176]{1,0:T(8,128)(2,1)S(1)}, bf16[16,2176]{1,0:T(8,128)(2,1)S(1)}, u32[]{:S(2)}, u32[]{:S(2)}) collective-permute-start(bf16[16,2176]{1,0:T(8,128)(2,1)S(1)} %shard_map.130.refs_0_), channel_id=1, source_target_pairs={{0,1},{1,0},{2,3},{3,2},{4,5},{5,4},{6,7},{7,6},{8,9},{9,8},{10,11... | collective-permute-start | bytes 208904 | tf_op jit(solution)/shard_map/ppermute | solution.py:410
  42.6 1.0 collective-permute-done.2.refs_1_
  43.5 1.4 %shard_map.132 = bf16[64,8,1152]{2,1,0:T(8,128)(2,1)S(1)} custom-call(bf16[16,2176]{1,0:T(8,128)(2,1)S(1)} %shard_map.130.refs_0_, bf16[16,2176]{1,0:T(8,128)(2,1)S(1)} %collective-permute-done.2.refs_1_, bf16[32,2048]{1,0:T(8,128)(2,1)S(1)} %get-tuple-element.21.refs_2_, bf16[2048,256]{1,0:T(8,128)(2,1)S(1)} %get-tuple-element.22.refs_3_, ...), custom_call_target="tpu_custom_call" | custom-call | tf_op jit(solution)/shard_map/pallas_call | solution.py:339
  45.0 37.4 %all_to_all.15.refs_0_ = bf16[64,8,1152]{2,1,0:T(8,128)(2,1)S(1)} all-to-all(bf16[64,8,1152]{2,1,0:T(8,128)(2,1)S(1)} %shard_map.132), channel_id=1, replica_groups={{576,592,608,624,640,656,672,688,704,720,736,752,768,784,800,816,832,84..., dimensions={0} | all-to-all | bytes 2359296 | tf_op jit(solution)/shard_map/all_to_all | solution.py:417
  82.4 0.9 shard_map.133
  83.3 11.0 %all-to-all-start.2 = ((bf16[16,8,1152]{2,1,0:T(8,128)(2,1)}), bf16[16,8,1152]{2,1,0:T(8,128)(2,1)S(1)}, u32[]{:S(2)}, u32[]{:S(2)}) async-start(bf16[16,8,1152]{2,1,0:T(8,128)(2,1)} %shard_map.133), calls=%async_computation.2 | async-start | bytes 589824 | tf_op jit(solution)/shard_map/all_to_all | solution.py:427
  94.3 3.7 %shard_map.131 = (f32[16,2048]{1,0:T(8,128)}, f32[32,384]{1,0:T(8,128)S(1)}) custom-call(bf16[16,2176]{1,0:T(8,128)(2,1)S(1)} %shard_map.130.refs_0_, bf16[16,2048]{1,0:T(8,128)(2,1)} %bitcast.13, bf16[2048,256]{1,0:T(8,128)(2,1)} %refs_2_.5, bf16[256,2048]{1,0:T(8,128)(2,1)} %refs_3_.1, f32[1,2048]{1,0:T(1,128)} %bitcast.16, bf16[16,128]{1,0:T(8,128)(2,1)} %bitcast.15), custom_call_target="tpu_custom_call" | custom-call | tf_op jit(solution)/shard_map/pallas_call | solution.py:339
  97.9 6.2 %all-to-all-done.2.refs_0_ = bf16[16,8,1152]{2,1,0:T(8,128)(2,1)S(1)} async-done(((bf16[16,8,1152]{2,1,0:T(8,128)(2,1)}), bf16[16,8,1152]{2,1,0:T(8,128)(2,1)S(1)}, u32[]{:S(2)}, u32[]{:S(2)}) %all-to-all-start.2) | async-done | bytes 294944 | tf_op jit(solution)/shard_map/all_to_all | solution.py:427
  104.2 0.9 shard_map.134
Async XLA Ops:
  0.6 34.2 %collective-permute-start = (bf16[256,2048]{1,0:T(8,128)(2,1)}, bf16[256,2048]{1,0:T(8,128)(2,1)S(1)}, u32[]{:S(2)}, u32[]{:S(2)}) collective-permute-start(bf16[256,2048]{1,0:T(8,128)(2,1)} %bitcast.8), channel_id=1, source_target_pairs={{0,1},{1,0},{2,3},{3,2},{4,5},{5,4},{6,7},{7,6},{8,9},{9,8},{10,11... | collective-permute-start | bytes 3145736 | tf_op jit(solution)/shard_map/ppermute | solution.py:381
  19.3 20.3 %all-to-all-start = ((bf16[64,2,1152]{2,1,0:T(2,128)(2,1)}), bf16[64,2,1152]{2,1,0:T(2,128)(2,1)S(1)}, u32[]{:S(2)}, u32[]{:S(2)}) async-start(bf16[64,2,1152]{2,1,0:T(2,128)(2,1)} %get-tuple-element.17), calls=%async_computation | async-start | bytes 589824 | tf_op jit(solution)/shard_map/all_to_all | solution.py:378
  31.4 3.5 %collective-permute-start.1 = (bf16[32,2048]{1,0:T(8,128)(2,1)S(1)}, bf16[32,2048]{1,0:T(8,128)(2,1)S(1)}, u32[]{:S(2)}, u32[]{:S(2)}) collective-permute-start(bf16[32,2048]{1,0:T(8,128)(2,1)S(1)} %get-tuple-element.18), channel_id=1, source_target_pairs={{0,1},{1,0},{2,3},{3,2},{4,5},{5,4},{6,7},{7,6},{8,9},{9,8},{10,11... | collective-permute-start | bytes 393224 | tf_op jit(solution)/shard_map/ppermute | solution.py:382
  40.4 3.1 %collective-permute-start.2 = (bf16[16,2176]{1,0:T(8,128)(2,1)S(1)}, bf16[16,2176]{1,0:T(8,128)(2,1)S(1)}, u32[]{:S(2)}, u32[]{:S(2)}) collective-permute-start(bf16[16,2176]{1,0:T(8,128)(2,1)S(1)} %shard_map.130.refs_0_), channel_id=1, source_target_pairs={{0,1},{1,0},{2,3},{3,2},{4,5},{5,4},{6,7},{7,6},{8,9},{9,8},{10,11... | collective-permute-start | bytes 208904 | tf_op jit(solution)/shard_map/ppermute | solution.py:410
  83.3 20.9 %all-to-all-start.2 = ((bf16[16,8,1152]{2,1,0:T(8,128)(2,1)}), bf16[16,8,1152]{2,1,0:T(8,128)(2,1)S(1)}, u32[]{:S(2)}, u32[]{:S(2)}) async-start(bf16[16,8,1152]{2,1,0:T(8,128)(2,1)} %shard_map.133), calls=%async_computation.2 | async-start | bytes 589824 | tf_op jit(solution)/shard_map/all_to_all | solution.py:427

commit v9 on v8

--- a/solution.py
+++ b/solution.py
@@ -49,11 +49,13 @@
         copy.start()
     wait(0, 1, 2)
     wanted = wanted_ref[...]
-    owner = lax.div(wanted, jnp.int32(req))
-    local = wanted - owner * req
+    assert req & (req - 1) == 0
+    local = wanted & (req - 1)
     scores = score_ref[...]
     turn = round(TURN * peers)
-    to_owner = (iota((peers, req), 0) == lax.rem(owner + (peers - turn), peers)).astype(BF16)
+    line = iota((peers, req), 0)
+    first = jnp.where(line < peers - turn, line + turn, line + (turn - peers)) * req
+    to_owner = (wanted - local == first).astype(BF16)
     place = (iota((LANES, req), 0) == local).astype(BF16)
     mine = iota((req, rows), 0) == seg_ref[...]
     total_high, total_low = split_in_two(
@@ -266,7 +268,8 @@
     part, rank = grad_u_ref.shape
     replicas = in_ref.shape[0]
     sums = [
-        sum(in_ref[k].astype(F32) for k in range(core, replicas, 2)) * factor for core in (0, 1)
+        sum(in_ref[k].astype(F32) for k in range(1 - core, replicas, 2)) * factor
+        for core in (0, 1)
     ]
     low, grad_low = (
         jnp.concatenate([s[:, q * rank : (q + 1) * rank] for q in range(4)], axis=0) for s in sums
@@ -362,7 +365,7 @@
     pairs = [(i, i ^ 1) for i in range(replicas)]
     turn = round(TURN * peers)
     plane = [[(j + turn) % peers for j in range(peers)]]
-    column = [[(j + replicas - 2) % replicas for j in range(replicas)]]
+    column = [[((j ^ 1) + replicas - 2) % replicas for j in range(replicas)]]
     message = (peers, PIECES, piece + LANES)
     slots, pack = call(
         request_kernel,

time: 106 us -> 104 us (0.981)
  starting transfers between devices: 43.8 us -> 41.9 us
    all_to_all x1, starting transfers between devices: 11 us -> 9.06 us  [per_device(): lax.all_to_all(copies, 'replica', split_axis=0, concat_axis=0, tiled=True...]
  transfers between devices with their start and end apart: 5 -> 5, of which waited for: 3 -> 3; matrix products, arithmetic and copies ran while one was open for 0% -> 0% of each run, Pallas kernels for 10% -> 11%
where the time goes in v9:
time: 104 us; the launch traced here: 103 us
  starting transfers between devices  41.9 us (40%)
  blocking collectives  37.4 us (36%)
  Pallas kernels  15 us (14%)
  waiting for transfers between devices  8.12 us (8%)
    all_to_all x1, blocking collectives, per_device(): lax.all_to_all(parts, 'dp', split_axis=0, concat_axis=0, tiled=True, axis...  37.4 us
    ppermute x1, starting transfers between devices, per_device(): swapped_feat = lax.ppermute(feat, 'replica', pairs)  16.1 us
    pallas_call x7, Pallas kernels, call(): pl.pallas_call(body, out_shape=pinned if several else pinned[0], in_specs...  15 us
    all_to_all x1, starting transfers between devices, per_device(): lax.all_to_all(slots, 'dp', split_axis=0, concat_axis=0, tiled=True, axis...  12.1 us
    all_to_all x1, starting transfers between devices, per_device(): lax.all_to_all(copies, 'replica', split_axis=0, concat_axis=0, tiled=True...  9.06 us
    all_to_all x1, waiting for transfers between devices, per_device(): lax.all_to_all(copies, 'replica', split_axis=0, concat_axis=0, tiled=True...  6.2 us
    ppermute x1, starting transfers between devices, per_device(): swapped = lax.ppermute(pack, 'replica', pairs)  2.48 us
    ppermute x1, starting transfers between devices, per_device(): other = lax.ppermute(own, 'replica', pairs)  2.19 us
  transfers between devices with their start and end apart: 5, of which 3 were waited for; matrix products, arithmetic and copies ran while one was open for 0% of the time, Pallas kernels for 11%

profile of v9, /device:TPU:1, one launch (start us, length us, event | category | flops | bytes accessed | tf_op | source)
XLA Modules:
  0.0 103.1 jit_solution(9897159039928982621)
XLA Ops:
  0.6 16.1 %collective-permute-start = (bf16[256,2048]{1,0:T(8,128)(2,1)}, bf16[256,2048]{1,0:T(8,128)(2,1)S(1)}, u32[]{:S(2)}, u32[]{:S(2)}) collective-permute-start(bf16[256,2048]{1,0:T(8,128)(2,1)} %bitcast.8), channel_id=1, source_target_pairs={{0,1},{1,0},{2,3},{3,2},{4,5},{5,4},{6,7},{7,6},{8,9},{9,8},{10,11... | collective-permute-start | bytes 3145736 | tf_op jit(solution)/shard_map/ppermute | solution.py:384
  16.7 2.6 %shard_map.128 = (bf16[64,2,1152]{2,1,0:T(2,128)(2,1)}, bf16[32,2048]{1,0:T(8,128)(2,1)S(1)}) custom-call(s32[1,16]{1,0:T(1,128)} %refs_0_.1, s32[1,256]{1,0:T(1,128)} %bitcast.17, f32[1,256]{1,0:T(1,128)} %refs_2_.4, bf16[16,2048]{1,0:T(8,128)(2,1)} %bitcast.11, bf16[256,2048]{1,0:T(8,128)(2,1)} %bitcast.9), custom_call_target="tpu_custom_call" | custom-call | tf_op jit(solution)/shard_map/pallas_call | solution.py:342
  19.3 12.1 %all-to-all-start = ((bf16[64,2,1152]{2,1,0:T(2,128)(2,1)}), bf16[64,2,1152]{2,1,0:T(2,128)(2,1)S(1)}, u32[]{:S(2)}, u32[]{:S(2)}) async-start(bf16[64,2,1152]{2,1,0:T(2,128)(2,1)} %get-tuple-element.17), calls=%async_computation | async-start | bytes 589824 | tf_op jit(solution)/shard_map/all_to_all | solution.py:381
  31.4 2.5 %collective-permute-start.1 = (bf16[32,2048]{1,0:T(8,128)(2,1)S(1)}, bf16[32,2048]{1,0:T(8,128)(2,1)S(1)}, u32[]{:S(2)}, u32[]{:S(2)}) collective-permute-start(bf16[32,2048]{1,0:T(8,128)(2,1)S(1)} %get-tuple-element.18), channel_id=1, source_target_pairs={{0,1},{1,0},{2,3},{3,2},{4,5},{5,4},{6,7},{7,6},{8,9},{9,8},{10,11... | collective-permute-start | bytes 393224 | tf_op jit(solution)/shard_map/ppermute | solution.py:385
  33.9 1.0 collective-permute-done.1.refs_4_
  34.9 0.0 collective-permute-done.refs_1_
  34.9 4.8 %shard_map.129 = (bf16[64,8,1024]{2,1,0:T(8,128)(2,1)}, bf16[2048,256]{1,0:T(8,128)(2,1)S(1)}, f32[32,256]{1,0:T(8,128)S(1)}, bf16[32,2048]{1,0:T(8,128)(2,1)S(1)}) custom-call(bf16[256,2048]{1,0:T(8,128)(2,1)} %bitcast.10, bf16[256,2048]{1,0:T(8,128)(2,1)S(1)} %collective-permute-done.refs_1_, f32[1,256]{1,0:T(1,128)} %refs_2_.4, ...), custom_call_target="tpu_custom_call" | custom-call | flops 1 | bytes 1 | tf_op jit(solution)/shard_map/pallas_call | solution.py:342
  39.6 0.0 all-to-all-done.refs_0_
  39.6 0.7 shard_map.130.refs_0_
  40.4 2.2 %collective-permute-start.2 = (bf16[16,2176]{1,0:T(8,128)(2,1)S(1)}, bf16[16,2176]{1,0:T(8,128)(2,1)S(1)}, u32[]{:S(2)}, u32[]{:S(2)}) collective-permute-start(bf16[16,2176]{1,0:T(8,128)(2,1)S(1)} %shard_map.130.refs_0_), channel_id=1, source_target_pairs={{0,1},{1,0},{2,3},{3,2},{4,5},{5,4},{6,7},{7,6},{8,9},{9,8},{10,11... | collective-permute-start | bytes 208904 | tf_op jit(solution)/shard_map/ppermute | solution.py:413
  42.6 1.0 collective-permute-done.2.refs_1_
  43.5 1.4 %shard_map.132 = bf16[64,8,1152]{2,1,0:T(8,128)(2,1)S(1)} custom-call(bf16[16,2176]{1,0:T(8,128)(2,1)S(1)} %shard_map.130.refs_0_, bf16[16,2176]{1,0:T(8,128)(2,1)S(1)} %collective-permute-done.2.refs_1_, bf16[32,2048]{1,0:T(8,128)(2,1)S(1)} %get-tuple-element.21.refs_2_, bf16[2048,256]{1,0:T(8,128)(2,1)S(1)} %get-tuple-element.22.refs_3_, ...), custom_call_target="tpu_custom_call" | custom-call | tf_op jit(solution)/shard_map/pallas_call | solution.py:342
  45.0 37.4 %all_to_all.15.refs_0_ = bf16[64,8,1152]{2,1,0:T(8,128)(2,1)S(1)} all-to-all(bf16[64,8,1152]{2,1,0:T(8,128)(2,1)S(1)} %shard_map.132), channel_id=1, replica_groups={{576,592,608,624,640,656,672,688,704,720,736,752,768,784,800,816,832,84..., dimensions={0} | all-to-all | bytes 2359296 | tf_op jit(solution)/shard_map/all_to_all | solution.py:420
  82.4 0.9 shard_map.133
  83.3 9.1 %all-to-all-start.2 = ((bf16[16,8,1152]{2,1,0:T(8,128)(2,1)}), bf16[16,8,1152]{2,1,0:T(8,128)(2,1)S(1)}, u32[]{:S(2)}, u32[]{:S(2)}) async-start(bf16[16,8,1152]{2,1,0:T(8,128)(2,1)} %shard_map.133), calls=%async_computation.2 | async-start | bytes 589824 | tf_op jit(solution)/shard_map/all_to_all | solution.py:430
  92.3 3.7 %shard_map.131 = (f32[16,2048]{1,0:T(8,128)}, f32[32,384]{1,0:T(8,128)S(1)}) custom-call(bf16[16,2176]{1,0:T(8,128)(2,1)S(1)} %shard_map.130.refs_0_, bf16[16,2048]{1,0:T(8,128)(2,1)} %bitcast.13, bf16[2048,256]{1,0:T(8,128)(2,1)} %refs_2_.5, bf16[256,2048]{1,0:T(8,128)(2,1)} %refs_3_.1, f32[1,2048]{1,0:T(1,128)} %bitcast.16, bf16[16,128]{1,0:T(8,128)(2,1)} %bitcast.15), custom_call_target="tpu_custom_call" | custom-call | tf_op jit(solution)/shard_map/pallas_call | solution.py:342
  96.0 6.2 %all-to-all-done.2.refs_0_ = bf16[16,8,1152]{2,1,0:T(8,128)(2,1)S(1)} async-done(((bf16[16,8,1152]{2,1,0:T(8,128)(2,1)}), bf16[16,8,1152]{2,1,0:T(8,128)(2,1)S(1)}, u32[]{:S(2)}, u32[]{:S(2)}) %all-to-all-start.2) | async-done | bytes 294944 | tf_op jit(solution)/shard_map/all_to_all | solution.py:430
  102.2 0.9 shard_map.134
Async XLA Ops:
  0.6 34.2 %collective-permute-start = (bf16[256,2048]{1,0:T(8,128)(2,1)}, bf16[256,2048]{1,0:T(8,128)(2,1)S(1)}, u32[]{:S(2)}, u32[]{:S(2)}) collective-permute-start(bf16[256,2048]{1,0:T(8,128)(2,1)} %bitcast.8), channel_id=1, source_target_pairs={{0,1},{1,0},{2,3},{3,2},{4,5},{5,4},{6,7},{7,6},{8,9},{9,8},{10,11... | collective-permute-start | bytes 3145736 | tf_op jit(solution)/shard_map/ppermute | solution.py:384
  19.3 20.3 %all-to-all-start = ((bf16[64,2,1152]{2,1,0:T(2,128)(2,1)}), bf16[64,2,1152]{2,1,0:T(2,128)(2,1)S(1)}, u32[]{:S(2)}, u32[]{:S(2)}) async-start(bf16[64,2,1152]{2,1,0:T(2,128)(2,1)} %get-tuple-element.17), calls=%async_computation | async-start | bytes 589824 | tf_op jit(solution)/shard_map/all_to_all | solution.py:381
  31.4 3.5 %collective-permute-start.1 = (bf16[32,2048]{1,0:T(8,128)(2,1)S(1)}, bf16[32,2048]{1,0:T(8,128)(2,1)S(1)}, u32[]{:S(2)}, u32[]{:S(2)}) collective-permute-start(bf16[32,2048]{1,0:T(8,128)(2,1)S(1)} %get-tuple-element.18), channel_id=1, source_target_pairs={{0,1},{1,0},{2,3},{3,2},{4,5},{5,4},{6,7},{7,6},{8,9},{9,8},{10,11... | collective-permute-start | bytes 393224 | tf_op jit(solution)/shard_map/ppermute | solution.py:385
  40.4 3.1 %collective-permute-start.2 = (bf16[16,2176]{1,0:T(8,128)(2,1)S(1)}, bf16[16,2176]{1,0:T(8,128)(2,1)S(1)}, u32[]{:S(2)}, u32[]{:S(2)}) collective-permute-start(bf16[16,2176]{1,0:T(8,128)(2,1)S(1)} %shard_map.130.refs_0_), channel_id=1, source_target_pairs={{0,1},{1,0},{2,3},{3,2},{4,5},{5,4},{6,7},{7,6},{8,9},{9,8},{10,11... | collective-permute-start | bytes 208904 | tf_op jit(solution)/shard_map/ppermute | solution.py:413
  83.3 18.9 %all-to-all-start.2 = ((bf16[16,8,1152]{2,1,0:T(8,128)(2,1)}), bf16[16,8,1152]{2,1,0:T(8,128)(2,1)S(1)}, u32[]{:S(2)}, u32[]{:S(2)}) async-start(bf16[16,8,1152]{2,1,0:T(8,128)(2,1)} %shard_map.133), calls=%async_computation.2 | async-start | bytes 589824 | tf_op jit(solution)/shard_map/all_to_all | solution.py:430

commit v10 on v9

--- a/solution.py
+++ b/solution.py
@@ -264,7 +264,6 @@
 
 
 def last_kernel(factor, wait, in_ref, tail_ref, grad_u_ref, grad_vt_ref, bias_ref, out_ref):
-    wait(1)
     part, rank = grad_u_ref.shape
     replicas = in_ref.shape[0]
     sums = [
@@ -440,7 +439,6 @@
             shape((1, part), F32),
         ),
         gathered, tail,
-        places="-n",
     )
     return (user_grad[None], grad_u, grad_vt, grad_bias[0], grad_out[0])
 

time: 104 us -> 104 us (level)
  no operation moved by 1% of the time
where the time goes in v10:
time: 104 us; the launch traced here: 103 us
  starting transfers between devices  41.9 us (40%)
  blocking collectives  37.4 us (36%)
  Pallas kernels  14.9 us (14%)
  waiting for transfers between devices  8.12 us (8%)
    all_to_all x1, blocking collectives, per_device(): lax.all_to_all(parts, 'dp', split_axis=0, concat_axis=0, tiled=True, axis...  37.4 us
    ppermute x1, starting transfers between devices, per_device(): swapped_feat = lax.ppermute(feat, 'replica', pairs)  16.1 us
    pallas_call x7, Pallas kernels, call(): pl.pallas_call(body, out_shape=pinned if several else pinned[0], in_specs...  14.9 us
    all_to_all x1, starting transfers between devices, per_device(): lax.all_to_all(slots, 'dp', split_axis=0, concat_axis=0, tiled=True, axis...  12.1 us
    all_to_all x1, starting transfers between devices, per_device(): lax.all_to_all(copies, 'replica', split_axis=0, concat_axis=0, tiled=True...  9.06 us
    all_to_all x1, waiting for transfers between devices, per_device(): lax.all_to_all(copies, 'replica', split_axis=0, concat_axis=0, tiled=True...  6.2 us
    ppermute x1, starting transfers between devices, per_device(): swapped = lax.ppermute(pack, 'replica', pairs)  2.48 us
    ppermute x1, starting transfers between devices, per_device(): other = lax.ppermute(own, 'replica', pairs)  2.19 us
  transfers between devices with their start and end apart: 5, of which 3 were waited for; matrix products, arithmetic and copies ran while one was open for 0% of the time, Pallas kernels for 11%

profile of v10, /device:TPU:1, one launch (start us, length us, event | category | flops | bytes accessed | tf_op | source)
XLA Modules:
  0.0 103.0 jit_solution(10362576161819172258)
XLA Ops:
  0.6 16.1 %collective-permute-start = (bf16[256,2048]{1,0:T(8,128)(2,1)}, bf16[256,2048]{1,0:T(8,128)(2,1)S(1)}, u32[]{:S(2)}, u32[]{:S(2)}) collective-permute-start(bf16[256,2048]{1,0:T(8,128)(2,1)} %bitcast.8), channel_id=1, source_target_pairs={{0,1},{1,0},{2,3},{3,2},{4,5},{5,4},{6,7},{7,6},{8,9},{9,8},{10,11... | collective-permute-start | bytes 3145736 | tf_op jit(solution)/shard_map/ppermute | solution.py:383
  16.7 2.6 %shard_map.128 = (bf16[64,2,1152]{2,1,0:T(2,128)(2,1)}, bf16[32,2048]{1,0:T(8,128)(2,1)S(1)}) custom-call(s32[1,16]{1,0:T(1,128)} %refs_0_.1, s32[1,256]{1,0:T(1,128)} %bitcast.17, f32[1,256]{1,0:T(1,128)} %refs_2_.4, bf16[16,2048]{1,0:T(8,128)(2,1)} %bitcast.11, bf16[256,2048]{1,0:T(8,128)(2,1)} %bitcast.9), custom_call_target="tpu_custom_call" | custom-call | tf_op jit(solution)/shard_map/pallas_call | solution.py:341
  19.3 12.1 %all-to-all-start = ((bf16[64,2,1152]{2,1,0:T(2,128)(2,1)}), bf16[64,2,1152]{2,1,0:T(2,128)(2,1)S(1)}, u32[]{:S(2)}, u32[]{:S(2)}) async-start(bf16[64,2,1152]{2,1,0:T(2,128)(2,1)} %get-tuple-element.17), calls=%async_computation | async-start | bytes 589824 | tf_op jit(solution)/shard_map/all_to_all | solution.py:380
  31.4 2.5 %collective-permute-start.1 = (bf16[32,2048]{1,0:T(8,128)(2,1)S(1)}, bf16[32,2048]{1,0:T(8,128)(2,1)S(1)}, u32[]{:S(2)}, u32[]{:S(2)}) collective-permute-start(bf16[32,2048]{1,0:T(8,128)(2,1)S(1)} %get-tuple-element.18), channel_id=1, source_target_pairs={{0,1},{1,0},{2,3},{3,2},{4,5},{5,4},{6,7},{7,6},{8,9},{9,8},{10,11... | collective-permute-start | bytes 393224 | tf_op jit(solution)/shard_map/ppermute | solution.py:384
  33.9 1.0 collective-permute-done.1.refs_4_
  34.9 0.0 collective-permute-done.refs_1_
  34.9 4.8 %shard_map.129 = (bf16[64,8,1024]{2,1,0:T(8,128)(2,1)}, bf16[2048,256]{1,0:T(8,128)(2,1)S(1)}, f32[32,256]{1,0:T(8,128)S(1)}, bf16[32,2048]{1,0:T(8,128)(2,1)S(1)}) custom-call(bf16[256,2048]{1,0:T(8,128)(2,1)} %bitcast.10, bf16[256,2048]{1,0:T(8,128)(2,1)S(1)} %collective-permute-done.refs_1_, f32[1,256]{1,0:T(1,128)} %refs_2_.4, ...), custom_call_target="tpu_custom_call" | custom-call | flops 1 | bytes 1 | tf_op jit(solution)/shard_map/pallas_call | solution.py:341
  39.6 0.0 all-to-all-done.refs_0_
  39.6 0.7 shard_map.130.refs_0_
  40.4 2.2 %collective-permute-start.2 = (bf16[16,2176]{1,0:T(8,128)(2,1)S(1)}, bf16[16,2176]{1,0:T(8,128)(2,1)S(1)}, u32[]{:S(2)}, u32[]{:S(2)}) collective-permute-start(bf16[16,2176]{1,0:T(8,128)(2,1)S(1)} %shard_map.130.refs_0_), channel_id=1, source_target_pairs={{0,1},{1,0},{2,3},{3,2},{4,5},{5,4},{6,7},{7,6},{8,9},{9,8},{10,11... | collective-permute-start | bytes 208904 | tf_op jit(solution)/shard_map/ppermute | solution.py:412
  42.6 1.0 collective-permute-done.2.refs_1_
  43.5 1.4 %shard_map.132 = bf16[64,8,1152]{2,1,0:T(8,128)(2,1)S(1)} custom-call(bf16[16,2176]{1,0:T(8,128)(2,1)S(1)} %shard_map.130.refs_0_, bf16[16,2176]{1,0:T(8,128)(2,1)S(1)} %collective-permute-done.2.refs_1_, bf16[32,2048]{1,0:T(8,128)(2,1)S(1)} %get-tuple-element.21.refs_2_, bf16[2048,256]{1,0:T(8,128)(2,1)S(1)} %get-tuple-element.22.refs_3_, ...), custom_call_target="tpu_custom_call" | custom-call | tf_op jit(solution)/shard_map/pallas_call | solution.py:341
  45.0 37.4 %all_to_all.15.refs_0_ = bf16[64,8,1152]{2,1,0:T(8,128)(2,1)S(1)} all-to-all(bf16[64,8,1152]{2,1,0:T(8,128)(2,1)S(1)} %shard_map.132), channel_id=1, replica_groups={{576,592,608,624,640,656,672,688,704,720,736,752,768,784,800,816,832,84..., dimensions={0} | all-to-all | bytes 2359296 | tf_op jit(solution)/shard_map/all_to_all | solution.py:419
  82.4 0.9 shard_map.133
  83.3 9.1 %all-to-all-start.2 = ((bf16[16,8,1152]{2,1,0:T(8,128)(2,1)}), bf16[16,8,1152]{2,1,0:T(8,128)(2,1)S(1)}, u32[]{:S(2)}, u32[]{:S(2)}) async-start(bf16[16,8,1152]{2,1,0:T(8,128)(2,1)} %shard_map.133), calls=%async_computation.2 | async-start | bytes 589824 | tf_op jit(solution)/shard_map/all_to_all | solution.py:429
  92.3 3.7 %shard_map.131 = (f32[16,2048]{1,0:T(8,128)}, f32[32,384]{1,0:T(8,128)S(1)}) custom-call(bf16[16,2176]{1,0:T(8,128)(2,1)S(1)} %shard_map.130.refs_0_, bf16[16,2048]{1,0:T(8,128)(2,1)} %bitcast.13, bf16[2048,256]{1,0:T(8,128)(2,1)} %refs_2_.5, bf16[256,2048]{1,0:T(8,128)(2,1)} %refs_3_.1, f32[1,2048]{1,0:T(1,128)} %bitcast.16, bf16[16,128]{1,0:T(8,128)(2,1)} %bitcast.15), custom_call_target="tpu_custom_call" | custom-call | tf_op jit(solution)/shard_map/pallas_call | solution.py:341
  96.0 6.2 %all-to-all-done.2.refs_0_ = bf16[16,8,1152]{2,1,0:T(8,128)(2,1)S(1)} async-done(((bf16[16,8,1152]{2,1,0:T(8,128)(2,1)}), bf16[16,8,1152]{2,1,0:T(8,128)(2,1)S(1)}, u32[]{:S(2)}, u32[]{:S(2)}) %all-to-all-start.2) | async-done | bytes 294944 | tf_op jit(solution)/shard_map/all_to_all | solution.py:429
  102.2 0.9 shard_map.134
Async XLA Ops:
  0.6 34.2 %collective-permute-start = (bf16[256,2048]{1,0:T(8,128)(2,1)}, bf16[256,2048]{1,0:T(8,128)(2,1)S(1)}, u32[]{:S(2)}, u32[]{:S(2)}) collective-permute-start(bf16[256,2048]{1,0:T(8,128)(2,1)} %bitcast.8), channel_id=1, source_target_pairs={{0,1},{1,0},{2,3},{3,2},{4,5},{5,4},{6,7},{7,6},{8,9},{9,8},{10,11... | collective-permute-start | bytes 3145736 | tf_op jit(solution)/shard_map/ppermute | solution.py:383
  19.3 20.3 %all-to-all-start = ((bf16[64,2,1152]{2,1,0:T(2,128)(2,1)}), bf16[64,2,1152]{2,1,0:T(2,128)(2,1)S(1)}, u32[]{:S(2)}, u32[]{:S(2)}) async-start(bf16[64,2,1152]{2,1,0:T(2,128)(2,1)} %get-tuple-element.17), calls=%async_computation | async-start | bytes 589824 | tf_op jit(solution)/shard_map/all_to_all | solution.py:380
  31.4 3.5 %collective-permute-start.1 = (bf16[32,2048]{1,0:T(8,128)(2,1)S(1)}, bf16[32,2048]{1,0:T(8,128)(2,1)S(1)}, u32[]{:S(2)}, u32[]{:S(2)}) collective-permute-start(bf16[32,2048]{1,0:T(8,128)(2,1)S(1)} %get-tuple-element.18), channel_id=1, source_target_pairs={{0,1},{1,0},{2,3},{3,2},{4,5},{5,4},{6,7},{7,6},{8,9},{9,8},{10,11... | collective-permute-start | bytes 393224 | tf_op jit(solution)/shard_map/ppermute | solution.py:384
  40.4 3.1 %collective-permute-start.2 = (bf16[16,2176]{1,0:T(8,128)(2,1)S(1)}, bf16[16,2176]{1,0:T(8,128)(2,1)S(1)}, u32[]{:S(2)}, u32[]{:S(2)}) collective-permute-start(bf16[16,2176]{1,0:T(8,128)(2,1)S(1)} %shard_map.130.refs_0_), channel_id=1, source_target_pairs={{0,1},{1,0},{2,3},{3,2},{4,5},{5,4},{6,7},{7,6},{8,9},{9,8},{10,11... | collective-permute-start | bytes 208904 | tf_op jit(solution)/shard_map/ppermute | solution.py:412
  83.3 18.9 %all-to-all-start.2 = ((bf16[16,8,1152]{2,1,0:T(8,128)(2,1)}), bf16[16,8,1152]{2,1,0:T(8,128)(2,1)S(1)}, u32[]{:S(2)}, u32[]{:S(2)}) async-start(bf16[16,8,1152]{2,1,0:T(8,128)(2,1)} %shard_map.133), calls=%async_computation.2 | async-start | bytes 589824 | tf_op jit(solution)/shard_map/all_to_all | solution.py:429
